TPU v7x, 128 devices: a whole 4x4x4 slice. The times are simulated.
128 devices in a mesh: dp: 32 (over z, x, core), hid: 4 (over y).
Axes of the slice: x: 4, y: 4, z: 4, core: 2. Of those that a mesh axis runs over, the one named last changes fastest.
Arguments:
- features: bfloat16 [16384, 80], P('dp'), may hold values from -6 to 6
- lengths: int32 [32], P('dp'), may hold values from 128 to 512, as said below
- routes: int32 [2, 16384, 1], P(None, 'dp'), may hold values from 0 to 31; in each aligned block of 512 rows (0 to 511, 512 to 1023, ..., all dimensions but the last counted through in order) at most 24 rows name the same one
- alignments: int32 [16384], P('dp'), may hold values from 0 to 4095
- input_weight: float32 [80, 512], P(None, 'dp'), may hold values from -0.625 to 0.625
- attention_in: float32 [512, 1536], P('dp'), may hold values from -0.25 to 0.25
- branch_out: float32 [2, 512, 512], P(None, 'dp'), may hold values from -0.5 to 0.5
- pointwise_in: float32 [512, 1024], P('dp'), may hold values from -0.25 to 0.25
- depthwise: float32 [15, 512], P(None, 'dp'), may hold values from -1.5 to 1.5
- router: float32 [2, 512, 32], P(None, 'dp'), may hold values from -0.19887379 to 0.19887379
- senone_table: float32 [512, 4096], P('dp', 'hid')
- norm_scales: float32 [7, 512], P(None, 'dp'), may hold values from 0.5 to 1.5
- expert_weights: float32 [2, 2, 32, 512, 2048], P(None, None, 'dp', None, 'hid')
- input_first: float32 [80, 512], P(None, 'dp'), may hold values from -5.722046e-06 to 5.722046e-06
- input_second: float32 [80, 512], P(None, 'dp'), may hold values from 6.589491e-14 to 2.6357963e-13
- attention_first: float32 [512, 1536], P('dp'), may hold values from -5.722046e-06 to 5.722046e-06
- attention_second: float32 [512, 1536], P('dp'), may hold values from 6.589491e-14 to 2.6357963e-13
- branch_first: float32 [2, 512, 512], P(None, 'dp'), may hold values from -5.722046e-06 to 5.722046e-06
- branch_second: float32 [2, 512, 512], P(None, 'dp'), may hold values from 6.589491e-14 to 2.6357963e-13
- pointwise_first: float32 [512, 1024], P('dp'), may hold values from -5.722046e-06 to 5.722046e-06
- pointwise_second: float32 [512, 1024], P('dp'), may hold values from 6.589491e-14 to 2.6357963e-13
- depthwise_first: float32 [15, 512], P(None, 'dp'), may hold values from -1.1444092e-05 to 1.1444092e-05
- depthwise_second: float32 [15, 512], P(None, 'dp'), may hold values from 2.6357963e-13 to 1.0543185e-12
- router_first: float32 [2, 512, 32], P(None, 'dp'), may hold values from -5.722046e-06 to 5.722046e-06
- router_second: float32 [2, 512, 32], P(None, 'dp'), may hold values from 6.589491e-14 to 2.6357963e-13
- senone_first: float32 [512, 4096], P('dp', 'hid'), may hold values from -5.722046e-06 to 5.722046e-06
- senone_second: float32 [512, 4096], P('dp', 'hid'), may hold values from 6.589491e-14 to 2.6357963e-13
- scales_first: float32 [7, 512], P(None, 'dp'), may hold values from -1.1444092e-05 to 1.1444092e-05
- scales_second: float32 [7, 512], P(None, 'dp'), may hold values from 2.6357963e-13 to 1.0543185e-12
- expert_momentum: float32 [2, 2, 32, 512, 2048], P(None, None, 'dp', None, 'hid')
Outputs:
- loss_sum: float32 [], replicated
- frame_count: float32 [], replicated
- grad_norm: float32 [], replicated
- input_first_new: float32 [80, 512], P(None, 'dp')
- input_second_new: float32 [80, 512], P(None, 'dp')
- input_new: float32 [80, 512], P(None, 'dp')
- attention_first_new: float32 [512, 1536], P('dp')
- attention_second_new: float32 [512, 1536], P('dp')
- attention_new: float32 [512, 1536], P('dp')
- branch_first_new: float32 [2, 512, 512], P(None, 'dp')
- branch_second_new: float32 [2, 512, 512], P(None, 'dp')
- branch_new: float32 [2, 512, 512], P(None, 'dp')
- pointwise_first_new: float32 [512, 1024], P('dp')
- pointwise_second_new: float32 [512, 1024], P('dp')
- pointwise_new: float32 [512, 1024], P('dp')
- depthwise_first_new: float32 [15, 512], P(None, 'dp')
- depthwise_second_new: float32 [15, 512], P(None, 'dp')
- depthwise_new: float32 [15, 512], P(None, 'dp')
- router_first_new: float32 [2, 512, 32], P(None, 'dp')
- router_second_new: float32 [2, 512, 32], P(None, 'dp')
- router_new: float32 [2, 512, 32], P(None, 'dp')
- senone_first_new: float32 [512, 4096], P('dp', 'hid')
- senone_second_new: float32 [512, 4096], P('dp', 'hid')
- senone_new: float32 [512, 4096], P('dp', 'hid')
- scales_first_new: float32 [7, 512], P(None, 'dp')
- scales_second_new: float32 [7, 512], P(None, 'dp')
- scales_new: float32 [7, 512], P(None, 'dp')
- momentum_new: float32 [2, 2, 32, 512, 2048], P(None, None, 'dp', None, 'hid')
- experts_new: float32 [2, 2, 32, 512, 2048], P(None, None, 'dp', None, 'hid')
Inputs may be any that keep to these rules, and one draw needn't show every extreme that they name: `lengths`: each utterance has at least a quarter of its 512 padded frames; the last utterance fills all 512. `routes`: within one utterance's frames of one feed-forward no expert is named more than 24 times, a bound that some block reaches.
All inputs are finite; a program needn't handle non-finite values.
Results may differ from a plain program's by a relative error of at most 0.015.
Values may be sent and summed in bfloat16 or wider, within the bound.
No kernel may reach another device: no remote copies, remote signals or barrier semaphores. Data moves between devices by JAX's collectives and lax.ppermute only.
A program may use at most 192 MiB of HBM per device.

v0:
```python
import jax
import jax.numpy as jnp
from jax import lax
from jax.sharding import PartitionSpec as P

D = 512
HEADS = 8
HEAD_DIM = 64
FF = 2048
STEP = 10


clip_limit = 0.02
beta_one = 0.9
beta_two = 0.999
adam_epsilon = 1e-08
adam_rate = 0.2
gain_rate = 0.6
weight_decay = 0.01
muon_beta = 0.95
muon_rate = 1.0
muon_decay = 0.01
newton_first = 3.4445
newton_second = -4.775
newton_third = 2.0315


def combined_all(shard, axis, combine):
    everything = jax.tree.map(lambda part: lax.all_gather(part, axis), shard)
    leading = jax.tree.map(lambda part: part[0], everything)

    def turn(k, so_far):
        return combine(so_far, jax.tree.map(lambda part: part[k], everything))

    return lax.fori_loop(1, lax.axis_size(axis), turn, leading)


def to_low(values):
    return values.astype(jnp.bfloat16)


def dot_low(left, right):
    return jnp.dot(left, right, preferred_element_type=jnp.float32)


def dot_left(left, right):
    return lax.dot_general(
        left, right, (((0,), (0,)), ((), ())), preferred_element_type=jnp.float32
    )


def dot_right(left, right):
    return lax.dot_general(
        left, right, (((1,), (1,)), ((), ())), preferred_element_type=jnp.float32
    )


def exact_dot(left, right):
    return jnp.dot(left, right, precision=lax.Precision.HIGHEST)


def norm_forward(values, gain):
    centered = values - jnp.mean(values, -1, keepdims=True)
    inverse = lax.rsqrt(jnp.mean(centered * centered, -1, keepdims=True) + 1e-05)
    unit = centered * inverse
    return (unit * gain, unit, inverse)


def norm_backward(grad, unit, inverse, gain):
    scaled = grad * gain
    back = inverse * (
        scaled
        - jnp.mean(scaled, -1, keepdims=True)
        - unit * jnp.mean(scaled * unit, -1, keepdims=True)
    )
    return (back, jnp.sum(grad * unit, 0))


def silu_slope(values):
    sigma = jax.nn.sigmoid(values)
    return sigma * (1.0 + values * (1.0 - sigma))


def combine_softmax(first, second):
    top = jnp.maximum(first[0], second[0])
    return (top, first[1] * jnp.exp(first[0] - top) + second[1] * jnp.exp(second[0] - top))


def orthogonal(matrix):
    current = matrix / (jnp.sqrt(jnp.sum(matrix * matrix)) + 1e-07)
    for turn in range(5):
        gram = exact_dot(current, current.T)
        poly = newton_second * gram + newton_third * exact_dot(gram, gram)
        current = newton_first * current + exact_dot(poly, current)
    return current


def adam_update(weight, grad, first, second, rate, decay):
    first_new = beta_one * first + (1.0 - beta_one) * grad
    second_new = beta_two * second + (1.0 - beta_two) * grad * grad
    corrected = (
        first_new
        / (1.0 - beta_one**STEP)
        / (jnp.sqrt(second_new / (1.0 - beta_two**STEP)) + adam_epsilon)
    )
    return (first_new, second_new, weight - rate * (corrected + decay * weight))


def send_to_experts(slots, experts, capacity):
    shaped = slots.reshape(experts, capacity, -1)
    moved = lax.all_to_all(shaped, "dp", split_axis=0, concat_axis=0, tiled=True)
    return moved.reshape(experts * capacity, -1)


def return_from_experts(partial_value, experts, capacity):
    shaped = partial_value.reshape(experts, capacity, -1)
    total = lax.psum(shaped, "hid")
    back = lax.all_to_all(to_low(total), "dp", split_axis=0, concat_axis=0, tiled=True)
    return back.reshape(experts * capacity, -1)


def mixture_forward(values, gain, router_part, weight_in, weight_out, route_rows):
    experts = lax.axis_size("dp")
    capacity = 3 * values.shape[0] // (2 * experts)
    normed, unit, inverse = norm_forward(values, gain)
    onehot_int = (route_rows[:, None] == jnp.arange(experts, dtype=jnp.int32)[None, :]).astype(
        jnp.int32
    )
    earlier = jnp.cumsum(onehot_int, 0) - onehot_int
    position = route_rows * capacity + jnp.sum(earlier * onehot_int, 1)
    dispatch = (
        jnp.arange(experts * capacity, dtype=jnp.int32)[:, None] == position[None, :]
    ).astype(jnp.bfloat16)
    onehot = onehot_int.astype(jnp.float32)
    chances = jax.nn.softmax(exact_dot(normed, router_part), -1)
    gate = jnp.sum(chances * onehot, 1)
    slots = to_low(dot_low(dispatch, to_low(normed)))
    rows = send_to_experts(slots, experts, capacity)
    active = dot_low(rows, weight_in)
    hidden = to_low(jax.nn.silu(active))
    back = return_from_experts(dot_right(hidden, weight_out), experts, capacity)
    expert_out = dot_left(dispatch, back)
    kept = (
        unit,
        inverse,
        normed,
        chances,
        onehot,
        gate,
        dispatch,
        rows,
        active,
        hidden,
        expert_out,
    )
    return (0.5 * gate[:, None] * expert_out, kept)


def mixture_backward(grad, gain, router_part, weight_in, weight_out, kept):
    unit, inverse, normed, chances, onehot, gate, dispatch, rows, active, hidden, expert_out = kept
    experts = lax.axis_size("dp")
    capacity = dispatch.shape[0] // experts
    branch = 0.5 * grad
    slot_grad = to_low(dot_low(dispatch, to_low(gate[:, None] * branch)))
    rows_grad = send_to_experts(slot_grad, experts, capacity)
    out_grad = dot_left(rows_grad, hidden)
    active_grad = to_low(dot_low(rows_grad, weight_out) * silu_slope(active))
    in_grad = dot_left(rows, active_grad)
    back = return_from_experts(dot_right(active_grad, weight_in), experts, capacity)
    gate_grad = jnp.sum(branch * expert_out, 1)
    logit_grad = (gate * gate_grad)[:, None] * (onehot - chances)
    router_grad = exact_dot(normed.T, logit_grad)
    normed_grad = exact_dot(logit_grad, router_part.T) + dot_left(dispatch, back)
    values_grad, gain_grad = norm_backward(normed_grad, unit, inverse, gain)
    return (grad + values_grad, gain_grad, router_grad, in_grad, out_grad)


def attention_scores(queries, keys, valid):
    scores = jnp.einsum(
        "qhd,khd->hqk", queries, keys, preferred_element_type=jnp.float32
    ) * HEAD_DIM ** (-0.5)
    return jnp.where(valid[None, None, :] > 0, scores, -1e30)


def attention_forward(values, gain, weight_in, weight_out, valid):
    tokens = values.shape[0]
    normed, unit, inverse = norm_forward(values, gain)
    low_normed = to_low(normed)
    shaped = to_low(dot_low(low_normed, weight_in)).reshape(tokens, 3, HEADS, HEAD_DIM)
    queries, keys, contents = (shaped[:, 0], shaped[:, 1], shaped[:, 2])
    scores = attention_scores(queries, keys, valid)
    top = jnp.max(scores, -1, keepdims=True)
    raised = jnp.exp(scores - top)
    total = jnp.sum(raised, -1, keepdims=True)
    log_total = top + jnp.log(total)
    mixed = jnp.einsum(
        "hqk,khd->qhd", to_low(raised / total), contents, preferred_element_type=jnp.float32
    )
    context = to_low(mixed.reshape(tokens, -1))
    kept = (unit, inverse, low_normed, queries, keys, contents, log_total, context)
    return (dot_low(context, weight_out), kept)


def attention_backward(grad, gain, weight_in, weight_out, valid, kept):
    unit, inverse, low_normed, queries, keys, contents, log_total, context = kept
    tokens = grad.shape[0]
    low_grad = to_low(grad)
    out_grad = dot_left(context, low_grad)
    context_grad = to_low(dot_right(low_grad, weight_out)).reshape(tokens, HEADS, HEAD_DIM)
    weights = jnp.exp(attention_scores(queries, keys, valid) - log_total)
    weight_grad = jnp.einsum(
        "qhd,khd->hqk", context_grad, contents, preferred_element_type=jnp.float32
    )
    content_grad = jnp.einsum(
        "hqk,qhd->khd", to_low(weights), context_grad, preferred_element_type=jnp.float32
    )
    score_grad = to_low(weights * (weight_grad - jnp.sum(weight_grad * weights, -1, keepdims=True)))
    query_grad = jnp.einsum(
        "hqk,khd->qhd", score_grad, keys, preferred_element_type=jnp.float32
    ) * HEAD_DIM ** (-0.5)
    key_grad = jnp.einsum(
        "hqk,qhd->khd", score_grad, queries, preferred_element_type=jnp.float32
    ) * HEAD_DIM ** (-0.5)
    project_grad = to_low(jnp.stack([query_grad, key_grad, content_grad], 1).reshape(tokens, -1))
    in_grad = dot_left(low_normed, project_grad)
    values_grad, gain_grad = norm_backward(dot_right(project_grad, weight_in), unit, inverse, gain)
    return (grad + values_grad, gain_grad, in_grad, out_grad)


def convolution_forward(values, gains, weight_in, depth, weight_out, valid):
    tokens = values.shape[0]
    normed, unit, inverse = norm_forward(values, gains[2])
    low_normed = to_low(normed)
    project = dot_low(low_normed, weight_in)
    width = project.shape[1] // 2
    linear = project[:, :width]
    gating = jax.nn.sigmoid(project[:, width:])
    mixed = linear * gating * valid[:, None]
    reach = (depth.shape[0] - 1) // 2
    padded = jnp.pad(mixed, ((reach, reach), (0, 0)))
    deep = jnp.zeros_like(mixed)
    for offset in range(depth.shape[0]):
        deep = deep + depth[offset] * padded[offset : offset + tokens]
    count = jnp.sum(valid)
    mask = valid[:, None]
    mean = jnp.sum(mask * deep, 0) / count
    spread = jnp.sum(mask * deep * deep, 0) / count - mean * mean
    scale = lax.rsqrt(spread + 1e-05)
    unit_batch = (deep - mean) * scale
    shifted = unit_batch * gains[5] + gains[6]
    activated = to_low(jax.nn.silu(shifted))
    kept = (
        unit,
        inverse,
        low_normed,
        linear,
        gating,
        padded,
        scale,
        unit_batch,
        shifted,
        activated,
    )
    return (dot_low(activated, weight_out), kept)


def convolution_backward(grad, gains, weight_in, depth, weight_out, valid, kept):
    unit, inverse, low_normed, linear, gating, padded, scale, unit_batch, shifted, activated = kept
    tokens = grad.shape[0]
    low_grad = to_low(grad)
    out_grad = dot_left(activated, low_grad)
    shifted_grad = dot_right(low_grad, weight_out) * silu_slope(shifted)
    gamma_grad = jnp.sum(shifted_grad * unit_batch, 0)
    beta_grad = jnp.sum(shifted_grad, 0)
    unit_grad = shifted_grad * gains[5]
    count = jnp.sum(valid)
    mask = valid[:, None]
    first_sum = jnp.sum(mask * unit_grad, 0) / count
    second_sum = jnp.sum(mask * unit_grad * unit_batch, 0) / count
    deep_grad = scale * (unit_grad - mask * (first_sum + unit_batch * second_sum))
    reach = (depth.shape[0] - 1) // 2
    padded_grad = jnp.pad(deep_grad, ((reach, reach), (0, 0)))
    mixed_grad = jnp.zeros_like(deep_grad)
    depth_rows = []
    for offset in range(depth.shape[0]):
        begin = 2 * reach - offset
        mixed_grad = mixed_grad + depth[offset] * padded_grad[begin : begin + tokens]
        depth_rows.append(jnp.sum(deep_grad * padded[offset : offset + tokens], 0))
    mixed_grad = mixed_grad * mask
    project_grad = to_low(
        jnp.concatenate([mixed_grad * gating, mixed_grad * linear * gating * (1.0 - gating)], 1)
    )
    in_grad = dot_left(low_normed, project_grad)
    values_grad, gain_grad = norm_backward(
        dot_right(project_grad, weight_in), unit, inverse, gains[2]
    )
    return (
        grad + values_grad,
        gain_grad,
        gamma_grad,
        beta_grad,
        in_grad,
        jnp.stack(depth_rows),
        out_grad,
    )


def senone_forward(values, gain, table, targets, valid):
    normed, unit, inverse = norm_forward(values, gain)
    low_normed = to_low(normed)
    logits = dot_low(low_normed, table)
    width = logits.shape[1]
    columns = jnp.arange(width, dtype=jnp.int32) + lax.axis_index("hid") * width
    top = jnp.max(logits, 1)
    total = jnp.sum(jnp.exp(logits - top[:, None]), 1)
    target = jnp.sum(jnp.where(columns[None, :] == targets[:, None], logits, 0.0), 1)
    top, total = combined_all((top, total), "hid", combine_softmax)
    log_total = top + jnp.log(total)
    leading = (lax.axis_index("hid") == 0).astype(jnp.float32)
    loss = leading * jnp.sum(valid * log_total) - jnp.sum(valid * target)
    return (loss, (unit, inverse, low_normed, logits, log_total, columns))


def senone_backward(gain, table, targets, valid, kept):
    unit, inverse, low_normed, logits, log_total, columns = kept
    picked = (columns[None, :] == targets[:, None]).astype(jnp.float32)
    logit_grad = to_low(valid[:, None] * (jnp.exp(logits - log_total[:, None]) - picked))
    table_grad = dot_left(low_normed, logit_grad)
    normed_grad = lax.psum(dot_right(logit_grad, table), "hid")
    values_grad, gain_grad = norm_backward(normed_grad, unit, inverse, gain)
    return (values_grad, gain_grad, table_grad)


def layer_forward(
    start,
    valid,
    routes,
    alignments,
    attention_full,
    branch_full,
    pointwise_full,
    senone_full,
    depth_full,
    router_full,
    scales_full,
    expert_low,
):
    mixed_one, kept_one = mixture_forward(
        start, scales_full[0], router_full[0], expert_low[0, 0], expert_low[0, 1], routes[0, :, 0]
    )
    first = start + mixed_one
    attended, kept_attend = attention_forward(
        first, scales_full[1], attention_full, branch_full[0], valid
    )
    second = first + attended
    convolved, kept_convolve = convolution_forward(
        second, scales_full, pointwise_full, depth_full, branch_full[1], valid
    )
    third = second + convolved
    mixed_two, kept_two = mixture_forward(
        third, scales_full[3], router_full[1], expert_low[1, 0], expert_low[1, 1], routes[1, :, 0]
    )
    fourth = third + mixed_two
    loss, kept_senone = senone_forward(fourth, scales_full[4], senone_full, alignments, valid)
    return (loss, (kept_one, kept_attend, kept_convolve, kept_two, kept_senone))


def layer_backward(
    valid,
    alignments,
    attention_full,
    branch_full,
    pointwise_full,
    senone_full,
    depth_full,
    router_full,
    scales_full,
    expert_low,
    kept,
):
    kept_one, kept_attend, kept_convolve, kept_two, kept_senone = kept
    grad, gain_five, senone_grad = senone_backward(
        scales_full[4], senone_full, alignments, valid, kept_senone
    )
    grad, gain_four, router_two, in_two, out_two = mixture_backward(
        grad, scales_full[3], router_full[1], expert_low[1, 0], expert_low[1, 1], kept_two
    )
    grad, gain_three, gamma_grad, beta_grad, pointwise_grad, depth_grad, conv_out_grad = (
        convolution_backward(
            grad, scales_full, pointwise_full, depth_full, branch_full[1], valid, kept_convolve
        )
    )
    grad, gain_two, attention_grad, attend_out_grad = attention_backward(
        grad, scales_full[1], attention_full, branch_full[0], valid, kept_attend
    )
    grad, gain_one, router_one, in_one, out_one = mixture_backward(
        grad, scales_full[0], router_full[0], expert_low[0, 0], expert_low[0, 1], kept_one
    )
    scales_grad = jnp.stack(
        [gain_one, gain_two, gain_three, gain_four, gain_five, gamma_grad, beta_grad]
    )
    branch_grad = jnp.stack([attend_out_grad, conv_out_grad])
    router_grad = jnp.stack([router_one, router_two])
    expert_grad = jnp.stack([jnp.stack([in_one, out_one]), jnp.stack([in_two, out_two])])[
        :, :, None
    ]
    return (
        grad,
        attention_grad,
        branch_grad,
        pointwise_grad,
        senone_grad,
        depth_grad,
        router_grad,
        scales_grad,
        expert_grad,
    )


def on_device(
    features,
    lengths,
    routes,
    alignments,
    input_weight,
    attention_in,
    branch_out,
    pointwise_in,
    depthwise,
    router,
    senone_table,
    norm_scales,
    expert_weights,
    input_first,
    input_second,
    attention_first,
    attention_second,
    branch_first,
    branch_second,
    pointwise_first,
    pointwise_second,
    depthwise_first,
    depthwise_second,
    router_first,
    router_second,
    senone_first,
    senone_second,
    scales_first,
    scales_second,
    expert_momentum,
):
    input_full, attention_full, branch_full, pointwise_full, senone_full = (
        lax.all_gather(to_low(input_weight), "dp", axis=1, tiled=True),
        lax.all_gather(to_low(attention_in), "dp", axis=0, tiled=True),
        lax.all_gather(to_low(branch_out), "dp", axis=1, tiled=True),
        lax.all_gather(to_low(pointwise_in), "dp", axis=0, tiled=True),
        lax.all_gather(to_low(senone_table), "dp", axis=0, tiled=True),
    )
    depth_full, router_full, scales_full = (
        lax.all_gather(depthwise, "dp", axis=1, tiled=True),
        lax.all_gather(router, "dp", axis=1, tiled=True),
        lax.all_gather(norm_scales, "dp", axis=1, tiled=True),
    )
    tokens = features.shape[0]
    valid = (jnp.arange(tokens, dtype=jnp.int32) < lengths[0]).astype(jnp.float32)
    expert_low = to_low(expert_weights[:, :, 0])
    start = dot_low(features, input_full)
    loss_local, kept = layer_forward(
        start,
        valid,
        routes,
        alignments,
        attention_full,
        branch_full,
        pointwise_full,
        senone_full,
        depth_full,
        router_full,
        scales_full,
        expert_low,
    )
    (
        start_grad,
        attention_grad,
        branch_grad,
        pointwise_grad,
        senone_grad,
        depth_grad,
        router_grad,
        scales_grad,
        expert_grad,
    ) = layer_backward(
        valid,
        alignments,
        attention_full,
        branch_full,
        pointwise_full,
        senone_full,
        depth_full,
        router_full,
        scales_full,
        expert_low,
        kept,
    )
    input_grad = dot_left(features, to_low(start_grad))
    shares = (
        lax.psum_scatter(input_grad, "dp", scatter_dimension=1, tiled=True),
        lax.psum_scatter(attention_grad, "dp", scatter_dimension=0, tiled=True),
        lax.psum_scatter(branch_grad, "dp", scatter_dimension=1, tiled=True),
        lax.psum_scatter(pointwise_grad, "dp", scatter_dimension=0, tiled=True),
        lax.psum_scatter(senone_grad, "dp", scatter_dimension=0, tiled=True),
        lax.psum_scatter(depth_grad, "dp", scatter_dimension=1, tiled=True),
        lax.psum_scatter(router_grad, "dp", scatter_dimension=1, tiled=True),
        lax.psum_scatter(scales_grad, "dp", scatter_dimension=1, tiled=True),
    )
    leading = (lax.axis_index("hid") == 0).astype(jnp.float32)
    replicated_square = sum(
        (
            jnp.sum(share * share)
            for share in (
                shares[0],
                shares[1],
                shares[2],
                shares[3],
                shares[5],
                shares[6],
                shares[7],
            )
        )
    )
    square = (
        leading * replicated_square
        + jnp.sum(shares[4] * shares[4])
        + jnp.sum(expert_grad * expert_grad)
    )
    square, count, loss_sum = lax.psum(
        (square, leading * lengths[0].astype(jnp.float32), loss_local), ("dp", "hid")
    )
    norm = jnp.sqrt(square) / count
    factor = jnp.minimum(1.0, clip_limit / (norm + 1e-06))
    input_first_new, input_second_new, input_new = adam_update(
        input_weight, shares[0] / count * factor, input_first, input_second, adam_rate, weight_decay
    )
    attention_first_new, attention_second_new, attention_new = adam_update(
        attention_in,
        shares[1] / count * factor,
        attention_first,
        attention_second,
        adam_rate,
        weight_decay,
    )
    branch_first_new, branch_second_new, branch_new = adam_update(
        branch_out, shares[2] / count * factor, branch_first, branch_second, adam_rate, weight_decay
    )
    pointwise_first_new, pointwise_second_new, pointwise_new = adam_update(
        pointwise_in,
        shares[3] / count * factor,
        pointwise_first,
        pointwise_second,
        adam_rate,
        weight_decay,
    )
    senone_first_new, senone_second_new, senone_new = adam_update(
        senone_table,
        shares[4] / count * factor,
        senone_first,
        senone_second,
        adam_rate,
        weight_decay,
    )
    depthwise_first_new, depthwise_second_new, depthwise_new = adam_update(
        depthwise,
        shares[5] / count * factor,
        depthwise_first,
        depthwise_second,
        adam_rate,
        weight_decay,
    )
    router_first_new, router_second_new, router_new = adam_update(
        router, shares[6] / count * factor, router_first, router_second, adam_rate, weight_decay
    )
    scales_first_new, scales_second_new, scales_new = adam_update(
        norm_scales, shares[7] / count * factor, scales_first, scales_second, gain_rate, 0.0
    )
    momentum_new = muon_beta * expert_momentum + expert_grad / count * factor
    owned = lax.all_to_all(
        momentum_new.reshape(4, D, -1), "hid", split_axis=0, concat_axis=2, tiled=True
    )
    owned_count = owned.shape[0]
    kind = (lax.axis_index("hid") * owned_count + jnp.arange(owned_count, dtype=jnp.int32)) % 2
    kind_scale = jnp.where(kind == 0, D ** (-0.5), 3 * lax.axis_size("dp") * FF ** (-0.5)) * (
        muon_rate * FF**0.5
    )
    orth = jnp.stack([orthogonal(owned[0])])
    update = lax.all_to_all(
        kind_scale[:, None, None] * orth, "hid", split_axis=2, concat_axis=0, tiled=True
    ).reshape(expert_weights.shape)
    experts_new = (1.0 - muon_decay) * expert_weights - update
    return (
        loss_sum,
        count,
        norm,
        input_first_new,
        input_second_new,
        input_new,
        attention_first_new,
        attention_second_new,
        attention_new,
        branch_first_new,
        branch_second_new,
        branch_new,
        pointwise_first_new,
        pointwise_second_new,
        pointwise_new,
        depthwise_first_new,
        depthwise_second_new,
        depthwise_new,
        router_first_new,
        router_second_new,
        router_new,
        senone_first_new,
        senone_second_new,
        senone_new,
        scales_first_new,
        scales_second_new,
        scales_new,
        momentum_new,
        experts_new,
    )


def solution(mesh):
    return jax.shard_map(
        on_device,
        mesh=mesh,
        in_specs=(
            P("dp", None),
            P("dp"),
            P(None, "dp", None),
            P("dp"),
            P(None, "dp"),
            P("dp", None),
            P(None, "dp", None),
            P("dp", None),
            P(None, "dp"),
            P(None, "dp", None),
            P("dp", "hid"),
            P(None, "dp"),
            P(None, None, "dp", None, "hid"),
            P(None, "dp"),
            P(None, "dp"),
            P("dp", None),
            P("dp", None),
            P(None, "dp", None),
            P(None, "dp", None),
            P("dp", None),
            P("dp", None),
            P(None, "dp"),
            P(None, "dp"),
            P(None, "dp", None),
            P(None, "dp", None),
            P("dp", "hid"),
            P("dp", "hid"),
            P(None, "dp"),
            P(None, "dp"),
            P(None, None, "dp", None, "hid"),
        ),
        out_specs=(
            P(),
            P(),
            P(),
            P(None, "dp"),
            P(None, "dp"),
            P(None, "dp"),
            P("dp", None),
            P("dp", None),
            P("dp", None),
            P(None, "dp", None),
            P(None, "dp", None),
            P(None, "dp", None),
            P("dp", None),
            P("dp", None),
            P("dp", None),
            P(None, "dp"),
            P(None, "dp"),
            P(None, "dp"),
            P(None, "dp", None),
            P(None, "dp", None),
            P(None, "dp", None),
            P("dp", "hid"),
            P("dp", "hid"),
            P("dp", "hid"),
            P(None, "dp"),
            P(None, "dp"),
            P(None, "dp"),
            P(None, None, "dp", None, "hid"),
            P(None, None, "dp", None, "hid"),
        ),
        check_vma=False,
    )
```

profile of v0, /device:TPU:1, one launch (start us, length us, event | category | flops | bytes accessed | tf_op | source)
XLA Modules:
  0.0 1518.6 jit_solution(11456095852745082531)
XLA Ops:
  13.2 27.3 %all-gather.2 = f32[32,16,7]{1,2,0:T(8,128)S(1)} all-gather(f32[1,16,7]{1,2,0:T(8,128)} %bitcast.403), channel_id=1, replica_groups=mesh['dp'=32,'hid'=4] {'dp'}, dimensions={0}, use_global_device_ids=true | all-gather | bytes 14784 | tf_op jit(solution)/shard_map/all_gather | solution.py:462
  40.6 23.9 %all_gather.36 = bf16[80,512]{0,1:T(8,128)(2,1)S(1)} all-gather(bf16[80,16]{0,1:T(8,128)(2,1)S(1)} %convert_element_type.168), channel_id=1, replica_groups=mesh['dp'=32,'hid'=4] {'dp'}, dimensions={1}, use_global_device_ids=true | all-gather | bytes 84480 | tf_op jit(solution)/shard_map/all_gather | solution.py:453
  67.4 4.4 all-to-all-start
  73.7 29.6 %all_gather.38 = f32[2,512,32]{2,1,0:T(8,128)S(1)} all-gather(f32[2,16,32]{2,1,0:T(8,128)S(1)} %copy-done.73), channel_id=1, replica_groups=mesh['dp'=32,'hid'=4] {'dp'}, dimensions={1}, use_global_device_ids=true | all-gather | bytes 135168 | tf_op jit(solution)/shard_map/all_gather | solution.py:461
  108.6 3.6 multiply_convert_fusion.4
  114.8 34.0 %all-reduce.14 = bf16[32,24,512]{2,1,0:T(8,128)(2,1)} all-reduce(f32[32,24,512]{2,1,0:T(8,128)} %fusion.85), channel_id=1, replica_groups=mesh['dp'=32,'hid'=4] {'hid'}, use_global_device_ids=true, to_apply=%region_8.9 | all-reduce | flops 393216 | bytes 2359296 | tf_op jit(solution)/shard_map/psum | solution.py:117
  148.8 7.9 all-to-all-start.1
  157.4 37.1 %all_gather.41 = f32[15,512]{0,1:T(8,128)S(1)} all-gather(f32[15,16]{0,1:T(8,128)S(1)} %copy.185), channel_id=1, replica_groups=mesh['dp'=32,'hid'=4] {'dp'}, dimensions={1}, use_global_device_ids=true | all-gather | bytes 31680 | tf_op jit(solution)/shard_map/all_gather | solution.py:460
  199.4 3.8 convolution_convert_fusion
  212.0 3.4 fusion.37
  228.4 5.1 all-to-all-start.2
  234.3 13.6 all-to-all-done.2
  247.8 3.2 multiply_convert_fusion.3
  254.8 32.0 %all-reduce.15 = bf16[32,24,512]{2,1,0:T(8,128)(2,1)} all-reduce(f32[32,24,512]{2,1,0:T(8,128)} %fusion.83), channel_id=1, replica_groups=mesh['dp'=32,'hid'=4] {'hid'}, use_global_device_ids=true, to_apply=%region_26.27 | all-reduce | flops 393216 | bytes 2359296 | tf_op jit(solution)/shard_map/psum | solution.py:117
  286.8 9.2 all-to-all-start.3
  298.5 11.9 all-to-all-done.3
  310.4 3.1 fusion.180
  318.4 8.1 all-gather.4
  326.5 8.1 all-gather.3
  340.3 45.8 %all-reduce.11.cloned.1.call-done = f32[512,512]{0,1:T(8,128)} async-done(((f32[512,512]{0,1:T(8,128)}), f32[512,512]{0,1:T(8,128)}) %all-reduce.11.cloned.1.call-update) | async-done | bytes 1048592 | tf_op jit(solution)/shard_map/psum | solution.py:329
  391.0 23.1 %all_to_all.64 = bf16[32,24,512]{2,1,0:T(8,128)(2,1)S(1)} all-to-all(bf16[32,24,512]{2,1,0:T(8,128)(2,1)S(1)} %bitcast.359), channel_id=1, replica_groups=mesh['dp'=32,'hid'=4] {'dp'}, dimensions={0} | all-to-all | bytes 1572864 | tf_op jit(solution)/shard_map/all_to_all | solution.py:111
  417.7 32.8 %all-reduce.16 = bf16[32,24,512]{2,1,0:T(8,128)(2,1)} all-reduce(f32[32,24,512]{2,1,0:T(8,128)} %fusion.81), channel_id=1, replica_groups=mesh['dp'=32,'hid'=4] {'hid'}, use_global_device_ids=true, to_apply=%region_42.43 | all-reduce | flops 393216 | bytes 2359296 | tf_op jit(solution)/shard_map/psum | solution.py:117
  450.5 9.1 all-to-all-start.5
  462.5 11.4 all-to-all-done.5
  473.9 3.4 multiply_reduce_fusion.6
  482.2 3.3 multiply_reduce_fusion.10
  508.4 4.6 all-to-all-start.6
  521.7 3.4 fusion.170
  534.0 32.3 %all-reduce.17 = bf16[32,24,512]{2,1,0:T(8,128)(2,1)} all-reduce(f32[32,24,512]{2,1,0:T(8,128)} %fusion.79), channel_id=1, replica_groups=mesh['dp'=32,'hid'=4] {'hid'}, use_global_device_ids=true, to_apply=%region_53.54 | all-reduce | flops 393216 | bytes 2359296 | tf_op jit(solution)/shard_map/psum | solution.py:117
  566.4 9.6 all-to-all-start.7
  578.0 12.3 all-to-all-done.7
  590.4 3.3 multiply_reduce_fusion.9
  597.5 3.3 fusion.77
  618.2 83.5 %all-reduce.13.cloned.1.call-done = f32[2,512,32]{2,0,1:T(2,128)} async-done(((f32[2,512,32]{2,0,1:T(2,128)}), f32[2,512,32]{2,0,1:T(2,128)}) %all-reduce.13.cloned.1.call-update) | async-done | bytes 131088
  703.0 79.1 %reduce-scatter.20.cloned.1.call-done = f32[16,1024]{1,0:T(8,128)} async-done(((f32[512,1024]{1,0:T(8,128)}), f32[16,1024]{1,0:T(8,128)}) %reduce-scatter.20.cloned.1.call-update) | async-done | bytes 65552 | tf_op jit(solution)/shard_map/reduce_scatter | solution.py:511
  790.4 71.0 %reduce-scatter.26.cloned.1.call-done = f32[16,7]{1,0:T(8,128)} async-done(((f32[512,7]{1,0:T(8,128)}), f32[16,7]{1,0:T(8,128)}) %reduce-scatter.26.cloned.1.call-update) | async-done | bytes 464
  862.8 78.2 %reduce-scatter.22.cloned.1.call-done = f32[16,80]{1,0:T(8,128)} async-done(((f32[512,80]{1,0:T(8,128)}), f32[16,80]{1,0:T(8,128)}) %reduce-scatter.22.cloned.1.call-update) | async-done | bytes 5136
  942.4 80.8 %reduce-scatter.18.cloned.1.call-done = f32[16,1024]{1,0:T(8,128)} async-done(((f32[512,1024]{1,0:T(8,128)}), f32[16,1024]{1,0:T(8,128)}) %reduce-scatter.18.cloned.1.call-update) | async-done | bytes 65552 | tf_op jit(solution)/shard_map/reduce_scatter | solution.py:510
  1024.7 80.7 %reduce-scatter.16.cloned.1.call-done = f32[2,16,512]{2,1,0:T(8,128)} async-done(((f32[2,512,512]{2,1,0:T(8,128)}), f32[2,16,512]{2,1,0:T(8,128)}) %reduce-scatter.16.cloned.1.call-update) | async-done | bytes 65552 | tf_op jit(solution)/shard_map/reduce_scatter | solution.py:509
  1106.8 82.5 %reduce-scatter.14.cloned.1.call-done = f32[16,1536]{1,0:T(8,128)} async-done(((f32[512,1536]{1,0:T(8,128)}), f32[16,1536]{1,0:T(8,128)}) %reduce-scatter.14.cloned.1.call-update) | async-done | bytes 98320 | tf_op jit(solution)/shard_map/reduce_scatter | solution.py:508
  1196.8 65.9 %all-reduce.3 = (f32[]{:T(128)}, f32[]{:T(128)}, f32[]{:T(128)}) all-reduce(f32[]{:T(128)S(6)} %sub.269, f32[]{:T(128)S(6)} %mul.1403, f32[]{:T(128)S(6)} %add.576), channel_id=1, replica_groups=mesh['dp'=32,'hid'=4] {'dp','hid'}, use_global_device_ids=true, to_apply=%region_36.37 | all-reduce | flops 3 | bytes 24 | tf_op jit(solution)/shard_map/psum | solution.py:536
  1264.1 6.6 fusion.6
  1270.6 5.0 all-to-all-start.8
  1275.7 47.8 %all-to-all-done.8 = f32[4,512,512]{2,1,0:T(8,128)} async-done(((f32[4,512,512]{2,1,0:T(8,128)}), f32[4,512,512]{2,1,0:T(8,128)}, u32[]{:S(2)}, u32[]{:S(2)}) %all-to-all-start.8) | async-done | bytes 4194336 | tf_op jit(solution)/shard_map/all_to_all | solution.py:586
  1323.5 3.9 multiply_reduce_fusion.1
  1328.0 4.7 fusion.14
  1332.7 5.2 copy.195
  1338.0 9.5 fusion.27
  1349.3 5.3 copy.196
  1354.7 9.6 multiply_add_fusion.4
  1364.3 6.9 fusion.192
  1373.1 7.3 multiply_add_fusion.3
  1380.5 6.9 fusion.193
  1389.5 6.9 multiply_add_fusion.2
  1396.4 7.1 fusion.194
  1405.4 6.9 multiply_add_fusion.1
  1412.4 7.3 fusion.195
  1421.6 8.5 multiply_bitcast_fusion
  1430.1 10.9 copy.197
  1441.3 5.2 all-to-all-start.9
  1457.4 5.9 fusion.263
  1463.3 30.1 %all-to-all-done.9 = f32[1,512,2048]{1,0,2:T(1,128)} async-done(((f32[1,512,2048]{1,0,2:T(1,128)}), f32[1,512,2048]{1,0,2:T(1,128)}, u32[]{:S(2)}, u32[]{:S(2)}) %all-to-all-start.9) | async-done | bytes 4194336 | tf_op jit(solution)/shard_map/all_to_all | solution.py:595
  1493.4 10.9 copy.198
  1504.2 6.5 multiply_subtract_fusion
  (601 shorter events, 176.5 us)
Async XLA Ops:
  7.2 57.4 %copy-start = (bf16[512,80]{0,1:T(8,128)(2,1)S(1)}, bf16[512,80]{0,1:T(8,128)(2,1)}, u32[]{:S(2)}) copy-start(bf16[512,80]{0,1:T(8,128)(2,1)} %param.32) | copy-start | bytes 245764
  7.2 192.1 %all-gather.10.cloned.1.call-start = ((), (), s32[]{:S(2)}) async-start(), calls=%async_computation.17 | async-start | bytes 1622016 | tf_op jit(solution)/shard_map/all_gather | solution.py:454
  8.8 206.6 %all-gather.12.cloned.1.call-start = ((), (), s32[]{:S(2)}) async-start(), calls=%async_computation.18 | async-start | bytes 1081344 | tf_op jit(solution)/shard_map/all_gather | solution.py:455
  11.7 507.1 %copy-start.62 = (s32[1,512,1]{1,2,0:T(1,128)}, s32[1,512,1]{1,2,0:T(1,128)S(1)}, u32[]{:S(2)}) copy-start(s32[1,512,1]{1,2,0:T(1,128)S(1)} %get-tuple-element.427) | copy-start | bytes 6148
  64.9 38.4 %copy-start.86 = (f32[512]{0:T(512)}, f32[512]{0:T(512)S(1)}, u32[]{:S(2)}) copy-start(f32[512]{0:T(512)S(1)} %broadcast_multiply_fusion.16) | copy-start | bytes 6148
  65.1 38.2 %copy-start.111 = (f32[512]{0:T(512)}, f32[512]{0:T(512)S(1)}, u32[]{:S(2)}) copy-start(f32[512]{0:T(512)S(1)} %add_rsqrt_fusion.5) | copy-start | bytes 6148
  65.1 132.3 %copy-start.164 = (s32[512]{0:T(512)}, s32[512]{0:T(512)S(1)}, u32[]{:S(2)}) copy-start(s32[512]{0:T(512)S(1)} %multiply_add_fusion.21) | copy-start | bytes 6148
  65.7 37.5 %copy-start.108 = (f32[1,512]{1,0:T(1,128)}, f32[1,512]{1,0:T(1,128)S(1)}, u32[]{:S(2)}) copy-start(f32[1,512]{1,0:T(1,128)S(1)} %get-tuple-element.425) | copy-start | bytes 6148
  65.7 133.6 %copy-start.144 = (f32[1,512]{1,0:T(1,128)}, f32[1,512]{1,0:T(1,128)S(1)}, u32[]{:S(2)}) copy-start(f32[1,512]{1,0:T(1,128)S(1)} %get-tuple-element.424) | copy-start | bytes 6148
  65.7 158.6 %copy-start.161 = (f32[1,512]{1,0:T(1,128)}, f32[1,512]{1,0:T(1,128)S(1)}, u32[]{:S(2)}) copy-start(f32[1,512]{1,0:T(1,128)S(1)} %get-tuple-element.422) | copy-start | bytes 6148
  65.7 322.7 %copy-start.75 = (f32[1,512]{1,0:T(1,128)}, f32[1,512]{1,0:T(1,128)S(1)}, u32[]{:S(2)}) copy-start(f32[1,512]{1,0:T(1,128)S(1)} %get-tuple-element.419) | copy-start | bytes 6148
  65.8 411.6 %copy-start.91 = (f32[1,512]{1,0:T(1,128)}, f32[1,512]{1,0:T(1,128)S(1)}, u32[]{:S(2)}) copy-start(f32[1,512]{1,0:T(1,128)S(1)} %get-tuple-element.420) | copy-start | bytes 6148
  65.8 425.3 %copy-start.89 = (f32[1,512]{1,0:T(1,128)}, f32[1,512]{1,0:T(1,128)S(1)}, u32[]{:S(2)}) copy-start(f32[1,512]{1,0:T(1,128)S(1)} %get-tuple-element.423) | copy-start | bytes 6148
  67.4 41.2 %all-to-all-start = ((bf16[32,24,512]{2,1,0:T(8,128)(2,1)}), bf16[32,24,512]{2,1,0:T(8,128)(2,1)}, u32[]{:S(2)}, u32[]{:S(2)}) async-start(bf16[32,24,512]{2,1,0:T(8,128)(2,1)} %bitcast.11), calls=%async_computation | async-start | bytes 1572864 | tf_op jit(solution)/shard_map/all_to_all | solution.py:111
  71.8 145.6 %all-gather.14.cloned.1.call-start = ((), (), s32[]{:S(2)}) async-start(), calls=%async_computation.19 | async-start | bytes 1081344 | tf_op jit(solution)/shard_map/all_gather | solution.py:456
  105.0 89.5 %copy-start.81 = (f32[512]{0:T(512)}, f32[512]{0:T(512)S(1)}, u32[]{:S(2)}) copy-start(f32[512]{0:T(512)S(1)} %get-tuple-element.434) | copy-start | bytes 6148
  106.0 88.6 %copy-start.99 = (f32[512]{0:T(512)}, f32[512]{0:T(512)S(1)}, u32[]{:S(2)}) copy-start(f32[512]{0:T(512)S(1)} %fusion.139) | copy-start | bytes 6148
  114.8 42.5 %copy-start.104 = (f32[15,16]{1,0:T(8,128)S(1)}, f32[15,16]{1,0:T(8,128)}, u32[]{:S(2)}) copy-start(f32[15,16]{1,0:T(8,128)} %param.40) | copy-start | bytes 2884
  148.8 48.6 %all-to-all-start.1 = ((bf16[32,24,512]{2,1,0:T(8,128)(2,1)}), bf16[32,24,512]{2,1,0:T(8,128)(2,1)S(1)}, u32[]{:S(2)}, u32[]{:S(2)}) async-start(bf16[32,24,512]{2,1,0:T(8,128)(2,1)} %all-reduce.14), calls=%async_computation.1 | async-start | bytes 1572864 | tf_op jit(solution)/shard_map/all_to_all | solution.py:118
  196.7 24.4 %copy-start.114 = (f32[512]{0:T(512)}, f32[512]{0:T(512)S(1)}, u32[]{:S(2)}) copy-start(f32[512]{0:T(512)S(1)} %get-tuple-element.347) | copy-start | bytes 6148
  196.7 24.4 %copy-start.116 = (f32[512]{0:T(512)}, f32[512]{0:T(512)S(1)}, u32[]{:S(2)}) copy-start(f32[512]{0:T(512)S(1)} %get-tuple-element.348) | copy-start | bytes 6148
  196.7 24.4 %copy-start.118 = (f32[512]{0:T(512)}, f32[512]{0:T(512)S(1)}, u32[]{:S(2)}) copy-start(f32[512]{0:T(512)S(1)} %get-tuple-element.349) | copy-start | bytes 6148
  196.7 24.4 %copy-start.120 = (f32[512]{0:T(512)}, f32[512]{0:T(512)S(1)}, u32[]{:S(2)}) copy-start(f32[512]{0:T(512)S(1)} %get-tuple-element.350) | copy-start | bytes 6148
  199.1 305.7 %copy-start.93 = (f32[512]{0:T(512)}, f32[512]{0:T(512)S(1)}, u32[]{:S(2)}) copy-start(f32[512]{0:T(512)S(1)} %broadcast_multiply_fusion.15) | copy-start | bytes 6148
  217.1 273.9 %copy-start.77 = (f32[512]{0:T(512)}, f32[512]{0:T(512)S(1)}, u32[]{:S(2)}) copy-start(f32[512]{0:T(512)S(1)} %broadcast_multiply_fusion.14) | copy-start | bytes 6148
  217.3 273.8 %copy-start.95 = (f32[512]{0:T(512)}, f32[512]{0:T(512)S(1)}, u32[]{:S(2)}) copy-start(f32[512]{0:T(512)S(1)} %add_rsqrt_fusion.3) | copy-start | bytes 6148
  225.8 70.7 %copy-start.5 = (f32[512,512]{0,1:T(8,128)}, f32[512,512]{0,1:T(8,128)S(1)}, u32[]{:S(2)}) copy-start(f32[512,512]{0,1:T(8,128)S(1)} %get-tuple-element.442) | copy-start | bytes 3145732
  225.8 251.5 %copy-start.79 = (f32[512]{0:T(512)}, f32[512]{0:T(512)S(1)}, u32[]{:S(2)}) copy-start(f32[512]{0:T(512)S(1)} %broadcast_multiply_fusion.13) | copy-start | bytes 6148
  226.0 251.3 %copy-start.97 = (f32[512]{0:T(512)}, f32[512]{0:T(512)S(1)}, u32[]{:S(2)}) copy-start(f32[512]{0:T(512)S(1)} %add_rsqrt_fusion.1) | copy-start | bytes 6148
  228.4 19.4 %all-to-all-start.2 = ((bf16[32,24,512]{2,1,0:T(8,128)(2,1)}), bf16[32,24,512]{2,1,0:T(8,128)(2,1)}, u32[]{:S(2)}, u32[]{:S(2)}) async-start(bf16[32,24,512]{2,1,0:T(8,128)(2,1)} %bitcast.358), calls=%async_computation.2 | async-start | bytes 1572864 | tf_op jit(solution)/shard_map/all_to_all | solution.py:111
  233.6 80.2 %all-gather.16.cloned.1.call-start = ((), (), s32[]{:S(2)}) async-start(), calls=%async_computation.20 | async-start | bytes 1081344 | tf_op jit(solution)/shard_map/all_gather | solution.py:457
  286.8 23.6 %all-to-all-start.3 = ((bf16[32,24,512]{2,1,0:T(8,128)(2,1)}), bf16[32,24,512]{2,1,0:T(8,128)(2,1)}, u32[]{:S(2)}, u32[]{:S(2)}) async-start(bf16[32,24,512]{2,1,0:T(8,128)(2,1)} %all-reduce.15), calls=%async_computation.3 | async-start | bytes 1572864 | tf_op jit(solution)/shard_map/all_to_all | solution.py:118
  296.0 90.1 %all-reduce.11.cloned.1.call-start = ((), (), s32[]{:S(2)}) async-start(), calls=%async_computation.21 | async-start | bytes 2097152 | tf_op jit(solution)/shard_map/psum | solution.py:329
  298.4 161.2 %copy-start.84 = (f32[512]{0:T(512)}, f32[512]{0:T(512)S(1)}, u32[]{:S(2)}) copy-start(f32[512]{0:T(512)S(1)} %get-tuple-element.445) | copy-start | bytes 6148
  298.4 161.2 %copy-start.102 = (f32[512]{0:T(512)}, f32[512]{0:T(512)S(1)}, u32[]{:S(2)}) copy-start(f32[512]{0:T(512)S(1)} %fusion.141) | copy-start | bytes 6148
  313.5 75.0 %copy-start.66 = (f32[512]{0:T(512)}, f32[512]{0:T(512)S(1)}, u32[]{:S(2)}) copy-start(f32[512]{0:T(512)S(1)} %broadcast_multiply_fusion.12) | copy-start | bytes 6148
  313.7 74.8 %copy-start.76 = (f32[512]{0:T(512)}, f32[512]{0:T(512)S(1)}, u32[]{:S(2)}) copy-start(f32[512]{0:T(512)S(1)} %add_rsqrt_fusion) | copy-start | bytes 6148
  389.0 26.0 %copy-start.29 = (f32[512,512]{0,1:T(8,128)}, f32[512,512]{0,1:T(8,128)S(1)}, u32[]{:S(2)}) copy-start(f32[512,512]{0,1:T(8,128)S(1)} %get-tuple-element.409) | copy-start | bytes 3145732
  389.0 25.1 %copy-start.19 = (bf16[2,2,512,512]{3,2,1,0:T(8,128)(2,1)S(1)}, bf16[2,2,512,512]{3,2,1,0:T(8,128)(2,1)}, u32[]{:S(2)}) copy-start(bf16[2,2,512,512]{3,2,1,0:T(8,128)(2,1)} %copy-done.18) | copy-start | bytes 6291460
  389.0 25.1 %copy-start.195 = (f32[768,512]{1,0:T(8,128)S(1)}, f32[768,512]{1,0:T(8,128)}, u32[]{:S(2)}) copy-start(f32[768,512]{1,0:T(8,128)} %get-tuple-element.444) | copy-start | bytes 4718596
  417.7 41.9 %copy-start.157 = (f32[512]{0:T(512)S(1)}, f32[512]{0:T(512)}, u32[]{:S(2)}) copy-start(f32[512]{0:T(512)} %copy-done.156) | copy-start | bytes 6148
  450.5 23.5 %all-to-all-start.5 = ((bf16[32,24,512]{2,1,0:T(8,128)(2,1)}), bf16[32,24,512]{2,1,0:T(8,128)(2,1)}, u32[]{:S(2)}, u32[]{:S(2)}) async-start(bf16[32,24,512]{2,1,0:T(8,128)(2,1)} %all-reduce.16), calls=%async_computation.5 | async-start | bytes 1572864 | tf_op jit(solution)/shard_map/all_to_all | solution.py:118
  508.4 19.0 %all-to-all-start.6 = ((bf16[32,24,512]{2,1,0:T(8,128)(2,1)}), bf16[32,24,512]{2,1,0:T(8,128)(2,1)}, u32[]{:S(2)}, u32[]{:S(2)}) async-start(bf16[32,24,512]{2,1,0:T(8,128)(2,1)} %bitcast.357), calls=%async_computation.6 | async-start | bytes 1572864 | tf_op jit(solution)/shard_map/all_to_all | solution.py:111
  513.1 103.7 %reduce-scatter.24.cloned.1.call-start = ((), (), s32[]{:S(2)}) async-start(), calls=%async_computation.27 | async-start | bytes 270336
  518.1 183.6 %all-reduce.13.cloned.1.call-start = ((), (), s32[]{:S(2)}) async-start(), calls=%async_computation.29 | async-start | bytes 1048576
  521.7 260.5 %reduce-scatter.20.cloned.1.call-start = ((), (), s32[]{:S(2)}) async-start(), calls=%async_computation.25 | async-start | bytes 2162688 | tf_op jit(solution)/shard_map/reduce_scatter | solution.py:511
  534.0 42.0 %copy-start.23 = (f32[2,512,32]{2,1,0:T(8,128)S(1)}, f32[2,512,32]{2,1,0:T(8,128)}, u32[]{:S(2)}) copy-start(f32[2,512,32]{2,1,0:T(8,128)} %copy-done.22) | copy-start | bytes 393220
  534.0 42.0 %copy-start.63 = (s32[1,512,1]{1,2,0:T(1,128)S(1)}, s32[1,512,1]{1,2,0:T(1,128)}, u32[]{:S(2)}) copy-start(s32[1,512,1]{1,2,0:T(1,128)} %copy-done.62) | copy-start | bytes 6148
  534.0 42.0 %copy-start.83 = (f32[512]{0:T(512)S(1)}, f32[512]{0:T(512)}, u32[]{:S(2)}) copy-start(f32[512]{0:T(512)} %copy-done.81) | copy-start | bytes 6148
  534.0 42.1 %copy-start.101 = (f32[512]{0:T(512)S(1)}, f32[512]{0:T(512)}, u32[]{:S(2)}) copy-start(f32[512]{0:T(512)} %copy-done.99) | copy-start | bytes 6148
  534.0 42.1 %copy-start.150 = (f32[512]{0:T(512)S(1)}, f32[512]{0:T(512)}, u32[]{:S(2)}) copy-start(f32[512]{0:T(512)} %copy-done.149) | copy-start | bytes 6148
  534.0 56.3 %copy-start.88 = (f32[512]{0:T(512)S(1)}, f32[512]{0:T(512)}, u32[]{:S(2)}) copy-start(f32[512]{0:T(512)} %copy-done.86) | copy-start | bytes 6148
  534.0 56.3 %copy-start.110 = (f32[1,512]{1,0:T(1,128)S(1)}, f32[1,512]{1,0:T(1,128)}, u32[]{:S(2)}) copy-start(f32[1,512]{1,0:T(1,128)} %copy-done.108) | copy-start | bytes 6148
  534.0 56.3 %copy-start.113 = (f32[512]{0:T(512)S(1)}, f32[512]{0:T(512)}, u32[]{:S(2)}) copy-start(f32[512]{0:T(512)} %copy-done.111) | copy-start | bytes 6148
  534.0 56.3 %copy-start.166 = (s32[512]{0:T(512)S(1)}, s32[512]{0:T(512)}, u32[]{:S(2)}) copy-start(s32[512]{0:T(512)} %copy-done.164) | copy-start | bytes 6148
  566.4 23.9 %all-to-all-start.7 = ((bf16[32,24,512]{2,1,0:T(8,128)(2,1)}), bf16[32,24,512]{2,1,0:T(8,128)(2,1)}, u32[]{:S(2)}, u32[]{:S(2)}) async-start(bf16[32,24,512]{2,1,0:T(8,128)(2,1)} %all-reduce.17), calls=%async_computation.7 | async-start | bytes 1572864 | tf_op jit(solution)/shard_map/all_to_all | solution.py:118
  575.9 285.5 %reduce-scatter.26.cloned.1.call-start = ((), (), s32[]{:S(2)}) async-start(), calls=%async_computation.28 | async-start | bytes 270336
  594.7 346.3 %reduce-scatter.22.cloned.1.call-start = ((), (), s32[]{:S(2)}) async-start(), calls=%async_computation.26 | async-start | bytes 270336
  597.4 425.8 %reduce-scatter.18.cloned.1.call-start = ((), (), s32[]{:S(2)}) async-start(), calls=%async_computation.24 | async-start | bytes 2162688 | tf_op jit(solution)/shard_map/reduce_scatter | solution.py:510
  600.8 504.6 %reduce-scatter.16.cloned.1.call-start = ((), (), s32[]{:S(2)}) async-start(), calls=%async_computation.23 | async-start | bytes 2162688 | tf_op jit(solution)/shard_map/reduce_scatter | solution.py:509
  606.4 583.0 %reduce-scatter.14.cloned.1.call-start = ((), (), s32[]{:S(2)}) async-start(), calls=%async_computation.22 | async-start | bytes 3244032 | tf_op jit(solution)/shard_map/reduce_scatter | solution.py:508
  616.6 167.1 %copy-start.40 = (bf16[768,512]{1,0:T(8,128)(2,1)S(1)}, bf16[768,512]{1,0:T(8,128)(2,1)}, u32[]{:S(2)}) copy-start(bf16[768,512]{1,0:T(8,128)(2,1)} %copy-done.39) | copy-start | bytes 2359300
  1270.6 52.8 %all-to-all-start.8 = ((f32[4,512,512]{2,1,0:T(8,128)}), f32[4,512,512]{2,1,0:T(8,128)}, u32[]{:S(2)}, u32[]{:S(2)}) async-start(f32[4,512,512]{2,1,0:T(8,128)} %bitcast.334), calls=%async_computation.12 | async-start | bytes 8388608 | tf_op jit(solution)/shard_map/all_to_all | solution.py:586
  1441.3 52.1 %all-to-all-start.9 = ((f32[1,512,2048]{1,0,2:T(1,128)}), f32[1,512,2048]{1,0,2:T(1,128)}, u32[]{:S(2)}, u32[]{:S(2)}) async-start(f32[1,512,2048]{1,0,2:T(1,128)} %copy.197), calls=%async_computation.13 | async-start | bytes 8388608 | tf_op jit(solution)/shard_map/all_to_all | solution.py:595
  (156 other events, 1046.2 us)
Sparse Core Ops, SparseCore 0:
  10.9 47.0 all-gather.9
  60.8 45.7 all-gather.11
  109.5 42.0 all-gather.13
  236.9 42.8 all-gather.15
  340.4 45.6 all-reduce.10
  518.2 76.6 reduce-scatter.23
  598.4 103.2 all-reduce.12
  705.2 76.8 reduce-scatter.19
  785.6 75.8 reduce-scatter.25
  864.7 76.2 reduce-scatter.21
  944.6 78.6 reduce-scatter.17
  1027.2 78.1 reduce-scatter.15
  1109.6 79.7 reduce-scatter.13
where the time goes:
time: 1530 us; the launch traced here: 1520 us
  waiting for transfers between devices  731 us (48%)
  blocking collectives  354 us (23%)
  matrix products  187 us (12%)
  other arithmetic  87.4 us (6%)
  local copies, waits for them, and re-layouts  68.5 us (4%)
  starting transfers between devices  61.4 us (4%)
  between operations  28.5 us (2%)
    unnamed x17, waiting for transfers between devices  233 us
    psum x4, blocking collectives, return_from_experts(): total = lax.psum(shaped, 'hid')  131 us
    dot_general x21, matrix products, exact_dot(): return jnp.dot(left, right, precision=lax.Precision.HIGHEST)  98 us
    reduce_scatter x1, waiting for transfers between devices, on_device(): lax.psum_scatter(attention_grad, 'dp', scatter_dimension=0, tiled=True)  82.5 us
    reduce_scatter x1, waiting for transfers between devices, on_device(): lax.psum_scatter(pointwise_grad, 'dp', scatter_dimension=0, tiled=True)  80.8 us
    reduce_scatter x1, waiting for transfers between devices, on_device(): lax.psum_scatter(branch_grad, 'dp', scatter_dimension=1, tiled=True)  80.7 us
    reduce_scatter x1, waiting for transfers between devices, on_device(): lax.psum_scatter(senone_grad, 'dp', scatter_dimension=0, tiled=True)  79.1 us
    psum x1, blocking collectives, on_device(): lax.psum((square, leading * lengths[0].astype(jnp.float32), loss_local),...  65.9 us
  transfers between devices with their start and end apart: 22, of which 15 were waited for; matrix products, arithmetic and copies ran while one was open for 8% of the time, Pallas kernels for 0%

commit v1 on v0

v1 whole, which is shorter than its diff:
```python
import jax
import jax.numpy as jnp
from jax import lax
from jax.experimental import pallas as pl
from jax.experimental.pallas import tpu as pltpu
from jax.sharding import PartitionSpec as P

D = 512
HEADS = 8
HEAD_DIM = 64
FF = 2048
STEP = 10


clip_limit = 0.02
beta_one = 0.9
beta_two = 0.999
adam_epsilon = 1e-08
adam_rate = 0.2
gain_rate = 0.6
weight_decay = 0.01
muon_beta = 0.95
muon_rate = 1.0
muon_decay = 0.01
newton_first = 3.4445
newton_second = -4.775
newton_third = 2.0315


def shift(values, step):
    size = lax.axis_size("hid")
    return lax.ppermute(values, "hid", [(i, (i + step) % size) for i in range(size)])


def gather_near(values):
    return [values] + [shift(values, step) for step in range(1, lax.axis_size("hid"))]


def gather_far(values):
    half = values.shape[0] // 2
    before, after = shift(values, 1), shift(values, -1)
    across = jnp.concatenate([shift(before[:half], 1), shift(after[half:], -1)])
    return [values, before, across, after]


def in_order(blocks, axis):
    size = len(blocks)
    width = blocks[0].shape[axis]
    rising = [blocks[(-1 - place) % size] for place in range(size)]
    doubled = jnp.concatenate(rising + rising[:-1], axis)
    begin = (size - 1 - lax.axis_index("hid")) % size
    return lax.dynamic_slice_in_dim(doubled, begin * width, size * width, axis)


def own_part(values, axis):
    width = values.shape[axis] // lax.axis_size("hid")
    return lax.dynamic_slice_in_dim(values, lax.axis_index("hid") * width, width, axis)


def exchange_rows(values):
    return lax.all_to_all(values, "dp", split_axis=0, concat_axis=0, tiled=True)


def summed_shares(values):
    owners = lax.axis_size("dp")
    moved = exchange_rows(to_low(values).reshape(owners, values.shape[0] // owners, -1))
    return jnp.sum(moved.astype(jnp.float32), 0)


def to_low(values):
    return values.astype(jnp.bfloat16)


def dot_low(left, right):
    return jnp.dot(left, right, preferred_element_type=jnp.float32)


def dot_left(left, right):
    return lax.dot_general(
        left, right, (((0,), (0,)), ((), ())), preferred_element_type=jnp.float32
    )


def dot_right(left, right):
    return lax.dot_general(
        left, right, (((1,), (1,)), ((), ())), preferred_element_type=jnp.float32
    )


def exact_dot(left, right):
    return jnp.dot(left, right, precision=lax.Precision.HIGHEST)


def norm_forward(values, gain):
    centered = values - jnp.mean(values, -1, keepdims=True)
    inverse = lax.rsqrt(jnp.mean(centered * centered, -1, keepdims=True) + 1e-05)
    unit = centered * inverse
    return (unit * gain, unit, inverse)


def norm_backward(grad, unit, inverse, gain):
    scaled = grad * gain
    back = inverse * (
        scaled
        - jnp.mean(scaled, -1, keepdims=True)
        - unit * jnp.mean(scaled * unit, -1, keepdims=True)
    )
    return (back, jnp.sum(grad * unit, 0))


def silu_slope(values):
    sigma = jax.nn.sigmoid(values)
    return sigma * (1.0 + values * (1.0 - sigma))


def two_parts(values):
    high = to_low(values)
    return high, to_low(values - high.astype(jnp.float32))


def close_dot(left, right):
    return dot_low(left[0], right[0]) + (dot_low(left[0], right[1]) + dot_low(left[1], right[0]))


def orthogonal_kernel(factor_ref, momentum_ref, grad_ref, out_ref, matrix_ref):
    pieces = momentum_ref.shape[0]
    gram = jnp.zeros((D, D), jnp.float32)
    for piece in range(pieces):
        current = muon_beta * momentum_ref[piece] + factor_ref[0] * grad_ref[piece].astype(
            jnp.float32
        )
        matrix_ref[piece] = current
        high, low = two_parts(current)
        cross = dot_right(high, low)
        gram = gram + (dot_right(high, high) + (cross + cross.T))
    row = lax.broadcasted_iota(jnp.int32, (D, D), 0)
    column = lax.broadcasted_iota(jnp.int32, (D, D), 1)
    square = jnp.sum(jnp.where(row == column, gram, 0.0))
    inverse = 1.0 / (jnp.sqrt(square) + 1e-07)
    gram = gram * (inverse * inverse)
    identity = jnp.where(row == column, newton_first, 0.0)
    total = None
    for turn in range(5):
        parts = two_parts(gram)
        poly = identity + newton_second * gram + newton_third * close_dot(parts, parts)
        poly_parts = two_parts(poly)
        total = poly if total is None else close_dot(poly_parts, two_parts(total))
        if turn < 4:
            gram = close_dot(poly_parts, two_parts(close_dot(poly_parts, parts)))
    total_parts = two_parts(total * (inverse * factor_ref[1]))
    for piece in range(pieces):
        out_ref[piece] = to_low(close_dot(total_parts, two_parts(matrix_ref[piece])))


def orthogonal(scalars, momentum, grad):
    return pl.pallas_call(
        orthogonal_kernel,
        out_shape=jax.ShapeDtypeStruct(momentum.shape, jnp.bfloat16),
        in_specs=[
            pl.BlockSpec(memory_space=pltpu.SMEM),
            pl.BlockSpec(memory_space=pltpu.VMEM),
            pl.BlockSpec(memory_space=pltpu.VMEM),
        ],
        out_specs=pl.BlockSpec(memory_space=pltpu.VMEM),
        scratch_shapes=[pltpu.VMEM(momentum.shape, jnp.float32)],
        compiler_params=pltpu.CompilerParams(vmem_limit_bytes=48 * 1024 * 1024),
        cost_estimate=pl.CostEstimate(
            flops=30_000_000_000, bytes_accessed=10_000_000, transcendentals=0
        ),
    )(scalars, momentum, grad)


def adam_update(weight, grad, first, second, rate, decay):
    first_new = beta_one * first + (1.0 - beta_one) * grad
    second_new = beta_two * second + (1.0 - beta_two) * grad * grad
    corrected = (
        first_new
        / (1.0 - beta_one**STEP)
        / (jnp.sqrt(second_new / (1.0 - beta_two**STEP)) + adam_epsilon)
    )
    return (first_new, second_new, weight - rate * (corrected + decay * weight))


def mixture_forward(values, gain, router_part, weights_in, weights_out, route_rows):
    experts, splits = lax.axis_size("dp"), lax.axis_size("hid")
    capacity = 3 * values.shape[0] // (2 * experts)
    share = capacity // splits
    normed, unit, inverse = norm_forward(values, gain)
    onehot_int = (route_rows[:, None] == jnp.arange(experts, dtype=jnp.int32)[None, :]).astype(
        jnp.int32
    )
    earlier = jnp.cumsum(onehot_int, 0) - onehot_int
    slot = jnp.sum(earlier * onehot_int, 1)
    turned = (lax.axis_index("hid") - slot // share) % splits
    position = (turned * experts + route_rows) * share + slot % share
    dispatch = (
        jnp.arange(experts * capacity, dtype=jnp.int32)[:, None] == position[None, :]
    ).astype(jnp.bfloat16)
    onehot = onehot_int.astype(jnp.float32)
    own = dispatch[: experts * share]
    rows = exchange_rows(to_low(dot_low(own, to_low(normed))))
    chances = jax.nn.softmax(exact_dot(normed, router_part), -1)
    gate = jnp.sum(chances * onehot, 1)
    active = [dot_low(rows, weight) for weight in weights_in]
    hidden = [to_low(jax.nn.silu(part)) for part in active]
    returned = sum(dot_right(part, weight) for part, weight in zip(hidden, weights_out))
    back = jnp.concatenate(gather_near(exchange_rows(to_low(returned))))
    expert_out = dot_left(dispatch, back)
    kept = (
        unit,
        inverse,
        normed,
        chances,
        onehot,
        gate,
        dispatch,
        rows,
        active,
        hidden,
        expert_out,
    )
    return (0.5 * gate[:, None] * expert_out, kept)


def feature_pieces(rows, parts):
    splits = lax.axis_size("hid")
    return (
        jnp.concatenate(gather_near(rows)),
        jnp.concatenate(
            [parts[0]] + [shift(parts[splits - step], step) for step in range(1, splits)]
        ),
    )


def mixture_backward(grad, gain, router_part, weights_in, weights_out, kept):
    unit, inverse, normed, chances, onehot, gate, dispatch, rows, active, hidden, expert_out = kept
    experts, splits = lax.axis_size("dp"), lax.axis_size("hid")
    own = dispatch[: dispatch.shape[0] // splits]
    branch = 0.5 * grad
    rows_grad = exchange_rows(to_low(dot_low(own, to_low(gate[:, None] * branch))))
    active_grad = [
        to_low(dot_low(rows_grad, weight) * silu_slope(part))
        for weight, part in zip(weights_out, active)
    ]
    returned = sum(dot_right(part, weight) for part, weight in zip(active_grad, weights_in))
    back = jnp.concatenate(gather_near(exchange_rows(to_low(returned))))
    all_rows, all_active_grad = feature_pieces(rows, active_grad)
    all_rows_grad, all_hidden = feature_pieces(rows_grad, hidden)
    in_grad = dot_left(all_rows, all_active_grad)
    out_grad = dot_left(all_rows_grad, all_hidden)
    gate_grad = jnp.sum(branch * expert_out, 1)
    logit_grad = (gate * gate_grad)[:, None] * (onehot - chances)
    router_grad = exact_dot(normed.T, logit_grad)
    normed_grad = exact_dot(logit_grad, router_part.T) + dot_left(dispatch, back)
    values_grad, gain_grad = norm_backward(normed_grad, unit, inverse, gain)
    return (grad + values_grad, gain_grad, router_grad, in_grad, out_grad)


def attention_scores(queries, keys, valid):
    scores = jnp.einsum(
        "qhd,khd->hqk", queries, keys, preferred_element_type=jnp.float32
    ) * HEAD_DIM ** (-0.5)
    return jnp.where(valid[None, None, :] > 0, scores, -1e30)


def attention_forward(values, gain, weight_in, weight_out, valid):
    tokens = values.shape[0]
    normed, unit, inverse = norm_forward(values, gain)
    low_normed = to_low(normed)
    shaped = to_low(dot_low(low_normed, weight_in)).reshape(tokens, 3, HEADS, HEAD_DIM)
    queries, keys, contents = (shaped[:, 0], shaped[:, 1], shaped[:, 2])
    scores = attention_scores(queries, keys, valid)
    top = jnp.max(scores, -1, keepdims=True)
    raised = jnp.exp(scores - top)
    total = jnp.sum(raised, -1, keepdims=True)
    log_total = top + jnp.log(total)
    mixed = jnp.einsum(
        "hqk,khd->qhd", to_low(raised / total), contents, preferred_element_type=jnp.float32
    )
    context = to_low(mixed.reshape(tokens, -1))
    kept = (unit, inverse, low_normed, queries, keys, contents, log_total, context)
    return (dot_low(context, weight_out), kept)


def attention_backward(grad, gain, weight_in, weight_out, valid, kept):
    unit, inverse, low_normed, queries, keys, contents, log_total, context = kept
    tokens = grad.shape[0]
    low_grad = to_low(grad)
    out_grad = dot_left(context, own_part(low_grad, 1))
    context_grad = to_low(dot_right(low_grad, weight_out)).reshape(tokens, HEADS, HEAD_DIM)
    weights = jnp.exp(attention_scores(queries, keys, valid) - log_total)
    weight_grad = jnp.einsum(
        "qhd,khd->hqk", context_grad, contents, preferred_element_type=jnp.float32
    )
    content_grad = jnp.einsum(
        "hqk,qhd->khd", to_low(weights), context_grad, preferred_element_type=jnp.float32
    )
    score_grad = to_low(weights * (weight_grad - jnp.sum(weight_grad * weights, -1, keepdims=True)))
    query_grad = jnp.einsum(
        "hqk,khd->qhd", score_grad, keys, preferred_element_type=jnp.float32
    ) * HEAD_DIM ** (-0.5)
    key_grad = jnp.einsum(
        "hqk,qhd->khd", score_grad, queries, preferred_element_type=jnp.float32
    ) * HEAD_DIM ** (-0.5)
    project_grad = to_low(jnp.stack([query_grad, key_grad, content_grad], 1).reshape(tokens, -1))
    in_grad = dot_left(low_normed, own_part(project_grad, 1))
    values_grad, gain_grad = norm_backward(dot_right(project_grad, weight_in), unit, inverse, gain)
    return (grad + values_grad, gain_grad, in_grad, out_grad)


def convolution_forward(values, gains, weight_in, depth, weight_out, valid):
    tokens = values.shape[0]
    normed, unit, inverse = norm_forward(values, gains[2])
    low_normed = to_low(normed)
    project = dot_low(low_normed, weight_in)
    width = project.shape[1] // 2
    linear = project[:, :width]
    gating = jax.nn.sigmoid(project[:, width:])
    mixed = linear * gating * valid[:, None]
    reach = (depth.shape[0] - 1) // 2
    padded = jnp.pad(mixed, ((reach, reach), (0, 0)))
    deep = jnp.zeros_like(mixed)
    for offset in range(depth.shape[0]):
        deep = deep + depth[offset] * padded[offset : offset + tokens]
    count = jnp.sum(valid)
    mask = valid[:, None]
    mean = jnp.sum(mask * deep, 0) / count
    spread = jnp.sum(mask * deep * deep, 0) / count - mean * mean
    scale = lax.rsqrt(spread + 1e-05)
    unit_batch = (deep - mean) * scale
    shifted = unit_batch * gains[5] + gains[6]
    activated = to_low(jax.nn.silu(shifted))
    kept = (
        unit,
        inverse,
        low_normed,
        linear,
        gating,
        padded,
        scale,
        unit_batch,
        shifted,
        activated,
    )
    return (dot_low(activated, weight_out), kept)


def convolution_backward(grad, gains, weight_in, depth, weight_out, valid, kept):
    unit, inverse, low_normed, linear, gating, padded, scale, unit_batch, shifted, activated = kept
    tokens = grad.shape[0]
    low_grad = to_low(grad)
    out_grad = dot_left(activated, own_part(low_grad, 1))
    shifted_grad = dot_right(low_grad, weight_out) * silu_slope(shifted)
    gamma_grad = jnp.sum(shifted_grad * unit_batch, 0)
    beta_grad = jnp.sum(shifted_grad, 0)
    unit_grad = shifted_grad * gains[5]
    count = jnp.sum(valid)
    mask = valid[:, None]
    first_sum = jnp.sum(mask * unit_grad, 0) / count
    second_sum = jnp.sum(mask * unit_grad * unit_batch, 0) / count
    deep_grad = scale * (unit_grad - mask * (first_sum + unit_batch * second_sum))
    reach = (depth.shape[0] - 1) // 2
    padded_grad = jnp.pad(deep_grad, ((reach, reach), (0, 0)))
    mixed_grad = jnp.zeros_like(deep_grad)
    depth_rows = []
    for offset in range(depth.shape[0]):
        begin = 2 * reach - offset
        mixed_grad = mixed_grad + depth[offset] * padded_grad[begin : begin + tokens]
        depth_rows.append(jnp.sum(deep_grad * padded[offset : offset + tokens], 0))
    mixed_grad = mixed_grad * mask
    project_grad = to_low(
        jnp.concatenate([mixed_grad * gating, mixed_grad * linear * gating * (1.0 - gating)], 1)
    )
    in_grad = dot_left(low_normed, own_part(project_grad, 1))
    values_grad, gain_grad = norm_backward(
        dot_right(project_grad, weight_in), unit, inverse, gains[2]
    )
    return (
        grad + values_grad,
        gain_grad,
        gamma_grad,
        beta_grad,
        in_grad,
        jnp.stack(depth_rows),
        out_grad,
    )


def senone_step(values, gain, tables, targets, valid):
    splits, place = lax.axis_size("hid"), lax.axis_index("hid")
    normed, unit, inverse = norm_forward(values, gain)
    low_normed = to_low(normed)
    own_rows, own_unit, own_inverse = (own_part(part, 0) for part in (low_normed, unit, inverse))
    own_targets, own_valid = own_part(targets, 0), own_part(valid, 0)
    logits = [dot_low(own_rows, table) for table in tables]
    width = logits[0].shape[1]
    picked = [
        own_targets[:, None]
        == jnp.arange(width, dtype=jnp.int32)[None, :] + (place - step) % splits * width
        for step in range(splits)
    ]
    top = jnp.max(jnp.stack([jnp.max(part, 1) for part in logits]), 0)
    total = sum(jnp.sum(jnp.exp(part - top[:, None]), 1) for part in logits)
    target = sum(
        jnp.sum(jnp.where(chosen, part, 0.0), 1) for chosen, part in zip(picked, logits)
    )
    log_total = top + jnp.log(total)
    loss = jnp.sum(own_valid * log_total) - jnp.sum(own_valid * target)
    logit_grad = [
        to_low(
            own_valid[:, None]
            * (jnp.exp(part - log_total[:, None]) - chosen.astype(jnp.float32))
        )
        for chosen, part in zip(picked, logits)
    ]
    normed_grad = sum(dot_right(part, table) for part, table in zip(logit_grad, tables))
    own_grad, own_gain_grad = norm_backward(normed_grad, own_unit, own_inverse, gain)
    values_grad = in_order(gather_near(to_low(own_grad)), 0).astype(jnp.float32)
    gain_grad = sum(gather_near(own_gain_grad))
    moved = [logit_grad[0]] + [shift(logit_grad[splits - step], step) for step in range(1, splits)]
    table_grad = dot_left(low_normed, in_order(moved, 0))
    return (loss, values_grad, gain_grad, table_grad)


def on_device(
    features,
    lengths,
    routes,
    alignments,
    input_weight,
    attention_in,
    branch_out,
    pointwise_in,
    depthwise,
    router,
    senone_table,
    norm_scales,
    expert_weights,
    input_first,
    input_second,
    attention_first,
    attention_second,
    branch_first,
    branch_second,
    pointwise_first,
    pointwise_second,
    depthwise_first,
    depthwise_second,
    router_first,
    router_second,
    senone_first,
    senone_second,
    scales_first,
    scales_second,
    expert_momentum,
):
    owners, splits = lax.axis_size("dp"), lax.axis_size("hid")
    place = lax.axis_index("hid")
    tokens = features.shape[0]
    bands, taps, gains = input_weight.shape[0], depthwise.shape[0], norm_scales.shape[0]
    own_width = input_weight.shape[1]

    small = jnp.concatenate(
        [
            jnp.pad(input_weight.T, ((0, 0), (0, 128 - bands))),
            router[0],
            router[1],
            depthwise.T,
            norm_scales.T,
            jnp.zeros((own_width, 128 - 2 * owners - taps - gains), jnp.float32),
        ],
        1,
    )
    small = exchange_rows(jnp.broadcast_to(small[None], (owners,) + small.shape))
    small = small.reshape(owners * own_width, -1)
    input_full = to_low(small[:, :bands])
    router_full = [small[:, 128 : 128 + owners], small[:, 128 + owners : 128 + 2 * owners]]
    begin = 128 + 2 * owners
    depth_full = small[:, begin : begin + taps].T
    scales_full = small[:, begin + taps : begin + taps + gains].T

    dense = to_low(jnp.concatenate([attention_in, branch_out[0], branch_out[1], pointwise_in], 1))
    dense = lax.all_gather(dense, "dp", axis=0, tiled=True)
    senone_own = lax.all_gather(to_low(senone_table), "dp", axis=0, tiled=True)
    attention_full, dense = dense[:, : 3 * D], dense[:, 3 * D :]
    branch_full, pointwise_full = (dense[:, :D], dense[:, D : 2 * D]), dense[:, 2 * D :]
    senone_full = gather_far(senone_own)
    expert_low = to_low(expert_weights[:, :, 0])
    expert_full = [[gather_far(expert_low[k, part]) for part in range(2)] for k in range(2)]
    momentum_pieces = expert_momentum.reshape((2 * 2,) + expert_momentum.shape[3:])

    def to_owners(pieces):
        return jnp.stack(
            [
                pieces[place] if step == 0 else shift(pieces[(place + step) % splits], step)
                for step in range(splits)
            ]
        )

    owned_momentum = to_owners(momentum_pieces)

    valid = (jnp.arange(tokens, dtype=jnp.int32) < lengths[0]).astype(jnp.float32)
    start = dot_right(features, input_full)
    mixed_one, kept_one = mixture_forward(
        start, scales_full[0], router_full[0], *expert_full[0], routes[0, :, 0]
    )
    first = start + mixed_one
    attended, kept_attend = attention_forward(
        first, scales_full[1], attention_full, branch_full[0], valid
    )
    second = first + attended
    convolved, kept_convolve = convolution_forward(
        second, scales_full, pointwise_full, depth_full, branch_full[1], valid
    )
    third = second + convolved
    mixed_two, kept_two = mixture_forward(
        third, scales_full[3], router_full[1], *expert_full[1], routes[1, :, 0]
    )
    fourth = third + mixed_two
    loss_local, grad, gain_five, senone_grad = senone_step(
        fourth, scales_full[4], senone_full, alignments, valid
    )
    senone_share = summed_shares(senone_grad)
    grad, gain_four, router_two, in_two, out_two = mixture_backward(
        grad, scales_full[3], router_full[1], *expert_full[1], kept_two
    )
    grad, gain_three, gamma_grad, beta_grad, pointwise_grad, depth_grad, conv_out_grad = (
        convolution_backward(
            grad, scales_full, pointwise_full, depth_full, branch_full[1], valid, kept_convolve
        )
    )
    grad, gain_two, attention_grad, attend_out_grad = attention_backward(
        grad, scales_full[1], attention_full, branch_full[0], valid, kept_attend
    )
    dense_share = summed_shares(
        jnp.concatenate([attention_grad, attend_out_grad, conv_out_grad, pointwise_grad], 1)
    )
    grad, gain_one, router_one, in_one, out_one = mixture_backward(
        grad, scales_full[0], router_full[0], *expert_full[0], kept_one
    )
    scales_grad = jnp.stack(
        [gain_one, gain_two, gain_three, gain_four, gain_five, gamma_grad, beta_grad]
    )
    expert_grad = jnp.stack([in_one, out_one, in_two, out_two])
    input_grad = dot_left(to_low(grad), features)
    small_share = summed_shares(
        jnp.concatenate(
            [
                jnp.pad(input_grad, ((0, 0), (0, 128 - bands))),
                router_one,
                router_two,
                depth_grad.T,
                scales_grad.T,
                jnp.zeros((D, 128 - 2 * owners - taps - gains), jnp.float32),
            ],
            1,
        )
    )
    leading = (place == 0).astype(jnp.float32)
    square = (
        leading * jnp.sum(small_share * small_share)
        + jnp.sum(dense_share * dense_share)
        + jnp.sum(senone_share * senone_share)
        + jnp.sum(expert_grad * expert_grad)
    )
    scalars = jnp.stack([square, leading * lengths[0].astype(jnp.float32), loss_local])
    scalars = jnp.broadcast_to(
        jnp.pad(scalars, (0, 125))[None, None], (owners * splits, 1, 128)
    )
    scalars = jnp.sum(
        lax.all_to_all(scalars, ("dp", "hid"), split_axis=0, concat_axis=0, tiled=True), (0, 1)
    )
    square, count, loss_sum = scalars[0], scalars[1], scalars[2]
    norm = jnp.sqrt(square) / count
    factor = jnp.minimum(1.0, clip_limit / (norm + 1e-06))

    owned_grad = to_owners(to_low(expert_grad))
    kind_scale = jnp.where(place % 2 == 0, D ** (-0.5), 3 * owners * FF ** (-0.5)) * (
        muon_rate * FF**0.5
    )
    expert_scale = factor / count
    orth = orthogonal(
        jnp.stack([expert_scale, kind_scale]), owned_momentum, owned_grad
    )
    momentum_new = muon_beta * expert_momentum + expert_scale * expert_grad.reshape(
        expert_momentum.shape
    )
    returned = [orth[0]] + [shift(orth[step], -step) for step in range(1, splits)]
    turned = [returned[0]] + returned[:0:-1]
    update = in_order(turned, 0).reshape(expert_weights.shape).astype(jnp.float32)
    experts_new = (1.0 - muon_decay) * expert_weights - update

    dense_share = gather_near(dense_share)
    quarter = D // splits
    parts = [
        in_order([block[:, begin : begin + width] for block in dense_share], 1)
        for begin, width in (
            (0, 3 * quarter),
            (3 * quarter, quarter),
            (4 * quarter, quarter),
            (5 * quarter, 2 * quarter),
        )
    ]
    begin = 128 + 2 * owners
    shares = (
        small_share[:, :bands].T,
        parts[0],
        jnp.stack(parts[1:3]),
        parts[3],
        senone_share,
        small_share[:, begin : begin + taps].T,
        jnp.stack([small_share[:, 128 : 128 + owners], small_share[:, 128 + owners : begin]]),
        small_share[:, begin + taps : begin + taps + gains].T,
    )
    input_first_new, input_second_new, input_new = adam_update(
        input_weight, shares[0] / count * factor, input_first, input_second, adam_rate, weight_decay
    )
    attention_first_new, attention_second_new, attention_new = adam_update(
        attention_in,
        shares[1] / count * factor,
        attention_first,
        attention_second,
        adam_rate,
        weight_decay,
    )
    branch_first_new, branch_second_new, branch_new = adam_update(
        branch_out, shares[2] / count * factor, branch_first, branch_second, adam_rate, weight_decay
    )
    pointwise_first_new, pointwise_second_new, pointwise_new = adam_update(
        pointwise_in,
        shares[3] / count * factor,
        pointwise_first,
        pointwise_second,
        adam_rate,
        weight_decay,
    )
    senone_first_new, senone_second_new, senone_new = adam_update(
        senone_table,
        shares[4] / count * factor,
        senone_first,
        senone_second,
        adam_rate,
        weight_decay,
    )
    depthwise_first_new, depthwise_second_new, depthwise_new = adam_update(
        depthwise,
        shares[5] / count * factor,
        depthwise_first,
        depthwise_second,
        adam_rate,
        weight_decay,
    )
    router_first_new, router_second_new, router_new = adam_update(
        router, shares[6] / count * factor, router_first, router_second, adam_rate, weight_decay
    )
    scales_first_new, scales_second_new, scales_new = adam_update(
        norm_scales, shares[7] / count * factor, scales_first, scales_second, gain_rate, 0.0
    )
    return (
        loss_sum,
        count,
        norm,
        input_first_new,
        input_second_new,
        input_new,
        attention_first_new,
        attention_second_new,
        attention_new,
        branch_first_new,
        branch_second_new,
        branch_new,
        pointwise_first_new,
        pointwise_second_new,
        pointwise_new,
        depthwise_first_new,
        depthwise_second_new,
        depthwise_new,
        router_first_new,
        router_second_new,
        router_new,
        senone_first_new,
        senone_second_new,
        senone_new,
        scales_first_new,
        scales_second_new,
        scales_new,
        momentum_new,
        experts_new,
    )


def solution(mesh):
    return jax.shard_map(
        on_device,
        mesh=mesh,
        in_specs=(
            P("dp", None),
            P("dp"),
            P(None, "dp", None),
            P("dp"),
            P(None, "dp"),
            P("dp", None),
            P(None, "dp", None),
            P("dp", None),
            P(None, "dp"),
            P(None, "dp", None),
            P("dp", "hid"),
            P(None, "dp"),
            P(None, None, "dp", None, "hid"),
            P(None, "dp"),
            P(None, "dp"),
            P("dp", None),
            P("dp", None),
            P(None, "dp", None),
            P(None, "dp", None),
            P("dp", None),
            P("dp", None),
            P(None, "dp"),
            P(None, "dp"),
            P(None, "dp", None),
            P(None, "dp", None),
            P("dp", "hid"),
            P("dp", "hid"),
            P(None, "dp"),
            P(None, "dp"),
            P(None, None, "dp", None, "hid"),
        ),
        out_specs=(
            P(),
            P(),
            P(),
            P(None, "dp"),
            P(None, "dp"),
            P(None, "dp"),
            P("dp", None),
            P("dp", None),
            P("dp", None),
            P(None, "dp", None),
            P(None, "dp", None),
            P(None, "dp", None),
            P("dp", None),
            P("dp", None),
            P("dp", None),
            P(None, "dp"),
            P(None, "dp"),
            P(None, "dp"),
            P(None, "dp", None),
            P(None, "dp", None),
            P(None, "dp", None),
            P("dp", "hid"),
            P("dp", "hid"),
            P("dp", "hid"),
            P(None, "dp"),
            P(None, "dp"),
            P(None, "dp"),
            P(None, None, "dp", None, "hid"),
            P(None, None, "dp", None, "hid"),
        ),
        check_vma=False,
    )
```

time: 1530 us -> 687 us (0.45)
  waiting for transfers between devices: 731 us -> 141 us
  blocking collectives: 354 us -> 0 us
  starting transfers between devices: 61.4 us -> 178 us
  matrix products: 187 us -> 121 us
  local copies, waits for them, and re-layouts: 68.5 us -> 107 us
  Pallas kernels: 0 us -> 23.1 us
    reduce_scatter x4 -> x0, waiting for transfers between devices: 323 us -> none  [the longest x1 82.5 us: on_device(): lax.psum_scatter(attention_grad, 'dp', scatter_dimension=0, tiled=True)]
    unnamed x17 -> x2, waiting for transfers between devices: 233 us -> 0.03 us
    psum x5 -> x0, blocking collectives: 197 us -> none  [the longest x4 131 us: return_from_experts(): total = lax.psum(shaped, 'hid')]
    all_gather x6 -> x0, blocking collectives: 134 us -> none  [the longest x1 37.1 us: on_device(): lax.all_gather(depthwise, 'dp', axis=1, tiled=True)]
    ppermute x0 -> x77, waiting for transfers between devices: none -> 106 us  [shift(): lax.ppermute(values, 'hid', [(i, (i + step) % size) for i in range(size)])]
    all_to_all x9 -> x13, waiting for transfers between devices: 129 us -> 34.7 us  [the longest x12 32.2 us: exchange_rows(): return lax.all_to_all(values, 'dp', split_axis=0, concat_axis=0, tiled=True)]
    ppermute x0 -> x77, starting transfers between devices: none -> 88.9 us  [shift(): lax.ppermute(values, 'hid', [(i, (i + step) % size) for i in range(size)])]
    dot_general x21 -> x6, matrix products: 98 us -> 10.5 us  [exact_dot(): return jnp.dot(left, right, precision=lax.Precision.HIGHEST)]
  transfers between devices with their start and end apart: 22 -> 92, of which waited for: 15 -> 27; matrix products, arithmetic and copies ran while one was open for 8% -> 33% of each run, Pallas kernels for 0% -> 0%
where the time goes in v1:
time: 687 us; the launch traced here: 674 us
  starting transfers between devices  178 us (26%)
  waiting for transfers between devices  141 us (21%)
  matrix products  121 us (18%)
  local copies, waits for them, and re-layouts  107 us (16%)
  other arithmetic  77.5 us (11%)
  between operations  26.3 us (4%)
  Pallas kernels  23.1 us (3%)
    ppermute x77, waiting for transfers between devices, shift(): lax.ppermute(values, 'hid', [(i, (i + step) % size) for i in range(size)])  106 us
    ppermute x77, starting transfers between devices, shift(): lax.ppermute(values, 'hid', [(i, (i + step) % size) for i in range(size)])  88.9 us
    all_to_all x12, starting transfers between devices, exchange_rows(): return lax.all_to_all(values, 'dp', split_axis=0, concat_axis=0, tiled=True)  84.6 us
    dot_general x28, matrix products, dot_low(): return jnp.dot(left, right, preferred_element_type=jnp.float32)  43.1 us
    unnamed x593, local copies, waits for them, and re-layouts  41 us
    all_to_all x12, waiting for transfers between devices, exchange_rows(): return lax.all_to_all(values, 'dp', split_axis=0, concat_axis=0, tiled=True)  32.2 us
    dot_general x14, matrix products, dot_left(): lax.dot_general(left, right, (((0,), (0,)), ((), ())), preferred_element_...  28.8 us
    dot_general x25, matrix products, dot_right(): lax.dot_general(left, right, (((1,), (1,)), ((), ())), preferred_element_...  27.2 us
  transfers between devices with their start and end apart: 92, of which 27 were waited for; matrix products, arithmetic and copies ran while one was open for 33% of the time, Pallas kernels for 0%

profile of v1, /device:TPU:1, one launch (start us, length us, event | category | flops | bytes accessed | tf_op | source)
XLA Modules:
  0.0 674.3 jit_solution(13904912190848591474)
XLA Ops:
  8.7 2.5 convert_bitcast_fusion
  12.7 3.6 collective-permute-start.3
  16.3 2.7 collective-permute-start.6
  20.1 9.4 %all-to-all-start = ((f32[32,16,256]{2,1,0:T(8,128)}), f32[32,16,256]{2,1,0:T(8,128)S(1)}, u32[]{:S(2)}, u32[]{:S(2)}) async-start(f32[32,16,256]{2,1,0:T(8,128)} %broadcast_in_dim.31), calls=%async_computation | async-start | bytes 1048576 | tf_op jit(solution)/shard_map/all_to_all | solution.py:61
  29.6 3.0 collective-permute-start.14
  45.3 4.3 constant_dynamic-slice_fusion.2
  57.5 7.7 %all-to-all-start.1 = ((bf16[32,6,512]{2,1,0:T(8,128)(2,1)}), bf16[32,6,512]{2,1,0:T(8,128)(2,1)S(1)}, u32[]{:S(2)}, u32[]{:S(2)}) async-start(bf16[32,6,512]{2,1,0:T(8,128)(2,1)} %all_to_all.80), calls=%async_computation.1 | async-start | bytes 524288 | tf_op jit(solution)/shard_map/all_to_all | solution.py:61
  68.2 2.7 collective-permute-start.17
  72.8 2.6 slice_reduce_fusion.19
  82.9 2.4 collective-permute-start.4
  87.7 6.6 collective-permute-done.12
  121.6 46.0 %collective-permute-done.16 = bf16[256,512]{1,0:T(8,128)(2,1)} collective-permute-done((bf16[256,512]{1,0:T(8,128)(2,1)S(1)}, bf16[256,512]{1,0:T(8,128)(2,1)}, u32[]{:S(2)}, u32[]{:S(2)}) %collective-permute-start.16) | collective-permute-done | bytes 262176 | tf_op jit(solution)/shard_map/ppermute | solution.py:32
  171.3 7.9 %all-to-all-start.2 = ((bf16[32,6,512]{2,1,0:T(8,128)(2,1)}), bf16[32,6,512]{2,1,0:T(8,128)(2,1)S(1)}, u32[]{:S(2)}, u32[]{:S(2)}) async-start(bf16[32,6,512]{2,1,0:T(8,128)(2,1)} %all_to_all.83), calls=%async_computation.2 | async-start | bytes 524288 | tf_op jit(solution)/shard_map/all_to_all | solution.py:61
  191.4 4.5 pad_maximum_fusion.1.momentum_ref
  198.1 5.0 collective-permute-done.8
  206.4 2.9 collective-permute-start.25
  209.5 11.1 %collective-permute-done.23 = bf16[256,1024]{1,0:T(8,128)(2,1)S(1)} collective-permute-done((bf16[256,1024]{1,0:T(8,128)(2,1)S(1)}, bf16[256,1024]{1,0:T(8,128)(2,1)S(1)}, u32[]{:S(2)}, u32[]{:S(2)}) %collective-permute-start.23) | collective-permute-done | bytes 524320 | tf_op jit(solution)/shard_map/ppermute | solution.py:32
  222.2 3.7 convolution_convert_fusion
  225.9 2.6 copy.271
  228.5 3.0 fusion.328
  234.9 2.8 fusion.9
  241.4 2.4 multiply_reduce_fusion.2
  250.2 7.0 %all-to-all-start.3 = ((bf16[32,6,512]{2,1,0:T(8,128)(2,1)}), bf16[32,6,512]{2,1,0:T(8,128)(2,1)}, u32[]{:S(2)}, u32[]{:S(2)}) async-start(bf16[32,6,512]{2,1,0:T(8,128)(2,1)} %all_to_all.86), calls=%async_computation.3 | async-start | bytes 524288 | tf_op jit(solution)/shard_map/all_to_all | solution.py:61
  259.8 6.2 all-to-all-done.3
  280.7 4.4 all-to-all-start.4
  286.5 7.7 %all-to-all-done.4 = bf16[32,6,512]{2,1,0:T(8,128)(2,1)} async-done(((bf16[32,6,512]{2,1,0:T(8,128)(2,1)}), bf16[32,6,512]{2,1,0:T(8,128)(2,1)}, u32[]{:S(2)}, u32[]{:S(2)}) %all-to-all-start.4) | async-done | bytes 196640 | tf_op jit(solution)/shard_map/all_to_all | solution.py:61
  302.5 2.4 collective-permute-done.20
  304.9 4.7 collective-permute-done.19
  332.4 2.4 collective-permute-start.38
  345.4 7.8 %all-to-all-start.5 = ((bf16[32,6,512]{2,1,0:T(8,128)(2,1)}), bf16[32,6,512]{2,1,0:T(8,128)(2,1)S(1)}, u32[]{:S(2)}, u32[]{:S(2)}) async-start(bf16[32,6,512]{2,1,0:T(8,128)(2,1)} %all_to_all.92), calls=%async_computation.5 | async-start | bytes 524288 | tf_op jit(solution)/shard_map/all_to_all | solution.py:61
  356.5 2.9 collective-permute-start.55
  386.2 8.5 %all-to-all-start.6 = ((bf16[32,6,512]{2,1,0:T(8,128)(2,1)}), bf16[32,6,512]{2,1,0:T(8,128)(2,1)S(1)}, u32[]{:S(2)}, u32[]{:S(2)}) async-start(bf16[32,6,512]{2,1,0:T(8,128)(2,1)} %all_to_all.95), calls=%async_computation.6 | async-start | bytes 524288 | tf_op jit(solution)/shard_map/all_to_all | solution.py:61
  395.4 2.7 collective-permute-start.58
  399.2 3.1 convolution_convert_fusion.1
  408.8 3.0 convolution_bitcast_fusion
  411.9 2.7 collective-permute-start.52
  416.7 3.0 convolution_bitcast_fusion.1
  419.7 2.7 collective-permute-start.43
  429.8 3.3 multiply_reduce_fusion.8
  433.2 2.4 multiply_convert_fusion.3
  442.9 2.8 multiply_convert_fusion
  458.2 7.8 %all-to-all-start.7 = ((bf16[32,6,512]{2,1,0:T(8,128)(2,1)}), bf16[32,6,512]{2,1,0:T(8,128)(2,1)}, u32[]{:S(2)}, u32[]{:S(2)}) async-start(bf16[32,6,512]{2,1,0:T(8,128)(2,1)} %all_to_all.98), calls=%async_computation.7 | async-start | bytes 524288 | tf_op jit(solution)/shard_map/all_to_all | solution.py:61
  466.5 2.8 convolution_convert_fusion.3
  471.1 3.9 all-to-all-done.7
  487.6 3.8 all-to-all-start.8
  491.4 2.4 collective-permute-start.51
  496.6 2.7 collective-permute-start.46
  503.9 2.6 collective-permute-start.44
  509.6 8.3 %all-to-all-start.11 = ((bf16[32,16,1024]{2,1,0:T(8,128)(2,1)}), bf16[32,16,1024]{2,1,0:T(8,128)(2,1)}, u32[]{:S(2)}, u32[]{:S(2)}) async-start(bf16[32,16,1024]{2,1,0:T(8,128)(2,1)} %bitcast.340), calls=%async_computation.11 | async-start | bytes 2097152 | tf_op jit(solution)/shard_map/all_to_all | solution.py:61
  521.0 2.8 convolution_bitcast_fusion.2
  523.8 3.1 convolution_bitcast_fusion.3
  526.9 5.1 collective-permute-done.32
  538.9 7.4 %all-to-all-start.9 = ((bf16[32,16,256]{2,1,0:T(8,128)(2,1)}), bf16[32,16,256]{2,1,0:T(8,128)(2,1)S(1)}, u32[]{:S(2)}, u32[]{:S(2)}) async-start(bf16[32,16,256]{2,1,0:T(8,128)(2,1)} %concatenate.127), calls=%async_computation.9 | async-start | bytes 524288 | tf_op jit(solution)/shard_map/all_to_all | solution.py:61
  551.2 4.1 all-to-all-done.9
  555.2 4.5 all-to-all-start.10
  559.7 2.9 multiply_reduce_fusion.1
  568.6 7.0 %all-to-all-done.10 = bf16[32,16,896]{2,1,0:T(8,128)(2,1)} async-done(((bf16[32,16,896]{2,1,0:T(8,128)(2,1)}), bf16[32,16,896]{2,1,0:T(8,128)(2,1)}, u32[]{:S(2)}, u32[]{:S(2)}) %all-to-all-start.10) | async-done | bytes 917536 | tf_op jit(solution)/shard_map/all_to_all | solution.py:61
  583.3 5.0 all-to-all-start.12
  589.9 3.1 pad_maximum_fusion.2.grad_ref
  595.3 2.5 all-to-all-done.12
  603.1 3.0 multiply_add_fusion
  606.2 23.1 %shard_map.509 = bf16[4,512,512]{2,1,0:T(8,128)(2,1)S(1)} custom-call(f32[2]{0:T(128)S(1)} %pad_maximum_fusion.8.factor_ref, f32[4,512,512]{2,1,0:T(8,128)} %pad_maximum_fusion.1.momentum_ref, bf16[4,512,512]{2,1,0:T(8,128)(2,1)S(1)} %copy-done.1), custom_call_target="tpu_custom_call" | custom-call | flops 30000001024 | bytes 10000000 | tf_op jit(solution)/shard_map/pallas_call | solution.py:156
  646.4 12.4 %collective-permute-done.76 = bf16[512,512]{1,0:T(8,128)(2,1)} collective-permute-done((bf16[512,512]{1,0:T(8,128)(2,1)}, bf16[512,512]{1,0:T(8,128)(2,1)}, u32[]{:S(2)}, u32[]{:S(2)}) %collective-permute-start.76) | collective-permute-done | bytes 524320 | tf_op jit(solution)/shard_map/ppermute | solution.py:32
  663.3 2.7 convert_subtract_fusion
  (1003 shorter events, 306.3 us)
Async XLA Ops:
  7.2 160.4 %all-gather.5.cloned.1.call-start = ((), (), s32[]{:S(2)}) async-start(), calls=%async_computation.14 | async-start | bytes 1081344 | tf_op jit(solution)/shard_map/all_gather | solution.py:484
  12.7 55.5 %collective-permute-start.3 = (bf16[512,512]{1,0:T(8,128)(2,1)}, bf16[512,512]{1,0:T(8,128)(2,1)}, u32[]{:S(2)}, u32[]{:S(2)}) collective-permute-start(bf16[512,512]{1,0:T(8,128)(2,1)} %get-tuple-element.360), channel_id=1, source_target_pairs={{0,3},{1,0},{2,1},{3,2},{4,7},{5,4},{6,5},{7,6},{8,11},{9,8},{10,9... | collective-permute-start | bytes 1572872 | tf_op jit(solution)/shard_map/ppermute | solution.py:32
  16.3 52.0 %collective-permute-start = (bf16[512,512]{1,0:T(8,128)(2,1)}, bf16[512,512]{1,0:T(8,128)(2,1)}, u32[]{:S(2)}, u32[]{:S(2)}) collective-permute-start(bf16[512,512]{1,0:T(8,128)(2,1)} %get-tuple-element.360), channel_id=1, source_target_pairs={{0,1},{1,2},{2,3},{3,0},{4,5},{5,6},{6,7},{7,4},{8,9},{9,10},{10,1... | collective-permute-start | bytes 1572872 | tf_op jit(solution)/shard_map/ppermute | solution.py:32
  16.3 64.2 %collective-permute-start.6 = (bf16[512,512]{1,0:T(8,128)(2,1)}, bf16[512,512]{1,0:T(8,128)(2,1)}, u32[]{:S(2)}, u32[]{:S(2)}) collective-permute-start(bf16[512,512]{1,0:T(8,128)(2,1)} %get-tuple-element.359), channel_id=1, source_target_pairs={{0,3},{1,0},{2,1},{3,2},{4,7},{5,4},{6,5},{7,6},{8,11},{9,8},{10,9... | collective-permute-start | bytes 1572872 | tf_op jit(solution)/shard_map/ppermute | solution.py:32
  18.9 52.0 %collective-permute-start.1 = (bf16[512,512]{1,0:T(8,128)(2,1)}, bf16[512,512]{1,0:T(8,128)(2,1)}, u32[]{:S(2)}, u32[]{:S(2)}) collective-permute-start(bf16[512,512]{1,0:T(8,128)(2,1)} %get-tuple-element.359), channel_id=1, source_target_pairs={{0,1},{1,2},{2,3},{3,0},{4,5},{5,6},{6,7},{7,4},{8,9},{9,10},{10,1... | collective-permute-start | bytes 1572872 | tf_op jit(solution)/shard_map/ppermute | solution.py:32
  20.1 31.0 %all-to-all-start = ((f32[32,16,256]{2,1,0:T(8,128)}), f32[32,16,256]{2,1,0:T(8,128)S(1)}, u32[]{:S(2)}, u32[]{:S(2)}) async-start(f32[32,16,256]{2,1,0:T(8,128)} %broadcast_in_dim.31), calls=%async_computation | async-start | bytes 1048576 | tf_op jit(solution)/shard_map/all_to_all | solution.py:61
  29.6 192.6 %all-gather.3.cloned.1.call-start = ((), (), s32[]{:S(2)}) async-start(), calls=%async_computation.13 | async-start | bytes 3784704 | tf_op jit(solution)/shard_map/all_gather | solution.py:483
  29.6 56.4 %collective-permute-start.14 = (bf16[512,512]{1,0:T(8,128)(2,1)}, bf16[512,512]{1,0:T(8,128)(2,1)}, u32[]{:S(2)}, u32[]{:S(2)}) collective-permute-start(bf16[512,512]{1,0:T(8,128)(2,1)} %get-tuple-element.358), channel_id=1, source_target_pairs={{0,3},{1,0},{2,1},{3,2},{4,7},{5,4},{6,5},{7,6},{8,11},{9,8},{10,9... | collective-permute-start | bytes 1572872 | tf_op jit(solution)/shard_map/ppermute | solution.py:32
  57.5 39.9 %all-to-all-start.1 = ((bf16[32,6,512]{2,1,0:T(8,128)(2,1)}), bf16[32,6,512]{2,1,0:T(8,128)(2,1)S(1)}, u32[]{:S(2)}, u32[]{:S(2)}) async-start(bf16[32,6,512]{2,1,0:T(8,128)(2,1)} %all_to_all.80), calls=%async_computation.1 | async-start | bytes 524288 | tf_op jit(solution)/shard_map/all_to_all | solution.py:61
  68.1 14.8 %collective-permute-start.11 = (bf16[512,512]{1,0:T(8,128)(2,1)}, bf16[512,512]{1,0:T(8,128)(2,1)S(1)}, u32[]{:S(2)}, u32[]{:S(2)}) collective-permute-start(bf16[512,512]{1,0:T(8,128)(2,1)} %get-tuple-element.358), channel_id=1, source_target_pairs={{0,1},{1,2},{2,3},{3,0},{4,5},{5,6},{6,7},{7,4},{8,9},{9,10},{10,1... | collective-permute-start | bytes 1572872 | tf_op jit(solution)/shard_map/ppermute | solution.py:32
  68.2 27.5 %collective-permute-start.17 = (bf16[512,512]{1,0:T(8,128)(2,1)}, bf16[512,512]{1,0:T(8,128)(2,1)S(1)}, u32[]{:S(2)}, u32[]{:S(2)}) collective-permute-start(bf16[512,512]{1,0:T(8,128)(2,1)} %get-tuple-element.357), channel_id=1, source_target_pairs={{0,3},{1,0},{2,1},{3,2},{4,7},{5,4},{6,5},{7,6},{8,11},{9,8},{10,9... | collective-permute-start | bytes 1572872 | tf_op jit(solution)/shard_map/ppermute | solution.py:32
  70.9 23.4 %collective-permute-start.12 = (bf16[512,512]{1,0:T(8,128)(2,1)}, bf16[512,512]{1,0:T(8,128)(2,1)S(1)}, u32[]{:S(2)}, u32[]{:S(2)}) collective-permute-start(bf16[512,512]{1,0:T(8,128)(2,1)} %get-tuple-element.357), channel_id=1, source_target_pairs={{0,1},{1,2},{2,3},{3,0},{4,5},{5,6},{6,7},{7,4},{8,9},{9,10},{10,1... | collective-permute-start | bytes 1572872 | tf_op jit(solution)/shard_map/ppermute | solution.py:32
  80.5 27.4 %collective-permute-start.2 = (bf16[256,512]{1,0:T(8,128)(2,1)}, bf16[256,512]{1,0:T(8,128)(2,1)}, u32[]{:S(2)}, u32[]{:S(2)}) collective-permute-start(bf16[256,512]{1,0:T(8,128)(2,1)} %slice.526), channel_id=1, source_target_pairs={{0,1},{1,2},{2,3},{3,0},{4,5},{5,6},{6,7},{7,4},{8,9},{9,10},{10,1... | collective-permute-start | bytes 786440 | tf_op jit(solution)/shard_map/ppermute | solution.py:32
  82.9 29.7 %collective-permute-start.4 = (bf16[256,512]{1,0:T(8,128)(2,1)}, bf16[256,512]{1,0:T(8,128)(2,1)}, u32[]{:S(2)}, u32[]{:S(2)}) collective-permute-start(bf16[256,512]{1,0:T(8,128)(2,1)} %slice.527), channel_id=1, source_target_pairs={{0,3},{1,0},{2,1},{3,2},{4,7},{5,4},{6,5},{7,6},{8,11},{9,8},{10,9... | collective-permute-start | bytes 786440 | tf_op jit(solution)/shard_map/ppermute | solution.py:32
  86.1 24.8 %collective-permute-start.5 = (bf16[256,512]{1,0:T(8,128)(2,1)}, bf16[256,512]{1,0:T(8,128)(2,1)}, u32[]{:S(2)}, u32[]{:S(2)}) collective-permute-start(bf16[256,512]{1,0:T(8,128)(2,1)} %slice.528), channel_id=1, source_target_pairs={{0,1},{1,2},{2,3},{3,0},{4,5},{5,6},{6,7},{7,4},{8,9},{9,10},{10,1... | collective-permute-start | bytes 786440 | tf_op jit(solution)/shard_map/ppermute | solution.py:32
  94.3 20.7 %collective-permute-start.7 = (bf16[256,512]{1,0:T(8,128)(2,1)}, bf16[256,512]{1,0:T(8,128)(2,1)}, u32[]{:S(2)}, u32[]{:S(2)}) collective-permute-start(bf16[256,512]{1,0:T(8,128)(2,1)} %slice.529), channel_id=1, source_target_pairs={{0,3},{1,0},{2,1},{3,2},{4,7},{5,4},{6,5},{7,6},{8,11},{9,8},{10,9... | collective-permute-start | bytes 786440 | tf_op jit(solution)/shard_map/ppermute | solution.py:32
  95.8 19.3 %collective-permute-start.13 = (bf16[256,512]{1,0:T(8,128)(2,1)}, bf16[256,512]{1,0:T(8,128)(2,1)}, u32[]{:S(2)}, u32[]{:S(2)}) collective-permute-start(bf16[256,512]{1,0:T(8,128)(2,1)} %slice.567), channel_id=1, source_target_pairs={{0,1},{1,2},{2,3},{3,0},{4,5},{5,6},{6,7},{7,4},{8,9},{9,10},{10,1... | collective-permute-start | bytes 786440 | tf_op jit(solution)/shard_map/ppermute | solution.py:32
  110.9 78.0 %collective-permute-start.70 = (f32[512,512]{1,0:T(8,128)}, f32[512,512]{1,0:T(8,128)}, u32[]{:S(2)}, u32[]{:S(2)}) collective-permute-start(f32[512,512]{1,0:T(8,128)} %get-tuple-element.347), channel_id=1, source_target_pairs={{0,3},{1,0},{2,1},{3,2},{4,7},{5,4},{6,5},{7,6},{8,11},{9,8},{10,9... | collective-permute-start | bytes 3145736 | tf_op jit(solution)/shard_map/ppermute | solution.py:32
  112.6 77.8 %collective-permute-start.69 = (f32[512,512]{1,0:T(8,128)}, f32[512,512]{1,0:T(8,128)}, u32[]{:S(2)}, u32[]{:S(2)}) collective-permute-start(f32[512,512]{1,0:T(8,128)} %get-tuple-element.348), channel_id=1, source_target_pairs={{0,2},{1,3},{2,0},{3,1},{4,6},{5,7},{6,4},{7,5},{8,10},{9,11},{10,... | collective-permute-start | bytes 3145736 | tf_op jit(solution)/shard_map/ppermute | solution.py:32
  115.0 76.1 %collective-permute-start.68 = (f32[512,512]{1,0:T(8,128)}, f32[512,512]{1,0:T(8,128)}, u32[]{:S(2)}, u32[]{:S(2)}) collective-permute-start(f32[512,512]{1,0:T(8,128)} %get-tuple-element.349), channel_id=1, source_target_pairs={{0,1},{1,2},{2,3},{3,0},{4,5},{5,6},{6,7},{7,4},{8,9},{9,10},{10,1... | collective-permute-start | bytes 3145736 | tf_op jit(solution)/shard_map/ppermute | solution.py:32
  115.1 52.5 %collective-permute-start.16 = (bf16[256,512]{1,0:T(8,128)(2,1)S(1)}, bf16[256,512]{1,0:T(8,128)(2,1)}, u32[]{:S(2)}, u32[]{:S(2)}) collective-permute-start(bf16[256,512]{1,0:T(8,128)(2,1)S(1)} %copy-done.76), channel_id=1, source_target_pairs={{0,1},{1,2},{2,3},{3,0},{4,5},{5,6},{6,7},{7,4},{8,9},{9,10},{10,1... | collective-permute-start | bytes 786440 | tf_op jit(solution)/shard_map/ppermute | solution.py:32
  116.3 51.3 %collective-permute-start.18 = (bf16[256,512]{1,0:T(8,128)(2,1)S(1)}, bf16[256,512]{1,0:T(8,128)(2,1)S(1)}, u32[]{:S(2)}, u32[]{:S(2)}) collective-permute-start(bf16[256,512]{1,0:T(8,128)(2,1)S(1)} %copy-done.75), channel_id=1, source_target_pairs={{0,3},{1,0},{2,1},{3,2},{4,7},{5,4},{6,5},{7,6},{8,11},{9,8},{10,9... | collective-permute-start | bytes 786440 | tf_op jit(solution)/shard_map/ppermute | solution.py:32
  167.6 38.7 %collective-permute-start.24 = (bf16[512,1024]{1,0:T(8,128)(2,1)}, bf16[512,1024]{1,0:T(8,128)(2,1)S(1)}, u32[]{:S(2)}, u32[]{:S(2)}) collective-permute-start(bf16[512,1024]{1,0:T(8,128)(2,1)} %all-gather.5.cloned.1.call-done), channel_id=1, source_target_pairs={{0,3},{1,0},{2,1},{3,2},{4,7},{5,4},{6,5},{7,6},{8,11},{9,8},{10,9... | collective-permute-start | bytes 3145736 | tf_op jit(solution)/shard_map/ppermute | solution.py:32
  167.6 37.2 %collective-permute-start.22 = (bf16[512,1024]{1,0:T(8,128)(2,1)}, bf16[512,1024]{1,0:T(8,128)(2,1)}, u32[]{:S(2)}, u32[]{:S(2)}) collective-permute-start(bf16[512,1024]{1,0:T(8,128)(2,1)} %all-gather.5.cloned.1.call-done), channel_id=1, source_target_pairs={{0,1},{1,2},{2,3},{3,0},{4,5},{5,6},{6,7},{7,4},{8,9},{9,10},{10,1... | collective-permute-start | bytes 3145736 | tf_op jit(solution)/shard_map/ppermute | solution.py:32
  171.3 16.8 %all-to-all-start.2 = ((bf16[32,6,512]{2,1,0:T(8,128)(2,1)}), bf16[32,6,512]{2,1,0:T(8,128)(2,1)S(1)}, u32[]{:S(2)}, u32[]{:S(2)}) async-start(bf16[32,6,512]{2,1,0:T(8,128)(2,1)} %all_to_all.83), calls=%async_computation.2 | async-start | bytes 524288 | tf_op jit(solution)/shard_map/all_to_all | solution.py:61
  206.4 15.0 %collective-permute-start.25 = (bf16[256,1024]{1,0:T(8,128)(2,1)S(1)}, bf16[256,1024]{1,0:T(8,128)(2,1)S(1)}, u32[]{:S(2)}, u32[]{:S(2)}) collective-permute-start(bf16[256,1024]{1,0:T(8,128)(2,1)S(1)} %slice.573), channel_id=1, source_target_pairs={{0,3},{1,0},{2,1},{3,2},{4,7},{5,4},{6,5},{7,6},{8,11},{9,8},{10,9... | collective-permute-start | bytes 1572872 | tf_op jit(solution)/shard_map/ppermute | solution.py:32
  250.2 15.8 %all-to-all-start.3 = ((bf16[32,6,512]{2,1,0:T(8,128)(2,1)}), bf16[32,6,512]{2,1,0:T(8,128)(2,1)}, u32[]{:S(2)}, u32[]{:S(2)}) async-start(bf16[32,6,512]{2,1,0:T(8,128)(2,1)} %all_to_all.86), calls=%async_computation.3 | async-start | bytes 524288 | tf_op jit(solution)/shard_map/all_to_all | solution.py:61
  298.8 82.5 %collective-permute-start.64 = (bf16[192,512]{1,0:T(8,128)(2,1)}, bf16[192,512]{1,0:T(8,128)(2,1)}, u32[]{:S(2)}, u32[]{:S(2)}) collective-permute-start(bf16[192,512]{1,0:T(8,128)(2,1)} %copy-done.93), channel_id=1, source_target_pairs={{0,3},{1,0},{2,1},{3,2},{4,7},{5,4},{6,5},{7,6},{8,11},{9,8},{10,9... | collective-permute-start | bytes 589832 | tf_op jit(solution)/shard_map/ppermute | solution.py:32
  300.8 81.4 %collective-permute-start.63 = (bf16[192,512]{1,0:T(8,128)(2,1)}, bf16[192,512]{1,0:T(8,128)(2,1)}, u32[]{:S(2)}, u32[]{:S(2)}) collective-permute-start(bf16[192,512]{1,0:T(8,128)(2,1)} %copy-done.92), channel_id=1, source_target_pairs={{0,2},{1,3},{2,0},{3,1},{4,6},{5,7},{6,4},{7,5},{8,10},{9,11},{10,... | collective-permute-start | bytes 589832 | tf_op jit(solution)/shard_map/ppermute | solution.py:32
  332.4 22.4 %collective-permute-start.38 = (bf16[128,1024]{1,0:T(8,128)(2,1)}, bf16[128,1024]{1,0:T(8,128)(2,1)}, u32[]{:S(2)}, u32[]{:S(2)}) collective-permute-start(bf16[128,1024]{1,0:T(8,128)(2,1)} %copy-done.58), channel_id=1, source_target_pairs={{0,3},{1,0},{2,1},{3,2},{4,7},{5,4},{6,5},{7,6},{8,11},{9,8},{10,9... | collective-permute-start | bytes 786440 | tf_op jit(solution)/shard_map/ppermute | solution.py:32
  335.1 21.3 %collective-permute-start.39 = (bf16[128,1024]{1,0:T(8,128)(2,1)}, bf16[128,1024]{1,0:T(8,128)(2,1)}, u32[]{:S(2)}, u32[]{:S(2)}) collective-permute-start(bf16[128,1024]{1,0:T(8,128)(2,1)} %copy-done.57), channel_id=1, source_target_pairs={{0,2},{1,3},{2,0},{3,1},{4,6},{5,7},{6,4},{7,5},{8,10},{9,11},{10,... | collective-permute-start | bytes 786440 | tf_op jit(solution)/shard_map/ppermute | solution.py:32
  337.0 24.0 %collective-permute-start.40 = (bf16[128,1024]{1,0:T(8,128)(2,1)}, bf16[128,1024]{1,0:T(8,128)(2,1)}, u32[]{:S(2)}, u32[]{:S(2)}) collective-permute-start(bf16[128,1024]{1,0:T(8,128)(2,1)} %copy-done.62), channel_id=1, source_target_pairs={{0,1},{1,2},{2,3},{3,0},{4,5},{5,6},{6,7},{7,4},{8,9},{9,10},{10,1... | collective-permute-start | bytes 786440 | tf_op jit(solution)/shard_map/ppermute | solution.py:32
  345.4 25.5 %all-to-all-start.5 = ((bf16[32,6,512]{2,1,0:T(8,128)(2,1)}), bf16[32,6,512]{2,1,0:T(8,128)(2,1)S(1)}, u32[]{:S(2)}, u32[]{:S(2)}) async-start(bf16[32,6,512]{2,1,0:T(8,128)(2,1)} %all_to_all.92), calls=%async_computation.5 | async-start | bytes 524288 | tf_op jit(solution)/shard_map/all_to_all | solution.py:61
  354.8 39.9 %collective-permute-start.62 = (bf16[192,512]{1,0:T(8,128)(2,1)}, bf16[192,512]{1,0:T(8,128)(2,1)}, u32[]{:S(2)}, u32[]{:S(2)}) collective-permute-start(bf16[192,512]{1,0:T(8,128)(2,1)} %copy-done.91), channel_id=1, source_target_pairs={{0,1},{1,2},{2,3},{3,0},{4,5},{5,6},{6,7},{7,4},{8,9},{9,10},{10,1... | collective-permute-start | bytes 589832 | tf_op jit(solution)/shard_map/ppermute | solution.py:32
  356.5 38.9 %collective-permute-start.55 = (bf16[192,512]{1,0:T(8,128)(2,1)}, bf16[192,512]{1,0:T(8,128)(2,1)}, u32[]{:S(2)}, u32[]{:S(2)}) collective-permute-start(bf16[192,512]{1,0:T(8,128)(2,1)} %all_to_all.88), channel_id=1, source_target_pairs={{0,3},{1,0},{2,1},{3,2},{4,7},{5,4},{6,5},{7,6},{8,11},{9,8},{10,9... | collective-permute-start | bytes 589832 | tf_op jit(solution)/shard_map/ppermute | solution.py:32
  361.1 34.3 %collective-permute-start.54 = (bf16[192,512]{1,0:T(8,128)(2,1)}, bf16[192,512]{1,0:T(8,128)(2,1)}, u32[]{:S(2)}, u32[]{:S(2)}) collective-permute-start(bf16[192,512]{1,0:T(8,128)(2,1)} %all_to_all.88), channel_id=1, source_target_pairs={{0,2},{1,3},{2,0},{3,1},{4,6},{5,7},{6,4},{7,5},{8,10},{9,11},{10,... | collective-permute-start | bytes 589832 | tf_op jit(solution)/shard_map/ppermute | solution.py:32
  381.3 16.8 %collective-permute-start.53 = (bf16[192,512]{1,0:T(8,128)(2,1)}, bf16[192,512]{1,0:T(8,128)(2,1)}, u32[]{:S(2)}, u32[]{:S(2)}) collective-permute-start(bf16[192,512]{1,0:T(8,128)(2,1)} %all_to_all.88), channel_id=1, source_target_pairs={{0,1},{1,2},{2,3},{3,0},{4,5},{5,6},{6,7},{7,4},{8,9},{9,10},{10,1... | collective-permute-start | bytes 589832 | tf_op jit(solution)/shard_map/ppermute | solution.py:32
  382.2 17.0 %collective-permute-start.61 = (bf16[192,512]{1,0:T(8,128)(2,1)}, bf16[192,512]{1,0:T(8,128)(2,1)}, u32[]{:S(2)}, u32[]{:S(2)}) collective-permute-start(bf16[192,512]{1,0:T(8,128)(2,1)} %all_to_all.94), channel_id=1, source_target_pairs={{0,3},{1,0},{2,1},{3,2},{4,7},{5,4},{6,5},{7,6},{8,11},{9,8},{10,9... | collective-permute-start | bytes 589832 | tf_op jit(solution)/shard_map/ppermute | solution.py:32
  386.2 17.4 %all-to-all-start.6 = ((bf16[32,6,512]{2,1,0:T(8,128)(2,1)}), bf16[32,6,512]{2,1,0:T(8,128)(2,1)S(1)}, u32[]{:S(2)}, u32[]{:S(2)}) async-start(bf16[32,6,512]{2,1,0:T(8,128)(2,1)} %all_to_all.95), calls=%async_computation.6 | async-start | bytes 524288 | tf_op jit(solution)/shard_map/all_to_all | solution.py:61
  399.2 17.3 %collective-permute-start.56 = (bf16[192,512]{1,0:T(8,128)(2,1)}, bf16[192,512]{1,0:T(8,128)(2,1)}, u32[]{:S(2)}, u32[]{:S(2)}) collective-permute-start(bf16[192,512]{1,0:T(8,128)(2,1)} %copy-done.100), channel_id=1, source_target_pairs={{0,1},{1,2},{2,3},{3,0},{4,5},{5,6},{6,7},{7,4},{8,9},{9,10},{10,1... | collective-permute-start | bytes 589832 | tf_op jit(solution)/shard_map/ppermute | solution.py:32
  404.3 15.4 %collective-permute-start.31 = (bf16[192,512]{1,0:T(8,128)(2,1)}, bf16[192,512]{1,0:T(8,128)(2,1)S(1)}, u32[]{:S(2)}, u32[]{:S(2)}) collective-permute-start(bf16[192,512]{1,0:T(8,128)(2,1)} %all_to_all.97), channel_id=1, source_target_pairs={{0,3},{1,0},{2,1},{3,2},{4,7},{5,4},{6,5},{7,6},{8,11},{9,8},{10,9... | collective-permute-start | bytes 589832 | tf_op jit(solution)/shard_map/ppermute | solution.py:32
  408.8 15.6 %collective-permute-start.29 = (bf16[192,512]{1,0:T(8,128)(2,1)}, bf16[192,512]{1,0:T(8,128)(2,1)S(1)}, u32[]{:S(2)}, u32[]{:S(2)}) collective-permute-start(bf16[192,512]{1,0:T(8,128)(2,1)} %all_to_all.97), channel_id=1, source_target_pairs={{0,1},{1,2},{2,3},{3,0},{4,5},{5,6},{6,7},{7,4},{8,9},{9,10},{10,1... | collective-permute-start | bytes 589832 | tf_op jit(solution)/shard_map/ppermute | solution.py:32
  411.9 79.5 %collective-permute-start.52 = (bf16[192,512]{1,0:T(8,128)(2,1)}, bf16[192,512]{1,0:T(8,128)(2,1)}, u32[]{:S(2)}, u32[]{:S(2)}) collective-permute-start(bf16[192,512]{1,0:T(8,128)(2,1)} %get-tuple-element.389), channel_id=1, source_target_pairs={{0,3},{1,0},{2,1},{3,2},{4,7},{5,4},{6,5},{7,6},{8,11},{9,8},{10,9... | collective-permute-start | bytes 589832 | tf_op jit(solution)/shard_map/ppermute | solution.py:32
  416.5 77.3 %collective-permute-start.50 = (bf16[192,512]{1,0:T(8,128)(2,1)}, bf16[192,512]{1,0:T(8,128)(2,1)}, u32[]{:S(2)}, u32[]{:S(2)}) collective-permute-start(bf16[192,512]{1,0:T(8,128)(2,1)} %get-tuple-element.385), channel_id=1, source_target_pairs={{0,1},{1,2},{2,3},{3,0},{4,5},{5,6},{6,7},{7,4},{8,9},{9,10},{10,1... | collective-permute-start | bytes 589832 | tf_op jit(solution)/shard_map/ppermute | solution.py:32
  419.7 76.1 %collective-permute-start.43 = (bf16[192,512]{1,0:T(8,128)(2,1)}, bf16[192,512]{1,0:T(8,128)(2,1)}, u32[]{:S(2)}, u32[]{:S(2)}) collective-permute-start(bf16[192,512]{1,0:T(8,128)(2,1)} %all_to_all.82), channel_id=1, source_target_pairs={{0,3},{1,0},{2,1},{3,2},{4,7},{5,4},{6,5},{7,6},{8,11},{9,8},{10,9... | collective-permute-start | bytes 589832 | tf_op jit(solution)/shard_map/ppermute | solution.py:32
  422.4 74.3 %collective-permute-start.42 = (bf16[192,512]{1,0:T(8,128)(2,1)}, bf16[192,512]{1,0:T(8,128)(2,1)}, u32[]{:S(2)}, u32[]{:S(2)}) collective-permute-start(bf16[192,512]{1,0:T(8,128)(2,1)} %all_to_all.82), channel_id=1, source_target_pairs={{0,2},{1,3},{2,0},{3,1},{4,6},{5,7},{6,4},{7,5},{8,10},{9,11},{10,... | collective-permute-start | bytes 589832 | tf_op jit(solution)/shard_map/ppermute | solution.py:32
  424.4 72.2 %collective-permute-start.41 = (bf16[192,512]{1,0:T(8,128)(2,1)}, bf16[192,512]{1,0:T(8,128)(2,1)}, u32[]{:S(2)}, u32[]{:S(2)}) collective-permute-start(bf16[192,512]{1,0:T(8,128)(2,1)} %all_to_all.82), channel_id=1, source_target_pairs={{0,1},{1,2},{2,3},{3,0},{4,5},{5,6},{6,7},{7,4},{8,9},{9,10},{10,1... | collective-permute-start | bytes 589832 | tf_op jit(solution)/shard_map/ppermute | solution.py:32
  458.2 16.8 %all-to-all-start.7 = ((bf16[32,6,512]{2,1,0:T(8,128)(2,1)}), bf16[32,6,512]{2,1,0:T(8,128)(2,1)}, u32[]{:S(2)}, u32[]{:S(2)}) async-start(bf16[32,6,512]{2,1,0:T(8,128)(2,1)} %all_to_all.98), calls=%async_computation.7 | async-start | bytes 524288 | tf_op jit(solution)/shard_map/all_to_all | solution.py:61
  487.6 21.9 %all-to-all-start.8 = ((bf16[32,6,512]{2,1,0:T(8,128)(2,1)}), bf16[32,6,512]{2,1,0:T(8,128)(2,1)S(1)}, u32[]{:S(2)}, u32[]{:S(2)}) async-start(bf16[32,6,512]{2,1,0:T(8,128)(2,1)} %all_to_all.101), calls=%async_computation.8 | async-start | bytes 524288 | tf_op jit(solution)/shard_map/all_to_all | solution.py:61
  495.8 22.2 %collective-permute-start.48 = (bf16[192,512]{1,0:T(8,128)(2,1)S(1)}, bf16[192,512]{1,0:T(8,128)(2,1)}, u32[]{:S(2)}, u32[]{:S(2)}) collective-permute-start(bf16[192,512]{1,0:T(8,128)(2,1)S(1)} %copy-done.84), channel_id=1, source_target_pairs={{0,2},{1,3},{2,0},{3,1},{4,6},{5,7},{6,4},{7,5},{8,10},{9,11},{10,... | collective-permute-start | bytes 589832 | tf_op jit(solution)/shard_map/ppermute | solution.py:32
  496.6 22.7 %collective-permute-start.47 = (bf16[192,512]{1,0:T(8,128)(2,1)S(1)}, bf16[192,512]{1,0:T(8,128)(2,1)}, u32[]{:S(2)}, u32[]{:S(2)}) collective-permute-start(bf16[192,512]{1,0:T(8,128)(2,1)S(1)} %copy-done.84), channel_id=1, source_target_pairs={{0,1},{1,2},{2,3},{3,0},{4,5},{5,6},{6,7},{7,4},{8,9},{9,10},{10,1... | collective-permute-start | bytes 589832 | tf_op jit(solution)/shard_map/ppermute | solution.py:32
  496.6 23.6 %collective-permute-start.46 = (bf16[192,512]{1,0:T(8,128)(2,1)}, bf16[192,512]{1,0:T(8,128)(2,1)}, u32[]{:S(2)}, u32[]{:S(2)}) collective-permute-start(bf16[192,512]{1,0:T(8,128)(2,1)} %copy-done.97), channel_id=1, source_target_pairs={{0,3},{1,0},{2,1},{3,2},{4,7},{5,4},{6,5},{7,6},{8,11},{9,8},{10,9... | collective-permute-start | bytes 589832 | tf_op jit(solution)/shard_map/ppermute | solution.py:32
  500.5 23.3 %collective-permute-start.45 = (bf16[192,512]{1,0:T(8,128)(2,1)S(1)}, bf16[192,512]{1,0:T(8,128)(2,1)}, u32[]{:S(2)}, u32[]{:S(2)}) collective-permute-start(bf16[192,512]{1,0:T(8,128)(2,1)S(1)} %fusion.34), channel_id=1, source_target_pairs={{0,2},{1,3},{2,0},{3,1},{4,6},{5,7},{6,4},{7,5},{8,10},{9,11},{10,... | collective-permute-start | bytes 589832 | tf_op jit(solution)/shard_map/ppermute | solution.py:32
  503.9 19.9 %collective-permute-start.44 = (bf16[192,512]{1,0:T(8,128)(2,1)}, bf16[192,512]{1,0:T(8,128)(2,1)}, u32[]{:S(2)}, u32[]{:S(2)}) collective-permute-start(bf16[192,512]{1,0:T(8,128)(2,1)} %copy-done.96), channel_id=1, source_target_pairs={{0,1},{1,2},{2,3},{3,0},{4,5},{5,6},{6,7},{7,4},{8,9},{9,10},{10,1... | collective-permute-start | bytes 589832 | tf_op jit(solution)/shard_map/ppermute | solution.py:32
  509.6 29.4 %all-to-all-start.11 = ((bf16[32,16,1024]{2,1,0:T(8,128)(2,1)}), bf16[32,16,1024]{2,1,0:T(8,128)(2,1)}, u32[]{:S(2)}, u32[]{:S(2)}) async-start(bf16[32,16,1024]{2,1,0:T(8,128)(2,1)} %bitcast.340), calls=%async_computation.11 | async-start | bytes 2097152 | tf_op jit(solution)/shard_map/all_to_all | solution.py:61
  538.9 16.3 %all-to-all-start.9 = ((bf16[32,16,256]{2,1,0:T(8,128)(2,1)}), bf16[32,16,256]{2,1,0:T(8,128)(2,1)S(1)}, u32[]{:S(2)}, u32[]{:S(2)}) async-start(bf16[32,16,256]{2,1,0:T(8,128)(2,1)} %concatenate.127), calls=%async_computation.9 | async-start | bytes 524288 | tf_op jit(solution)/shard_map/all_to_all | solution.py:61
  549.4 38.9 %collective-permute-start.73 = (bf16[512,512]{1,0:T(8,128)(2,1)}, bf16[512,512]{1,0:T(8,128)(2,1)}, u32[]{:S(2)}, u32[]{:S(2)}) collective-permute-start(bf16[512,512]{1,0:T(8,128)(2,1)} %get-tuple-element.354), channel_id=1, source_target_pairs={{0,3},{1,0},{2,1},{3,2},{4,7},{5,4},{6,5},{7,6},{8,11},{9,8},{10,9... | collective-permute-start | bytes 1572872 | tf_op jit(solution)/shard_map/ppermute | solution.py:32
  549.7 40.2 %collective-permute-start.72 = (bf16[512,512]{1,0:T(8,128)(2,1)}, bf16[512,512]{1,0:T(8,128)(2,1)}, u32[]{:S(2)}, u32[]{:S(2)}) collective-permute-start(bf16[512,512]{1,0:T(8,128)(2,1)} %get-tuple-element.355), channel_id=1, source_target_pairs={{0,2},{1,3},{2,0},{3,1},{4,6},{5,7},{6,4},{7,5},{8,10},{9,11},{10,... | collective-permute-start | bytes 1572872 | tf_op jit(solution)/shard_map/ppermute | solution.py:32
  550.6 39.3 %collective-permute-start.71 = (bf16[512,512]{1,0:T(8,128)(2,1)}, bf16[512,512]{1,0:T(8,128)(2,1)}, u32[]{:S(2)}, u32[]{:S(2)}) collective-permute-start(bf16[512,512]{1,0:T(8,128)(2,1)} %get-tuple-element.356), channel_id=1, source_target_pairs={{0,1},{1,2},{2,3},{3,0},{4,5},{5,6},{6,7},{7,4},{8,9},{9,10},{10,1... | collective-permute-start | bytes 1572872 | tf_op jit(solution)/shard_map/ppermute | solution.py:32
  555.2 20.4 %all-to-all-start.10 = ((bf16[32,16,896]{2,1,0:T(8,128)(2,1)}), bf16[32,16,896]{2,1,0:T(8,128)(2,1)}, u32[]{:S(2)}, u32[]{:S(2)}) async-start(bf16[32,16,896]{2,1,0:T(8,128)(2,1)} %pad_maximum_fusion.6), calls=%async_computation.10 | async-start | bytes 1835008 | tf_op jit(solution)/shard_map/all_to_all | solution.py:61
  577.0 16.1 %collective-permute-start.65 = (f32[16,896]{1,0:T(8,128)S(1)}, f32[16,896]{1,0:T(8,128)S(1)}, u32[]{:S(2)}, u32[]{:S(2)}) collective-permute-start(f32[16,896]{1,0:T(8,128)S(1)} %convert_reduce_fusion.1), channel_id=1, source_target_pairs={{0,3},{1,0},{2,1},{3,2},{4,7},{5,4},{6,5},{7,6},{8,11},{9,8},{10,9... | collective-permute-start | bytes 172040 | tf_op jit(solution)/shard_map/ppermute | solution.py:32
  583.3 14.5 %all-to-all-start.12 = ((f32[128,1,128]{2,1,0:T(1,128)}), f32[128,1,128]{2,1,0:T(1,128)S(1)}, u32[]{:S(2)}, u32[]{:S(2)}) async-start(f32[128,1,128]{2,1,0:T(1,128)} %broadcast_in_dim.36), calls=%async_computation.12 | async-start | bytes 131072 | tf_op jit(solution)/shard_map/all_to_all | solution.py:571
  630.9 15.3 %collective-permute-start.74 = (bf16[512,512]{1,0:T(8,128)(2,1)}, bf16[512,512]{1,0:T(8,128)(2,1)S(1)}, u32[]{:S(2)}, u32[]{:S(2)}) collective-permute-start(bf16[512,512]{1,0:T(8,128)(2,1)} %get-tuple-element.352), channel_id=1, source_target_pairs={{0,3},{1,0},{2,1},{3,2},{4,7},{5,4},{6,5},{7,6},{8,11},{9,8},{10,9... | collective-permute-start | bytes 1572872 | tf_op jit(solution)/shard_map/ppermute | solution.py:32
  633.0 25.8 %collective-permute-start.76 = (bf16[512,512]{1,0:T(8,128)(2,1)}, bf16[512,512]{1,0:T(8,128)(2,1)}, u32[]{:S(2)}, u32[]{:S(2)}) collective-permute-start(bf16[512,512]{1,0:T(8,128)(2,1)} %get-tuple-element.350), channel_id=1, source_target_pairs={{0,1},{1,2},{2,3},{3,0},{4,5},{5,6},{6,7},{7,4},{8,9},{9,10},{10,1... | collective-permute-start | bytes 1572872 | tf_op jit(solution)/shard_map/ppermute | solution.py:32
  (299 other events, 2274.9 us)
Sparse Core Ops, SparseCore 0:
  10.9 48.0 all-gather.4
  61.2 45.1 all-gather.2

commit v2 on v1

v2 whole, which is shorter than its diff:
```python
import functools

import jax
import jax.numpy as jnp
from jax import lax
from jax.experimental import pallas as pl
from jax.experimental.pallas import tpu as pltpu
from jax.sharding import PartitionSpec as P

D = 512
HEADS = 8
HEAD_DIM = 64
FF = 2048
STEP = 10
LANES = 128


clip_limit = 0.02
beta_one = 0.9
beta_two = 0.999
adam_epsilon = 1e-08
adam_rate = 0.2
gain_rate = 0.6
weight_decay = 0.01
muon_beta = 0.95
muon_rate = 1.0
muon_decay = 0.01
newton_first = 3.4445
newton_second = -4.775
newton_third = 2.0315


def shift(values, step):
    size = lax.axis_size("hid")
    return lax.ppermute(values, "hid", [(i, (i + step) % size) for i in range(size)])


def gather_near(values):
    return [values] + [shift(values, step) for step in range(1, lax.axis_size("hid"))]


def after(values, *earlier):
    return lax.optimization_barrier((values,) + earlier)[0]


def spread(pieces, *earlier):
    pieces = after(tuple(pieces), *earlier)
    return [pieces[0]] + [shift(pieces[step], step) for step in range(1, len(pieces))]


def own_part(values, axis):
    width = values.shape[axis] // lax.axis_size("hid")
    return lax.dynamic_slice_in_dim(values, lax.axis_index("hid") * width, width, axis)


def exchange_rows(values):
    owners = lax.axis_size("dp")
    shape = values.shape
    shaped_rows = values.reshape((owners, shape[0] // owners) + shape[1:])
    moved = lax.all_to_all(shaped_rows, "dp", split_axis=0, concat_axis=0, tiled=True)
    return moved.reshape(shape)


def to_low(values):
    return values.astype(jnp.bfloat16)


def dot_low(left, right):
    return jnp.dot(left, right, preferred_element_type=jnp.float32)


def dot_left(left, right):
    return lax.dot_general(
        left, right, (((0,), (0,)), ((), ())), preferred_element_type=jnp.float32
    )


def dot_right(left, right):
    return lax.dot_general(
        left, right, (((1,), (1,)), ((), ())), preferred_element_type=jnp.float32
    )


def exact_dot(left, right, dims=((1,), (0,))):
    return lax.dot_general(
        left,
        right,
        (dims, ((), ())),
        precision=lax.Precision.HIGHEST,
        preferred_element_type=jnp.float32,
    )


def two_parts(values):
    high = to_low(values)
    return high, to_low(values - high.astype(jnp.float32))


def close_dot(left, right):
    return dot_low(left[0], right[0]) + (dot_low(left[0], right[1]) + dot_low(left[1], right[0]))


def norm_forward(values, gain):
    centered = values - jnp.mean(values, -1, keepdims=True)
    inverse = lax.rsqrt(jnp.mean(centered * centered, -1, keepdims=True) + 1e-05)
    unit = centered * inverse
    return (unit * gain, unit, inverse)


def norm_backward(grad, unit, inverse, gain):
    scaled = grad * gain
    back = inverse * (
        scaled
        - jnp.mean(scaled, -1, keepdims=True)
        - unit * jnp.mean(scaled * unit, -1, keepdims=True)
    )
    return (back, jnp.sum(grad * unit, 0, keepdims=True))


def silu_slope(values):
    sigma = jax.nn.sigmoid(values)
    return sigma * (1.0 + values * (1.0 - sigma))


def shaped(shape, dtype):
    return jax.ShapeDtypeStruct(shape, dtype)


def place_of(shape, axis):
    return lax.broadcasted_iota(jnp.int32, shape, axis)


def whole_call(kernel, out_shapes, scalars, arrays, flops, scratch=()):
    parts = [part if isinstance(part, tuple) else (part, None, None) for part in arrays]
    specs = [
        pl.BlockSpec(memory_space=pltpu.VMEM)
        if block is None
        else pl.BlockSpec(block, functools.partial(lambda fixed, step: fixed, at))
        for _, block, at in parts
    ]
    moved = sum(part.size * part.dtype.itemsize for part, _, _ in parts) + sum(
        part.size * part.dtype.itemsize for part in out_shapes
    )
    return pl.pallas_call(
        kernel,
        grid=(1,),
        out_shape=out_shapes,
        in_specs=[pl.BlockSpec(memory_space=pltpu.SMEM)] * len(scalars) + specs,
        out_specs=[pl.BlockSpec(memory_space=pltpu.VMEM)] * len(out_shapes),
        scratch_shapes=list(scratch),
        compiler_params=pltpu.CompilerParams(vmem_limit_bytes=48 * 1024 * 1024),
        cost_estimate=pl.CostEstimate(flops=flops, bytes_accessed=moved, transcendentals=0),
    )(*scalars, *[part for part, _, _ in parts])


def pack_small_kernel(owners, input_ref, router_ref, depth_ref, gains_ref, out_ref, turn_ref):
    bands, taps, gains = input_ref.shape[1], depth_ref.shape[0], gains_ref.shape[0]
    width = input_ref.shape[0]
    turn_ref[...] = jnp.zeros(turn_ref.shape, jnp.float32)
    turn_ref[2 * owners : 2 * owners + taps, :width] = depth_ref[...]
    turn_ref[2 * owners + taps : 2 * owners + taps + gains, :width] = gains_ref[...]
    turned = turn_ref[...].T[:width]
    out_ref[...] = jnp.zeros(out_ref.shape, jnp.float32)
    for owner in range(owners):
        out_ref[owner, :, LANES:] = turned
        out_ref[owner, :, :bands] = input_ref[...]
        out_ref[owner, :, LANES : LANES + owners] = router_ref[0]
        out_ref[owner, :, LANES + owners : LANES + 2 * owners] = router_ref[1]


def pack_small(input_turned, router, depthwise, norm_scales):
    owners, width = lax.axis_size("dp"), input_turned.shape[0]
    return whole_call(
        functools.partial(pack_small_kernel, owners),
        [shaped((owners, width, 2 * LANES), jnp.float32)],
        [],
        [input_turned, router, depthwise, norm_scales],
        1000,
        [pltpu.VMEM((LANES, LANES), jnp.float32)],
    )[0]


def pack_dense_kernel(attention_ref, branch_ref, pointwise_ref, *refs):
    out_ref = refs[-1]
    for part in range(3):
        out_ref[part] = to_low(attention_ref[:, part * D : (part + 1) * D])
    for part in range(2):
        out_ref[3 + part] = to_low(branch_ref[part])
        out_ref[5 + part] = to_low(pointwise_ref[:, part * D : (part + 1) * D])
    place = 7
    for ref in refs[:-1]:
        for part in range(ref.shape[1] // D):
            out_ref[place] = ref[:, part * D : (part + 1) * D]
            place += 1


def pack_dense(attention_in, branch_out, pointwise_in, senone_rows):
    rows = attention_in.shape[0]
    count = 7 + sum(part.shape[1] // D for part in senone_rows)
    return whole_call(
        pack_dense_kernel,
        [shaped((count, rows, D), jnp.bfloat16)],
        [],
        [attention_in, branch_out, pointwise_in, *senone_rows],
        1000,
    )[0]


def plan_kernel(experts, splits, share, wide, place_ref, routes_ref, out_ref):
    tokens = routes_ref.shape[1]
    before = (place_of((tokens, tokens), 0) < place_of((tokens, tokens), 1)).astype(jnp.float32)
    for mixture in range(2):
        route = routes_ref[mixture : mixture + 1]
        onehot = (place_of((experts, tokens), 0) == route).astype(jnp.float32)
        earlier = dot_low(to_low(onehot), to_low(before))
        slot = jnp.sum(earlier * onehot, 0, keepdims=True).astype(jnp.int32)
        quarter = sum((slot >= (part + 1) * share).astype(jnp.int32) for part in range(splits - 1))
        within = slot - quarter * share
        turned = (place_ref[0] - quarter + splits) % splits
        out_ref[2 * mixture : 2 * mixture + 1] = jnp.where(
            turned == 0, route * wide + within, -1
        )
        out_ref[2 * mixture + 1 : 2 * mixture + 2] = (turned * experts + route) * share + within


def plan_slots(place, routes, share, wide):
    return whole_call(
        functools.partial(
            plan_kernel, lax.axis_size("dp"), lax.axis_size("hid"), share, wide
        ),
        [shaped((4, routes.shape[1]), jnp.int32)],
        [place],
        [routes],
        1_000_000,
    )[0]


def narrowing(share_rows, wide_rows, share, wide):
    at = place_of((share_rows, wide_rows), 1)
    within = at % wide
    return to_low(
        ((place_of((share_rows, wide_rows), 0) == at // wide * share + within) & (within < share))
        .astype(jnp.float32)
    )


def routing(mixture, experts, normed, router, route):
    column = place_of((normed.shape[0], LANES), 1) - mixture * experts
    inside = (column >= 0) & (column < experts)
    logits = jnp.where(inside, exact_dot(normed, router), -1e30)
    raised = jnp.where(inside, jnp.exp(logits - jnp.max(logits, 1, keepdims=True)), 0.0)
    return raised / jnp.sum(raised, 1, keepdims=True), (column == route).astype(jnp.float32)


def dispatch(mixture, experts, values, gain, router, route, index, slots_ref, gate_ref, chances_ref):
    normed, _, _ = norm_forward(values, gain)
    chosen = (place_of((slots_ref.shape[0], values.shape[0]), 0) == index).astype(jnp.float32)
    slots_ref[...] = to_low(dot_low(to_low(chosen), to_low(normed)))
    chances, onehot = routing(mixture, experts, normed, router, route)
    gate_ref[...] = jnp.sum(chances * onehot, 1, keepdims=True)
    chances_ref[...] = chances


def dispatch_shapes(tokens, wide_rows):
    return [
        shaped((wide_rows, D), jnp.bfloat16),
        shaped((tokens, 1), jnp.float32),
        shaped((tokens, LANES), jnp.float32),
    ]


def start_kernel(
    experts, gain_row, small_ref, features_ref, plan_ref, route_ref, start_ref, turned_ref, *out
):
    bands = features_ref.shape[0]
    start = lax.dot_general(
        features_ref[...],
        to_low(small_ref[:, :bands]),
        (((0,), (1,)), ((), ())),
        preferred_element_type=jnp.float32,
    )
    start_ref[...] = start
    router = small_ref[:, LANES:]
    turned_ref[...] = router.T
    gain = turned_ref[gain_row : gain_row + 1]
    dispatch(0, experts, start, gain, router, route_ref[0], plan_ref[:1], *out)


def start_step(small, features_turned, plan, routes, gain_row, wide_rows):
    tokens = features_turned.shape[1]
    return whole_call(
        functools.partial(start_kernel, lax.axis_size("dp"), gain_row),
        [shaped((tokens, D), jnp.float32), shaped((LANES, D), jnp.float32)]
        + dispatch_shapes(tokens, wide_rows),
        [],
        [small, features_turned, plan, routes],
        700_000_000,
    )


def dispatch_kernel(
    mixture, experts, gain_row, values_ref, small_ref, turned_ref, plan_ref, route_ref, *out
):
    dispatch(
        mixture,
        experts,
        values_ref[...],
        turned_ref[gain_row : gain_row + 1],
        small_ref[:, LANES:],
        route_ref[mixture],
        plan_ref[2 * mixture : 2 * mixture + 1],
        *out,
    )


def dispatch_step(mixture, values, small, turned, plan, routes, gain_row, wide_rows):
    return whole_call(
        functools.partial(dispatch_kernel, mixture, lax.axis_size("dp"), gain_row),
        dispatch_shapes(values.shape[0], wide_rows),
        [],
        [values, small, turned, plan, routes],
        700_000_000,
    )


def expert_pieces(refs, place, step, splits):
    if len(refs) == 1:
        return tuple(refs[0][(place + splits - step) % splits, part] for part in range(2))
    own, before, behind, across_in, across_out = refs
    if step == 2:
        return across_in[...], across_out[...]
    chosen = (own, before, None, behind)[step]
    return chosen[0], chosen[1]


def expert_forward_kernel(splits, share, wide, place_ref, rows_ref, *refs):
    weights, sent_refs, returned_ref = refs[: -splits - 1], refs[-splits - 1 : -1], refs[-1]
    place, count = place_ref[0], sent_refs[0].shape[0] // 2
    narrow = narrowing(count, rows_ref.shape[0], share, wide)
    rows = to_low(dot_low(narrow, rows_ref[...]))
    total = jnp.zeros(rows.shape, jnp.float32)
    for step in range(splits):
        weight_in, weight_out = expert_pieces(weights, place, step, splits)
        active = dot_low(rows, weight_in)
        hidden = to_low(active * jax.nn.sigmoid(active))
        sent_ref = sent_refs[(splits - step) % splits]
        sent_ref[:count] = rows
        sent_ref[count:] = hidden
        total = total + dot_right(hidden, weight_out)
    returned_ref[...] = to_low(dot_left(narrow, to_low(total)))


def expert_backward_kernel(splits, share, wide, place_ref, kept_ref, grad_ref, *refs):
    weights, sent_refs, returned_ref = refs[: -splits - 1], refs[-splits - 1 : -1], refs[-1]
    place, count = place_ref[0], kept_ref.shape[0] // 2
    narrow = narrowing(count, grad_ref.shape[0], share, wide)
    rows, rows_grad = kept_ref[:count], to_low(dot_low(narrow, grad_ref[...]))
    total = jnp.zeros(rows.shape, jnp.float32)
    for step in range(splits):
        weight_in, weight_out = expert_pieces(weights, place, step, splits)
        active = dot_low(rows, weight_in)
        active_grad = to_low(dot_low(rows_grad, weight_out) * silu_slope(active))
        sent_ref = sent_refs[(splits - step) % splits]
        sent_ref[:count] = rows_grad
        sent_ref[count:] = active_grad
        total = total + dot_right(active_grad, weight_in)
    returned_ref[...] = to_low(dot_left(narrow, to_low(total)))


def expert_call(kernel, place, arrays, weights, slots, rows, flops):
    splits, experts = lax.axis_size("hid"), lax.axis_size("dp")
    share, wide = slots
    *sent, returned = whole_call(
        functools.partial(kernel, splits, share, wide),
        [shaped((2 * experts * share, D), jnp.bfloat16)] * splits
        + [shaped(rows.shape, jnp.bfloat16)],
        [place],
        [*arrays, *weights],
        flops,
    )
    return sent, returned


def expert_forward(place, rows, weights, slots):
    return expert_call(
        expert_forward_kernel, place, [rows], weights, slots, rows, 4 * rows.shape[0] * D * FF
    )


def expert_backward(place, kept, rows_grad, weights, slots):
    return expert_call(
        expert_backward_kernel,
        place,
        [kept, rows_grad],
        weights,
        slots,
        rows_grad,
        6 * rows_grad.shape[0] * D * FF,
    )


def narrow_kernel(share, wide, rows_ref, out_ref):
    narrow = narrowing(out_ref.shape[0], rows_ref.shape[0], share, wide)
    out_ref[...] = to_low(dot_low(narrow, rows_ref[...]))


def gather_slots(rows, slots):
    share, wide = slots
    narrow = whole_call(
        functools.partial(narrow_kernel, share, wide),
        [shaped((rows.shape[0] // wide * share, D), jnp.bfloat16)],
        [],
        [rows],
        50_000_000,
    )[0]
    return gather_near(narrow)


def combined(position, blocks):
    share, tokens = blocks[0].shape[0], position.shape[1]
    row = place_of((share, tokens), 0)
    return sum(
        dot_left(to_low((position - step * share == row).astype(jnp.float32)), block[...])
        for step, block in enumerate(blocks)
    )


def combine_kernel(mixture, plan_ref, gate_ref, base_ref, *refs):
    blocks, expert_out_ref, out_ref = refs[:-2], refs[-2], refs[-1]
    total = combined(plan_ref[2 * mixture + 1 : 2 * mixture + 2], blocks)
    expert_out_ref[...] = total
    out_ref[...] = base_ref[...] + 0.5 * gate_ref[...] * total


def combine_step(mixture, plan, gate, base, blocks):
    return whole_call(
        functools.partial(combine_kernel, mixture),
        [shaped(base.shape, jnp.float32)] * 2,
        [],
        [plan, gate, base, *blocks],
        500_000_000,
    )


def both_grads(forward, backward):
    share = forward[0].shape[0] // 2
    return (
        sum(dot_left(ahead[:share], behind[share:]) for ahead, behind in zip(forward, backward)),
        sum(dot_left(behind[:share], ahead[share:]) for ahead, behind in zip(forward, backward)),
    )


def expert_grad_kernel(splits, *refs):
    out_ref = refs[-1]
    out_ref[0], out_ref[1] = both_grads(refs[:splits], refs[splits : 2 * splits])


def last_grad_kernel(splits, place_ref, *refs):
    later_ref, out_ref = refs[2 * splits], refs[2 * splits + 1]
    square_ref, sent_refs, all_ref = refs[2 * splits + 2], refs[2 * splits + 3 : -1], refs[-1]
    all_ref[0], all_ref[1] = both_grads(refs[:splits], refs[splits : 2 * splits])
    out_ref[...] = all_ref[:2]
    all_ref[2:] = later_ref[...]
    square = jnp.zeros((1, D), jnp.float32)
    for part in range(4):
        square = square + jnp.sum(all_ref[part] * all_ref[part], 0, keepdims=True)
    square_ref[...] = square
    for step, sent_ref in enumerate(sent_refs):
        sent_ref[...] = to_low(all_ref[(place_ref[0] + step) % 4])


def expert_grads(forward, backward):
    rows, width = forward[0].shape
    return whole_call(
        functools.partial(expert_grad_kernel, len(forward)),
        [shaped((2, width, width), jnp.float32)],
        [],
        [*forward, *backward],
        4 * rows * width * width * len(forward) // 2,
    )[0]


def last_expert_grads(place, forward, backward, later):
    rows, width = forward[0].shape
    splits = len(forward)
    out, square, *sent = whole_call(
        functools.partial(last_grad_kernel, splits),
        [shaped(later.shape, jnp.float32), shaped((1, width), jnp.float32)]
        + [shaped((width, width), jnp.bfloat16)] * splits,
        [place],
        [*forward, *backward, later],
        4 * rows * width * width * splits // 2,
        [pltpu.VMEM((4, width, width), jnp.float32)],
    )
    return out, square, sent


def attention_forward_kernel(
    gain_row, length_ref, values_ref, turned_ref, weight_ref, branch_ref, out_ref, parts_ref, log_ref, context_ref
):
    values = values_ref[...]
    tokens = values.shape[0]
    normed, _, _ = norm_forward(values, turned_ref[gain_row : gain_row + 1])
    low_normed = to_low(normed)
    for part in range(3):
        parts_ref[part] = to_low(dot_low(low_normed, weight_ref[part]))
    seen = place_of((tokens, tokens), 1) < length_ref[0]
    lane = place_of((tokens, LANES), 1)
    logs = jnp.zeros((tokens, LANES), jnp.float32)
    pair = LANES // HEAD_DIM
    for first in range(0, HEADS, pair):
        columns = slice(first * HEAD_DIM, (first + pair) * HEAD_DIM)
        queries, keys, contents = (parts_ref[part, :, columns] for part in range(3))
        context = jnp.zeros((tokens, LANES), jnp.float32)
        for head in range(pair):
            mine = lane // HEAD_DIM == head
            scores = dot_right(jnp.where(mine, queries, jnp.zeros_like(queries)), keys)
            scores = jnp.where(seen, scores * HEAD_DIM ** (-0.5), -1e30)
            top = jnp.max(scores, 1, keepdims=True)
            raised = jnp.exp(scores - top)
            total = jnp.sum(raised, 1, keepdims=True)
            mixed = dot_low(to_low(raised * (1.0 / total)), contents)
            context = jnp.where(mine, mixed, context)
            logs = jnp.where(lane == first + head, top + jnp.log(total), logs)
        context_ref[:, columns] = to_low(context)
    log_ref[...] = logs
    out_ref[...] = values + dot_low(context_ref[...], branch_ref[0])


def attention_forward(length, values, turned, dense, gain_row):
    tokens = values.shape[0]
    return whole_call(
        functools.partial(attention_forward_kernel, gain_row),
        [
            shaped((tokens, D), jnp.float32),
            shaped((3, tokens, D), jnp.bfloat16),
            shaped((tokens, LANES), jnp.float32),
            shaped((tokens, D), jnp.bfloat16),
        ],
        [length],
        [values, turned, (dense, (3, D, D), (0, 0, 0)), (dense, (1, D, D), (3, 0, 0))],
        4_000_000_000,
    )


def attention_backward_kernel(
    gain_row,
    length_ref,
    place_ref,
    grad_ref,
    values_ref,
    turned_ref,
    weight_ref,
    branch_ref,
    parts_ref,
    log_ref,
    context_ref,
    out_ref,
    gain_grad_ref,
    weight_grad_ref,
    low_ref,
    project_ref,
):
    grad = grad_ref[...]
    tokens = grad.shape[0]
    low_grad = to_low(grad)
    low_ref[...] = low_grad
    context_grad = to_low(dot_right(low_grad, branch_ref[0]))
    seen = place_of((tokens, tokens), 1) < length_ref[0]
    lane = place_of((tokens, LANES), 1)
    pair = LANES // HEAD_DIM
    scale = HEAD_DIM ** (-0.5)
    for first in range(0, HEADS, pair):
        columns = slice(first * HEAD_DIM, (first + pair) * HEAD_DIM)
        queries, keys, contents = (parts_ref[part, :, columns] for part in range(3))
        mixed_grad = context_grad[:, columns]
        grads = [jnp.zeros((tokens, LANES), jnp.float32)] * 3
        for head in range(pair):
            mine = lane // HEAD_DIM == head
            none = jnp.zeros_like(queries)
            scores = dot_right(jnp.where(mine, queries, none), keys) * scale
            log_total = jnp.sum(
                jnp.where(lane == first + head, log_ref[...], 0.0), 1, keepdims=True
            )
            weights = jnp.where(seen, jnp.exp(jnp.where(seen, scores, -1e30) - log_total), 0.0)
            weight_grad = dot_right(jnp.where(mine, mixed_grad, none), contents)
            score_grad = to_low(
                weights * (weight_grad - jnp.sum(weight_grad * weights, 1, keepdims=True))
            )
            found = (
                dot_low(score_grad, keys) * scale,
                dot_left(score_grad, queries) * scale,
                dot_left(to_low(weights), mixed_grad),
            )
            grads = [jnp.where(mine, new, old) for new, old in zip(found, grads)]
        for part in range(3):
            project_ref[part, :, columns] = to_low(grads[part])
    gain = turned_ref[gain_row : gain_row + 1]
    normed, unit, inverse = norm_forward(values_ref[...], gain)
    low_normed = to_low(normed)
    normed_grad = sum(dot_right(project_ref[part], weight_ref[part]) for part in range(3))
    back, gain_grad_ref[...] = norm_backward(normed_grad, unit, inverse, gain)
    out_ref[...] = grad + back
    width = weight_grad_ref.shape[1] // 4
    own = pl.ds(pl.multiple_of(place_ref[0] * width, width), width)
    for part in range(3):
        weight_grad_ref[:, part * width : (part + 1) * width] = to_low(
            dot_left(low_normed, project_ref[part, :, own])
        )
    weight_grad_ref[:, 3 * width :] = to_low(dot_left(context_ref[...], low_ref[:, own]))


def attention_backward(length, place, grad, values, turned, dense, kept, gain_row):
    tokens = values.shape[0]
    splits = lax.axis_size("hid")
    return whole_call(
        functools.partial(attention_backward_kernel, gain_row),
        [
            shaped((tokens, D), jnp.float32),
            shaped((1, D), jnp.float32),
            shaped((D, 4 * D // splits), jnp.bfloat16),
        ],
        [length, place],
        [
            grad,
            values,
            turned,
            (dense, (3, D, D), (0, 0, 0)),
            (dense, (1, D, D), (3, 0, 0)),
            *kept,
        ],
        9_000_000_000,
        [pltpu.VMEM((tokens, D), jnp.bfloat16), pltpu.VMEM((3, tokens, D), jnp.bfloat16)],
    )


def senone_kernel(
    gain_row, splits, length_ref, place_ref, values_ref, turned_ref, targets_ref, *refs
):
    low_ref, loss_ref, sent_ref = refs[-3 - splits], refs[-2 - splits], refs[-1 - splits]
    logit_refs = refs[-splits:]
    tables = refs[: -3 - splits]
    rows = values_ref.shape[0] // splits
    place = place_ref[0]
    gain = turned_ref[gain_row : gain_row + 1]
    normed, _, _ = norm_forward(values_ref[...], gain)
    low_ref[...] = to_low(normed)
    own = pl.ds(pl.multiple_of(place * rows, rows), rows)
    normed, unit, inverse = norm_forward(values_ref[own], gain)
    own_rows, targets = to_low(normed), targets_ref[own]
    halves = len(tables) // splits
    width = tables[0].shape[2]
    logits, picked = [], []
    for number, table in enumerate(tables):
        begin = ((place + splits - number // halves) % splits * halves + number % halves) * width
        logits.append(dot_low(own_rows, table[0]))
        picked.append(place_of((rows, width), 1) + begin == targets)
    top = functools.reduce(
        jnp.maximum, [jnp.max(part, 1, keepdims=True) for part in logits]
    )
    total = sum(jnp.sum(jnp.exp(part - top), 1, keepdims=True) for part in logits)
    target = sum(
        jnp.sum(jnp.where(chosen, part, 0.0), 1, keepdims=True)
        for chosen, part in zip(picked, logits)
    )
    log_total = top + jnp.log(total)
    valid = (place_of((rows, 1), 0) + place * rows < length_ref[0]).astype(jnp.float32)
    loss_ref[...] = jnp.sum(valid * (log_total - target), 0, keepdims=True)
    normed_grad = jnp.zeros((rows, D), jnp.float32)
    for number, (chosen, part, table) in enumerate(zip(picked, logits, tables)):
        logit_grad = to_low(
            valid * (jnp.exp(part - log_total) - chosen.astype(jnp.float32))
        )
        half = number % halves
        logit_refs[(splits - number // halves) % splits][
            :, half * width : (half + 1) * width
        ] = logit_grad
        normed_grad = normed_grad + dot_right(logit_grad, table[0])
    own_grad, gain_grad = norm_backward(normed_grad, unit, inverse, gain)
    high, low = two_parts(gain_grad)
    extra = place_of((sent_ref.shape[0] - rows, D), 0)
    sent_ref[:rows] = to_low(own_grad)
    sent_ref[rows:] = to_low(
        jnp.where(
            extra == 0,
            high.astype(jnp.float32),
            jnp.where(extra == 1, low.astype(jnp.float32), 0.0),
        )
    )


def senone_step(length, place, values, turned, targets, dense, gain_row):
    splits, tokens = lax.axis_size("hid"), values.shape[0]
    rows, first = tokens // splits, 7
    count = dense.shape[0] - first
    return whole_call(
        functools.partial(senone_kernel, gain_row, splits),
        [
            shaped((tokens, D), jnp.bfloat16),
            shaped((1, 1), jnp.float32),
            shaped((rows + 16, D), jnp.bfloat16),
        ]
        + [shaped((rows, count * D // splits), jnp.bfloat16)] * splits,
        [length, place],
        [values, turned, targets]
        + [(dense, (1, D, D), (first + number, 0, 0)) for number in range(count)],
        1_100_000_000,
    )


def pack_early_kernel(splits, place_ref, low_ref, *refs):
    blocks, others, out_ref = refs[:splits], refs[splits:-1], refs[-1]
    rows, width = blocks[0].shape
    total = None
    for step, block in enumerate(blocks):
        begin = pl.multiple_of((place_ref[0] + splits - step) % splits * rows, rows)
        part = dot_left(low_ref[pl.ds(begin, rows)], block[...])
        total = part if total is None else total + part
    out_ref[:, :width] = to_low(total)
    for other in others:
        out_ref[:, width : width + other.shape[1]] = to_low(other[...])
        width += other.shape[1]


def pack_early(place, low_normed, blocks, others):
    width = blocks[0].shape[1] + sum(part.shape[1] for part in others)
    return whole_call(
        functools.partial(pack_early_kernel, len(blocks)),
        [shaped((D, width), jnp.bfloat16)],
        [place],
        [low_normed, *blocks, *others],
        600_000_000,
    )[0]


def send_back(mixture, grad, plan_ref, gate_ref, rows_ref):
    index = plan_ref[2 * mixture : 2 * mixture + 1]
    chosen = (place_of((rows_ref.shape[0], grad.shape[0]), 0) == index).astype(jnp.float32)
    rows_ref[...] = to_low(dot_low(to_low(chosen), to_low(gate_ref[...] * (0.5 * grad))))


def assemble_kernel(mixture, place_ref, plan_ref, gate_ref, *refs):
    blocks, grad_ref, gain_grad_ref, rows_ref = refs[:-3], refs[-3], refs[-2], refs[-1]
    splits = len(blocks)
    rows = grad_ref.shape[0] // splits
    for step, block in enumerate(blocks):
        begin = pl.multiple_of((place_ref[0] + splits - step) % splits * rows, rows)
        grad_ref[pl.ds(begin, rows)] = block[:rows].astype(jnp.float32)
    gain_grad_ref[...] = sum(
        jnp.sum(block[rows:].astype(jnp.float32), 0, keepdims=True) for block in blocks
    )
    send_back(mixture, grad_ref[...], plan_ref, gate_ref, rows_ref)


def assemble_step(mixture, place, plan, gate, blocks, wide_rows):
    tokens = gate.shape[0]
    return whole_call(
        functools.partial(assemble_kernel, mixture),
        [
            shaped((tokens, D), jnp.float32),
            shaped((1, D), jnp.float32),
            shaped((wide_rows, D), jnp.bfloat16),
        ],
        [place],
        [plan, gate, *blocks],
        200_000_000,
    )


def send_back_kernel(mixture, plan_ref, gate_ref, grad_ref, rows_ref):
    send_back(mixture, grad_ref[...], plan_ref, gate_ref, rows_ref)


def send_back_step(mixture, plan, gate, grad, wide_rows):
    return whole_call(
        functools.partial(send_back_kernel, mixture),
        [shaped((wide_rows, D), jnp.bfloat16)],
        [],
        [plan, gate, grad],
        200_000_000,
    )[0]


def gate_backward_kernel(
    mixture,
    experts,
    gain_row,
    grad_ref,
    expert_out_ref,
    gate_ref,
    chances_ref,
    route_ref,
    values_ref,
    small_ref,
    turned_ref,
    side_ref,
    router_grad_ref,
):
    column = place_of((values_ref.shape[0], LANES), 1) - mixture * experts
    onehot = (column == route_ref[mixture]).astype(jnp.float32)
    gate_grad = jnp.sum(0.5 * grad_ref[...] * expert_out_ref[...], 1, keepdims=True)
    logit_grad = (gate_ref[...] * gate_grad) * (onehot - chances_ref[...])
    normed, _, _ = norm_forward(values_ref[...], turned_ref[gain_row : gain_row + 1])
    router_grad_ref[...] = exact_dot(normed, logit_grad, ((0,), (0,)))
    side_ref[...] = exact_dot(logit_grad, small_ref[:, LANES:], ((1,), (1,)))


def gate_backward(mixture, gain_row, grad, expert_out, gate, chances, routes, values, small, turned):
    return whole_call(
        functools.partial(gate_backward_kernel, mixture, lax.axis_size("dp"), gain_row),
        [shaped(grad.shape, jnp.float32), shaped((D, LANES), jnp.float32)],
        [],
        [grad, expert_out, gate, chances, routes, values, small, turned],
        800_000_000,
    )


def combine_backward_kernel(
    mixture, gain_row, plan_ref, grad_ref, side_ref, values_ref, turned_ref, *refs
):
    blocks, out_ref, gain_grad_ref = refs[:-2], refs[-2], refs[-1]
    gain = turned_ref[gain_row : gain_row + 1]
    normed_grad = side_ref[...] + combined(
        plan_ref[2 * mixture + 1 : 2 * mixture + 2], blocks
    )
    _, unit, inverse = norm_forward(values_ref[...], gain)
    back, gain_grad_ref[...] = norm_backward(normed_grad, unit, inverse, gain)
    out_ref[...] = grad_ref[...] + back


def combine_backward(mixture, gain_row, plan, grad, side, values, turned, blocks):
    return whole_call(
        functools.partial(combine_backward_kernel, mixture, gain_row),
        [shaped(grad.shape, jnp.float32), shaped((1, D), jnp.float32)],
        [],
        [plan, grad, side, values, turned, *blocks],
        500_000_000,
    )


def pack_grads_kernel(
    owners, grad_ref, features_ref, router_one_ref, router_two_ref, taps_ref, attend_ref, *refs
):
    gain_refs, out_ref, turn_ref = refs[:-2], refs[-2], refs[-1]
    bands, taps = features_ref.shape[0], taps_ref.shape[0]
    turn_ref[...] = jnp.zeros(turn_ref.shape, jnp.float32)
    turn_ref[2 * owners : 2 * owners + taps] = taps_ref[...]
    for number, gain_ref in enumerate(gain_refs):
        at = 2 * owners + taps + number
        turn_ref[at : at + 1] = gain_ref[...]
    out_ref[:, :LANES] = jnp.zeros((D, LANES), jnp.bfloat16)
    out_ref[:, :bands] = to_low(
        lax.dot_general(
            to_low(grad_ref[...]),
            features_ref[...],
            (((0,), (1,)), ((), ())),
            preferred_element_type=jnp.float32,
        )
    )
    out_ref[:, LANES : 2 * LANES] = to_low(
        turn_ref[...].T + router_one_ref[...] + router_two_ref[...]
    )
    out_ref[:, 2 * LANES :] = attend_ref[...]


def pack_grads(grad, features_turned, router_one, router_two, taps_grad, attend_grad, gain_grads):
    return whole_call(
        functools.partial(pack_grads_kernel, lax.axis_size("dp")),
        [shaped((D, 2 * LANES + attend_grad.shape[1]), jnp.bfloat16)],
        [],
        [grad, features_turned, router_one, router_two, taps_grad, attend_grad, *gain_grads],
        60_000_000,
        [pltpu.VMEM((LANES, D), jnp.float32)],
    )[0]


def shares_kernel(
    place_ref, length_ref, moved_ref, early_ref, square_ref, loss_ref, share_ref, out_ref
):
    share = jnp.zeros(share_ref.shape, jnp.float32)
    for owner in range(moved_ref.shape[0]):
        share = share + moved_ref[owner].astype(jnp.float32)
    share_ref[...] = share
    leading = place_ref[0] == 0
    small = share[:, : 2 * LANES]
    rest = share[:, 2 * LANES :]
    square = (
        jnp.where(leading, jnp.sum(small * small), 0.0)
        + jnp.sum(rest * rest)
        + jnp.sum(early_ref[...] * early_ref[...])
        + jnp.sum(square_ref[...])
    )
    count = jnp.where(leading, length_ref[0], 0).astype(jnp.float32)
    lane = place_of((1, LANES), 1)
    row = jnp.where(
        lane == 0, square, jnp.where(lane == 1, count, jnp.where(lane == 2, loss_ref[...], 0.0))
    )
    for device in range(out_ref.shape[0]):
        out_ref[device] = row


def shares_step(place, length, moved, early_share, squares, loss):
    devices = lax.axis_size("dp") * lax.axis_size("hid")
    return whole_call(
        shares_kernel,
        [shaped(moved.shape[1:], jnp.float32), shaped((devices, 1, LANES), jnp.float32)],
        [place, length],
        [moved, early_share, squares, loss],
        1_000_000,
    )


def totals_of(ref):
    rows = jnp.sum(ref[...], 0)
    lane = place_of(rows.shape, 1)
    square, count, loss = (jnp.sum(jnp.where(lane == part, rows, 0.0)) for part in range(3))
    norm = jnp.sqrt(square) / count
    return count, loss, norm, jnp.minimum(1.0, clip_limit / (norm + 1e-06)) / count


def orthogonal_kernel(pieces, experts, place_ref, totals_ref, *refs):
    momentum_refs, grad_refs = refs[:pieces], refs[pieces : 2 * pieces]
    out_refs, matrix_ref = refs[2 * pieces : 3 * pieces], refs[3 * pieces]
    _, _, _, factor = totals_of(totals_ref)
    gram = jnp.zeros((D, D), jnp.float32)
    for piece in range(pieces):
        current = muon_beta * momentum_refs[piece][...] + factor * grad_refs[piece][...].astype(
            jnp.float32
        )
        matrix_ref[piece] = current
        high, low = two_parts(current)
        cross = dot_right(high, low)
        gram = gram + (dot_right(high, high) + (cross + cross.T))
    row, column = place_of((D, D), 0), place_of((D, D), 1)
    square = jnp.sum(jnp.where(row == column, gram, 0.0))
    inverse = 1.0 / (jnp.sqrt(square) + 1e-07)
    gram = gram * (inverse * inverse)
    identity = jnp.where(row == column, newton_first, 0.0)
    total = None
    for turn in range(5):
        parts = two_parts(gram)
        poly = identity + newton_second * gram + newton_third * close_dot(parts, parts)
        poly_parts = two_parts(poly)
        total = poly if total is None else close_dot(poly_parts, two_parts(total))
        if turn < 4:
            gram = close_dot(poly_parts, two_parts(close_dot(poly_parts, parts)))
    kind_scale = jnp.where(
        place_ref[0] % 2 == 0,
        D ** (-0.5) * muon_rate * FF**0.5,
        3 * experts * FF ** (-0.5) * muon_rate * FF**0.5,
    )
    total_parts = two_parts(total * (inverse * kind_scale))
    for piece in range(pieces):
        out_refs[piece][...] = to_low(close_dot(total_parts, two_parts(matrix_ref[piece])))


def orthogonal(place, totals, momentum, grads):
    pieces = len(momentum)
    return whole_call(
        functools.partial(orthogonal_kernel, pieces, lax.axis_size("dp")),
        [shaped((D, D), jnp.bfloat16)] * pieces,
        [place],
        [totals, *momentum, *grads],
        19_000_000_000,
        [pltpu.VMEM((pieces, D, D), jnp.float32)],
    )


def momentum_kernel(totals_ref, momentum_ref, one_ref, two_ref, out_ref):
    _, _, _, factor = totals_of(totals_ref)
    first = pl.program_id(0) < 2
    grad = jnp.where(first, one_ref[0], two_ref[0])
    out_ref[0] = muon_beta * momentum_ref[0] + factor * grad


def momentum_update(totals, momentum, grads_one, grads_two):
    block = (1,) + momentum.shape[1:]
    return pl.pallas_call(
        momentum_kernel,
        grid=(4,),
        out_shape=shaped(momentum.shape, jnp.float32),
        in_specs=[
            pl.BlockSpec(totals.shape, lambda step: (0, 0, 0)),
            pl.BlockSpec(block, lambda step: (step, 0, 0)),
            pl.BlockSpec(block, lambda step: (jnp.minimum(step, 1), 0, 0)),
            pl.BlockSpec(block, lambda step: (jnp.maximum(step - 2, 0), 0, 0)),
        ],
        out_specs=pl.BlockSpec(block, lambda step: (step, 0, 0)),
        compiler_params=pltpu.CompilerParams(vmem_limit_bytes=32 * 1024 * 1024),
        cost_estimate=pl.CostEstimate(
            flops=3_000_000, bytes_accessed=12_000_000, transcendentals=0
        ),
    )(totals, momentum, grads_one, grads_two)


def update_kernel(place_ref, weight_ref, *refs):
    out_ref, turn = refs[-1], pl.program_id(0)
    for step, update_ref in enumerate(refs[:-1]):

        @pl.when(turn == step)
        def _():
            out_ref[0] = (1.0 - muon_decay) * weight_ref[0] - update_ref[...].astype(jnp.float32)


def expert_update(place, weights, updates):
    count = weights.shape[0]

    def turned(step, place_ref):
        return ((place_ref[0] + step) % count, 0, 0)

    block = (1,) + weights.shape[1:]
    return pl.pallas_call(
        update_kernel,
        out_shape=jax.ShapeDtypeStruct(weights.shape, jnp.float32),
        grid_spec=pltpu.PrefetchScalarGridSpec(
            num_scalar_prefetch=1,
            grid=(count,),
            in_specs=[pl.BlockSpec(block, turned)]
            + [pl.BlockSpec(update.shape, lambda step, place_ref: (0, 0)) for update in updates],
            out_specs=pl.BlockSpec(block, turned),
        ),
        compiler_params=pltpu.CompilerParams(vmem_limit_bytes=32 * 1024 * 1024),
        cost_estimate=pl.CostEstimate(
            flops=3_000_000, bytes_accessed=10_000_000, transcendentals=0
        ),
    )(place, weights, *updates)


def adam_update(weight, grad, first, second, rate, decay):
    first_new = beta_one * first + (1.0 - beta_one) * grad
    second_new = beta_two * second + (1.0 - beta_two) * grad * grad
    corrected = (
        first_new
        / (1.0 - beta_one**STEP)
        / (jnp.sqrt(second_new / (1.0 - beta_two**STEP)) + adam_epsilon)
    )
    return (first_new, second_new, weight - rate * (corrected + decay * weight))


def adam_kernel(owners, splits, place_ref, totals_ref, share_ref, senone_ref, *refs):
    blocks, states = refs[:splits], refs[splits : splits + 24]
    outs, scalars_ref = refs[splits + 24 : splits + 48], refs[splits + 48]
    turn_ref, gather_ref = refs[splits + 49 :]
    count, loss, norm, factor = totals_of(totals_ref)
    lane = place_of((1, LANES), 1)
    scalars_ref[...] = jnp.where(
        lane == 0, loss, jnp.where(lane == 1, count, jnp.where(lane == 2, norm, 0.0))
    )
    width = blocks[0].shape[1] // 7
    for step, block in enumerate(blocks):
        begin = pl.multiple_of((place_ref[0] + splits - step) % splits * width, width)
        for part in range(7):
            gather_ref[part, :, pl.ds(begin, width)] = block[:, part * width : (part + 1) * width]
    own = share_ref.shape[0]
    bands = states[0].shape[1]
    taps, gains = states[4].shape[0], states[7].shape[0]
    turn_ref[...] = jnp.zeros(turn_ref.shape, jnp.float32)
    turn_ref[:own] = share_ref[:, LANES : 2 * LANES]
    turned = turn_ref[...].T
    begin = 2 * owners

    def apply(number, at, grad, rate=adam_rate, decay=weight_decay):
        first, second, weight = (states[number + 8 * part] for part in (1, 2, 0))
        found = adam_update(weight[at], grad * factor, first[at], second[at], rate, decay)
        for ref, value in zip(outs[3 * number : 3 * number + 3], found):
            ref[at] = value

    everything = (slice(None), slice(None))
    apply(0, everything, share_ref[:, :bands])
    for part in range(3):
        apply(1, (slice(None), slice(part * D, (part + 1) * D)), gather_ref[part])
    for part in range(2):
        apply(2, (part,), gather_ref[3 + part])
        apply(3, (slice(None), slice(part * D, (part + 1) * D)), gather_ref[5 + part])
        apply(
            5,
            (part,),
            share_ref[:, LANES + part * owners : LANES + (part + 1) * owners],
        )
    apply(4, everything, turned[begin : begin + taps, :own])
    apply(6, everything, senone_ref[...])
    apply(7, everything, turned[begin + taps : begin + taps + gains, :own], gain_rate, 0.0)


def adam_step(place, totals, share, senone_share, blocks, weights, firsts, seconds):
    rows, splits = share.shape[0], len(blocks)
    outs = [shaped(part.shape, jnp.float32) for part in weights for _ in range(3)]
    return whole_call(
        functools.partial(adam_kernel, lax.axis_size("dp"), splits),
        outs + [shaped((1, LANES), jnp.float32)],
        [place],
        [totals, share, senone_share, *blocks, *weights, *firsts, *seconds],
        4_000_000,
        [
            pltpu.VMEM((LANES, LANES), jnp.float32),
            pltpu.VMEM((7, rows, D), jnp.float32),
        ],
    )


def convolution_forward(values, gains, weight_in, depth, weight_out, valid):
    tokens = values.shape[0]
    normed, unit, inverse = norm_forward(values, gains[2])
    low_normed = to_low(normed)
    linear = dot_low(low_normed, weight_in[0])
    gating = jax.nn.sigmoid(dot_low(low_normed, weight_in[1]))
    mixed = linear * gating * valid[:, None]
    reach = (depth.shape[0] - 1) // 2
    padded = jnp.pad(mixed, ((reach, reach), (0, 0)))
    deep = jnp.zeros_like(mixed)
    for offset in range(depth.shape[0]):
        deep = deep + depth[offset] * padded[offset : offset + tokens]
    count = jnp.sum(valid)
    mask = valid[:, None]
    mean = jnp.sum(mask * deep, 0) / count
    spread = jnp.sum(mask * deep * deep, 0) / count - mean * mean
    scale = lax.rsqrt(spread + 1e-05)
    unit_batch = (deep - mean) * scale
    shifted = unit_batch * gains[5] + gains[6]
    activated = to_low(jax.nn.silu(shifted))
    kept = (
        unit,
        inverse,
        low_normed,
        linear,
        gating,
        padded,
        scale,
        unit_batch,
        shifted,
        activated,
    )
    return (values + dot_low(activated, weight_out), kept)


def convolution_backward(grad, gains, weight_in, depth, weight_out, valid, kept):
    unit, inverse, low_normed, linear, gating, padded, scale, unit_batch, shifted, activated = kept
    tokens = grad.shape[0]
    low_grad = to_low(grad)
    out_grad = dot_left(activated, own_part(low_grad, 1))
    shifted_grad = dot_right(low_grad, weight_out) * silu_slope(shifted)
    gamma_grad = jnp.sum(shifted_grad * unit_batch, 0)
    beta_grad = jnp.sum(shifted_grad, 0)
    unit_grad = shifted_grad * gains[5]
    count = jnp.sum(valid)
    mask = valid[:, None]
    first_sum = jnp.sum(mask * unit_grad, 0) / count
    second_sum = jnp.sum(mask * unit_grad * unit_batch, 0) / count
    deep_grad = scale * (unit_grad - mask * (first_sum + unit_batch * second_sum))
    reach = (depth.shape[0] - 1) // 2
    padded_grad = jnp.pad(deep_grad, ((reach, reach), (0, 0)))
    mixed_grad = jnp.zeros_like(deep_grad)
    depth_rows = []
    for offset in range(depth.shape[0]):
        begin = 2 * reach - offset
        mixed_grad = mixed_grad + depth[offset] * padded_grad[begin : begin + tokens]
        depth_rows.append(jnp.sum(deep_grad * padded[offset : offset + tokens], 0))
    mixed_grad = mixed_grad * mask
    project_grad = [
        to_low(mixed_grad * gating),
        to_low(mixed_grad * linear * gating * (1.0 - gating)),
    ]
    in_grad = [dot_left(low_normed, own_part(part, 1)) for part in project_grad]
    normed_grad = sum(dot_right(part, weight_in[place]) for place, part in enumerate(project_grad))
    values_grad, gain_grad = norm_backward(normed_grad, unit, inverse, gains[2])
    return (
        grad + values_grad,
        gain_grad,
        gamma_grad[None],
        beta_grad[None],
        in_grad,
        jnp.stack(depth_rows),
        out_grad,
    )


def on_device(
    features,
    lengths,
    routes,
    alignments,
    input_weight,
    attention_in,
    branch_out,
    pointwise_in,
    depthwise,
    router,
    senone_table,
    norm_scales,
    expert_weights,
    input_first,
    input_second,
    attention_first,
    attention_second,
    branch_first,
    branch_second,
    pointwise_first,
    pointwise_second,
    depthwise_first,
    depthwise_second,
    router_first,
    router_second,
    senone_first,
    senone_second,
    scales_first,
    scales_second,
    expert_momentum,
):
    owners, splits = lax.axis_size("dp"), lax.axis_size("hid")
    tokens = features.shape[0]
    taps, gains = depthwise.shape[0], norm_scales.shape[0]
    place = lax.axis_index("hid")
    place_array = place[None].astype(jnp.int32)
    gain_begin = 2 * owners + taps
    share = 3 * tokens // (2 * owners) // splits
    wide = -(-share // 8) * 8
    slots, wide_rows = (share, wide), owners * wide

    small = pack_small(input_weight.T, router, depthwise, norm_scales)
    near = to_low(expert_weights[0, :, 0])
    before, behind = shift(near, 1), shift(near, -1)
    small = after(
        exchange_rows(small.reshape(owners * small.shape[1], -1)), before, behind
    )
    weights_one = [near, before, behind, shift(before[0], 1), shift(behind[1], -1)]
    dense = pack_dense(
        attention_in, branch_out, pointwise_in, gather_near(to_low(senone_table))
    )
    dense = lax.all_gather(dense, "dp", axis=1, tiled=True)
    low_two = to_low(expert_weights[1, :, 0])
    momentum_pieces = expert_momentum.reshape((2 * 2,) + expert_momentum.shape[3:])
    valid = (jnp.arange(tokens, dtype=jnp.int32) < lengths[0]).astype(jnp.float32)
    plan = plan_slots(place_array, routes[:, :, 0], share, wide)
    targets = alignments[:, None]
    features_turned = features.T

    start, turned, rows, gate_one, chances_one = start_step(
        small, features_turned, plan, routes, gain_begin, wide_rows
    )
    depth_full = turned[2 * owners : gain_begin]
    scales_full = turned[gain_begin : gain_begin + gains]
    weights_two = [lax.all_gather(after(low_two, rows), "hid", axis=0, tiled=False)]
    forward_one, returned = expert_forward(place_array, exchange_rows(rows), weights_one, slots)
    blocks = gather_slots(exchange_rows(returned), slots)
    expert_out_one, first = combine_step(0, plan, gate_one, start, blocks)

    second, *kept_attend = attention_forward(lengths, first, turned, dense, gain_begin + 1)
    third, kept_convolve = convolution_forward(
        second, scales_full, dense[5:7], depth_full, dense[4], valid
    )

    rows, gate_two, chances_two = dispatch_step(
        1, third, small, turned, plan, routes, gain_begin + 3, wide_rows
    )
    kept_rows_one = forward_one[0]
    forward_one = spread(forward_one, rows)
    forward_two, returned = expert_forward(place_array, exchange_rows(rows), weights_two, slots)
    blocks = gather_slots(after(exchange_rows(returned), *forward_one), slots)
    expert_out_two, fourth = combine_step(1, plan, gate_two, third, blocks)
    kept_rows_two = forward_two[0]

    low_normed, loss_local, sent, *logit_grad = senone_step(
        lengths, place_array, fourth, turned, targets, dense, gain_begin + 4
    )
    blocks = gather_near(sent)
    grad, gain_five, rows = assemble_step(1, place_array, plan, gate_two, blocks, wide_rows)
    logit_grad = spread(logit_grad, grad)
    forward_two = spread(forward_two, grad)

    rows_grad = after(exchange_rows(rows), *logit_grad)
    backward_two, returned = expert_backward(
        place_array, kept_rows_two, rows_grad, weights_two, slots
    )
    side, router_two = gate_backward(
        1,
        gain_begin + 3,
        grad,
        expert_out_two,
        gate_two,
        chances_two,
        routes,
        third,
        small,
        turned,
    )
    blocks = gather_slots(after(exchange_rows(returned), *forward_two), slots)
    grad, gain_four = combine_backward(
        1, gain_begin + 3, plan, grad, side, third, turned, blocks
    )
    backward_two = spread(backward_two, grad)
    ready = after(momentum_pieces, grad)
    owned_momentum = [ready[place]] + [
        shift(ready[(place + step) % splits], step) for step in range(1, splits)
    ]

    grad, gain_three, gamma_grad, beta_grad, pointwise_grad, depth_grad, conv_out_grad = (
        convolution_backward(
            grad, scales_full, dense[5:7], depth_full, dense[4], valid, kept_convolve
        )
    )
    early = pack_early(place_array, low_normed, logit_grad, [conv_out_grad] + pointwise_grad)
    grad = after(grad, *backward_two)
    experts_two = expert_grads(forward_two, backward_two)
    grad, gain_two, attend_grad = attention_backward(
        lengths, place_array, grad, first, turned, dense, kept_attend, gain_begin + 1
    )

    grad = after(grad, owned_momentum[1])
    rows_grad = exchange_rows(send_back_step(0, plan, gate_one, grad, wide_rows))
    rows_grad = after(rows_grad, owned_momentum[3])
    backward_one, returned = expert_backward(
        place_array, kept_rows_one, rows_grad, weights_one, slots
    )
    side, router_one = gate_backward(
        0, gain_begin, grad, expert_out_one, gate_one, chances_one, routes, start, small, turned
    )
    returned = after(exchange_rows(returned), owned_momentum[2])
    early_moved = exchange_rows(after(early, returned))
    blocks = gather_slots(returned, slots)
    grad, gain_one = combine_backward(0, gain_begin, plan, grad, side, start, turned, blocks)
    last = pack_grads(
        grad,
        features_turned,
        router_one,
        router_two,
        depth_grad,
        attend_grad,
        [gain_one, gain_two, gain_three, gain_four, gain_five, gamma_grad, beta_grad],
    )
    received = spread(backward_one, *blocks)
    experts_one, squares, sent = last_expert_grads(
        place_array, forward_one, after(tuple(received), last), experts_two
    )
    owned_grad = spread(sent)
    moved = exchange_rows(last)
    early_share = jnp.sum(
        early_moved.reshape(owners, D // owners, -1).astype(jnp.float32), 0
    )
    width = senone_table.shape[1]
    senone_share, conv_share = early_share[:, :width], early_share[:, width:]
    last_share, totals = shares_step(
        place_array,
        lengths,
        moved.reshape(owners, D // owners, -1),
        early_share,
        squares,
        loss_local,
    )
    blocks = gather_near(jnp.concatenate([last_share[:, 2 * LANES :], conv_share], 1))
    totals = lax.all_to_all(totals, ("dp", "hid"), split_axis=0, concat_axis=0, tiled=True)
    totals = after(totals, *blocks)

    orth = orthogonal(place_array, totals, owned_momentum, owned_grad)
    returned = [orth[0]] + [shift(orth[step], -step) for step in range(1, splits)]
    momentum_new = momentum_update(totals, momentum_pieces, experts_one, experts_two)
    *updated, scalars = adam_step(
        place_array,
        totals,
        last_share,
        senone_share,
        blocks,
        [
            input_weight.T,
            attention_in,
            branch_out,
            pointwise_in,
            depthwise,
            router,
            senone_table,
            norm_scales,
        ],
        [
            input_first.T,
            attention_first,
            branch_first,
            pointwise_first,
            depthwise_first,
            router_first,
            senone_first,
            scales_first,
        ],
        [
            input_second.T,
            attention_second,
            branch_second,
            pointwise_second,
            depthwise_second,
            router_second,
            senone_second,
            scales_second,
        ],
    )
    experts_new = expert_update(
        place_array, expert_weights.reshape(momentum_pieces.shape), returned
    )
    return (
        scalars[0, 0],
        scalars[0, 1],
        scalars[0, 2],
        *[part.T for part in updated[:3]],
        *updated[3:],
        momentum_new.reshape(expert_momentum.shape),
        experts_new.reshape(expert_weights.shape),
    )


def solution(mesh):
    return jax.shard_map(
        on_device,
        mesh=mesh,
        in_specs=(
            P("dp", None),
            P("dp"),
            P(None, "dp", None),
            P("dp"),
            P(None, "dp"),
            P("dp", None),
            P(None, "dp", None),
            P("dp", None),
            P(None, "dp"),
            P(None, "dp", None),
            P("dp", "hid"),
            P(None, "dp"),
            P(None, None, "dp", None, "hid"),
            P(None, "dp"),
            P(None, "dp"),
            P("dp", None),
            P("dp", None),
            P(None, "dp", None),
            P(None, "dp", None),
            P("dp", None),
            P("dp", None),
            P(None, "dp"),
            P(None, "dp"),
            P(None, "dp", None),
            P(None, "dp", None),
            P("dp", "hid"),
            P("dp", "hid"),
            P(None, "dp"),
            P(None, "dp"),
            P(None, None, "dp", None, "hid"),
        ),
        out_specs=(
            P(),
            P(),
            P(),
            P(None, "dp"),
            P(None, "dp"),
            P(None, "dp"),
            P("dp", None),
            P("dp", None),
            P("dp", None),
            P(None, "dp", None),
            P(None, "dp", None),
            P(None, "dp", None),
            P("dp", None),
            P("dp", None),
            P("dp", None),
            P(None, "dp"),
            P(None, "dp"),
            P(None, "dp"),
            P(None, "dp", None),
            P(None, "dp", None),
            P(None, "dp", None),
            P("dp", "hid"),
            P("dp", "hid"),
            P("dp", "hid"),
            P(None, "dp"),
            P(None, "dp"),
            P(None, "dp"),
            P(None, None, "dp", None, "hid"),
            P(None, None, "dp", None, "hid"),
        ),
        check_vma=False,
    )
```

time: 687 us -> 535 us (0.78)
  matrix products: 121 us -> 17.6 us
  Pallas kernels: 23.1 us -> 113 us
  other arithmetic: 77.5 us -> 16.5 us
  local copies, waits for them, and re-layouts: 107 us -> 62.2 us
  starting transfers between devices: 178 us -> 140 us
  blocking collectives: 0 us -> 19.5 us
  between operations: 26.3 us -> 17.5 us
    pallas_call x1 -> x33, Pallas kernels: 23.1 us -> 113 us  [the longest x31 107 us: whole_call(): pl.pallas_call(kernel, grid=(1,), out_shape=out_shapes, in_specs=[pl.Bloc...]
    dot_general x28 -> x3, matrix products: 43.1 us -> 6.15 us  [dot_low(): return jnp.dot(left, right, preferred_element_type=jnp.float32)]
    dot_general x14 -> x3, matrix products: 28.8 us -> 5.57 us  [dot_left(): lax.dot_general(left, right, (((0,), (0,)), ((), ())), preferred_element_...]
    dot_general x12 -> x0, matrix products: 21.7 us -> none  [the longest x6 10.5 us: exact_dot(): return jnp.dot(left, right, precision=lax.Precision.HIGHEST)]
    dot_general x25 -> x3, matrix products: 27.2 us -> 5.92 us  [dot_right(): lax.dot_general(left, right, (((1,), (1,)), ((), ())), preferred_element_...]
    ppermute x77 -> x49, waiting for transfers between devices: 106 us -> 85.1 us  [shift(): lax.ppermute(values, 'hid', [(i, (i + step) % size) for i in range(size)])]
    ppermute x77 -> x49, starting transfers between devices: 88.9 us -> 68.4 us  [shift(): lax.ppermute(values, 'hid', [(i, (i + step) % size) for i in range(size)])]
    all_to_all x0 -> x1, blocking collectives: none -> 19.5 us  [exchange_rows(): lax.all_to_all(shaped_rows, 'dp', split_axis=0, concat_axis=0, tiled=True)]
  transfers between devices with their start and end apart: 92 -> 62, of which waited for: 27 -> 26; matrix products, arithmetic and copies ran while one was open for 33% -> 6% of each run, Pallas kernels for 0% -> 13%
where the time goes in v2:
time: 535 us; the launch traced here: 525 us
  starting transfers between devices  140 us (26%)
  waiting for transfers between devices  139 us (26%)
  Pallas kernels  113 us (21%)
  local copies, waits for them, and re-layouts  62.2 us (12%)
  blocking collectives  19.5 us (4%)
  matrix products  17.6 us (3%)
  between operations  17.5 us (3%)
  other arithmetic  16.5 us (3%)
    pallas_call x31, Pallas kernels, whole_call(): pl.pallas_call(kernel, grid=(1,), out_shape=out_shapes, in_specs=[pl.Bloc...  107 us
    ppermute x49, waiting for transfers between devices, shift(): lax.ppermute(values, 'hid', [(i, (i + step) % size) for i in range(size)])  85.1 us
    ppermute x49, starting transfers between devices, shift(): lax.ppermute(values, 'hid', [(i, (i + step) % size) for i in range(size)])  68.4 us
    all_to_all x10, starting transfers between devices, exchange_rows(): lax.all_to_all(shaped_rows, 'dp', split_axis=0, concat_axis=0, tiled=True)  62 us
    unnamed x386, local copies, waits for them, and re-layouts  53.9 us
    all_to_all x10, waiting for transfers between devices, exchange_rows(): lax.all_to_all(shaped_rows, 'dp', split_axis=0, concat_axis=0, tiled=True)  53.3 us
    all_to_all x1, blocking collectives, exchange_rows(): lax.all_to_all(shaped_rows, 'dp', split_axis=0, concat_axis=0, tiled=True)  19.5 us
  transfers between devices with their start and end apart: 62, of which 26 were waited for; matrix products, arithmetic and copies ran while one was open for 6% of the time, Pallas kernels for 13%

profile of v2, /device:TPU:1, one launch (start us, length us, event | category | flops | bytes accessed | tf_op | source)
XLA Modules:
  0.0 525.1 jit_solution(5556493034996142579)
XLA Ops:
  10.2 2.6 collective-permute-start.8
  19.2 2.5 bitcast_convert_fusion
  22.9 2.7 collective-permute-start.1
  26.6 10.6 %all-to-all-start = ((f32[32,16,256]{2,1,0:T(8,128)}), f32[32,16,256]{2,1,0:T(8,128)S(1)}, u32[]{:S(2)}, u32[]{:S(2)}) async-start(f32[32,16,256]{2,1,0:T(8,128)} %shard_map.510), calls=%async_computation | async-start | bytes 1048576 | tf_op jit(solution)/shard_map/all_to_all | solution.py:60
  37.8 12.1 %all-to-all-done = f32[32,16,256]{2,1,0:T(8,128)S(1)} async-done(((f32[32,16,256]{2,1,0:T(8,128)}), f32[32,16,256]{2,1,0:T(8,128)S(1)}, u32[]{:S(2)}, u32[]{:S(2)}) %all-to-all-start) | async-done | bytes 524320 | tf_op jit(solution)/shard_map/all_to_all | solution.py:60
  57.8 2.7 collective-permute-start.3
  60.5 19.5 %all_to_all.60 = bf16[32,8,512]{2,1,0:T(8,128)(2,1)S(1)} all-to-all(bf16[32,8,512]{2,1,0:T(8,128)(2,1)S(1)} %bitcast.140), channel_id=1, replica_groups=mesh['dp'=32,'hid'=4] {'dp'}, dimensions={0} | all-to-all | bytes 524288 | tf_op jit(solution)/shard_map/all_to_all | solution.py:60
  80.1 3.4 shard_map.512
  87.2 4.3 all-to-all-start.2
  92.8 7.8 %all-to-all-done.2 = bf16[32,8,512]{2,1,0:T(8,128)(2,1)S(1)} async-done(((bf16[32,8,512]{2,1,0:T(8,128)(2,1)}), bf16[32,8,512]{2,1,0:T(8,128)(2,1)S(1)}, u32[]{:S(2)}, u32[]{:S(2)}) %all-to-all-start.2) | async-done | bytes 262176 | tf_op jit(solution)/shard_map/all_to_all | solution.py:60
  104.4 9.1 %collective-permute-done.4.refs_1_ = bf16[192,512]{1,0:T(8,128)(2,1)S(1)} collective-permute-done((bf16[192,512]{1,0:T(8,128)(2,1)S(1)}, bf16[192,512]{1,0:T(8,128)(2,1)S(1)}, u32[]{:S(2)}, u32[]{:S(2)}) %collective-permute-start.4) | collective-permute-done | bytes 196640 | tf_op jit(solution)/shard_map/ppermute | solution.py:35
  113.5 7.0 %collective-permute-done.5.refs_2_ = bf16[192,512]{1,0:T(8,128)(2,1)S(1)} collective-permute-done((bf16[192,512]{1,0:T(8,128)(2,1)S(1)}, bf16[192,512]{1,0:T(8,128)(2,1)S(1)}, u32[]{:S(2)}, u32[]{:S(2)}) %collective-permute-start.5) | collective-permute-done | bytes 196640 | tf_op jit(solution)/shard_map/ppermute | solution.py:35
  124.6 7.3 %shard_map.516 = (f32[512,512]{1,0:T(8,128)S(1)}, bf16[3,512,512]{2,1,0:T(8,128)(2,1)S(1)}, f32[512,128]{1,0:T(8,128)S(1)}, bf16[512,512]{1,0:T(8,128)(2,1)S(1)}) custom-call(s32[1]{0:T(128)} %copy.93.length_ref, f32[512,512]{1,0:T(8,128)S(1)} %get-tuple-element.168.values_ref, f32[128,512]{1,0:T(8,128)S(1)} %get-tuple-element.169.turned_ref, ...), custom_call_target="tpu_custom_call" | custom-call | flops 4000000000 | bytes 20447232 | tf_op jit(solution)/shard_map/pallas_call | solution.py:144
  137.8 2.9 multiply_multiply_fusion.1
  140.8 2.4 multiply_reduce_fusion
  150.8 5.4 %all-to-all-start.3 = ((bf16[32,8,512]{2,1,0:T(8,128)(2,1)}), bf16[32,8,512]{2,1,0:T(8,128)(2,1)}, u32[]{:S(2)}, u32[]{:S(2)}) async-start(bf16[32,8,512]{2,1,0:T(8,128)(2,1)} %bitcast.141), calls=%async_computation.3 | async-start | bytes 524288 | tf_op jit(solution)/shard_map/all_to_all | solution.py:60
  156.8 2.6 collective-permute-start.12
  159.4 5.9 %all-to-all-done.3 = bf16[32,8,512]{2,1,0:T(8,128)(2,1)} async-done(((bf16[32,8,512]{2,1,0:T(8,128)(2,1)}), bf16[32,8,512]{2,1,0:T(8,128)(2,1)}, u32[]{:S(2)}, u32[]{:S(2)}) %all-to-all-start.3) | async-done | bytes 262176 | tf_op jit(solution)/shard_map/all_to_all | solution.py:60
  165.3 4.1 shard_map.518
  173.1 4.4 all-to-all-start.4
  177.5 9.0 %all-to-all-done.4 = bf16[32,8,512]{2,1,0:T(8,128)(2,1)} async-done(((bf16[32,8,512]{2,1,0:T(8,128)(2,1)}), bf16[32,8,512]{2,1,0:T(8,128)(2,1)}, u32[]{:S(2)}, u32[]{:S(2)}) %all-to-all-start.4) | async-done | bytes 262176 | tf_op jit(solution)/shard_map/all_to_all | solution.py:60
  188.8 2.3 collective-permute-start.15
  192.0 8.5 %collective-permute-done.13.refs_1_ = bf16[192,512]{1,0:T(8,128)(2,1)} collective-permute-done((bf16[192,512]{1,0:T(8,128)(2,1)}, bf16[192,512]{1,0:T(8,128)(2,1)}, u32[]{:S(2)}, u32[]{:S(2)}) %collective-permute-start.13) | collective-permute-done | bytes 196640 | tf_op jit(solution)/shard_map/ppermute | solution.py:35
  203.7 6.1 %shard_map.521 = (bf16[512,512]{1,0:T(8,128)(2,1)S(1)}, f32[1,1]{1,0:T(1,128)}, bf16[144,512]{1,0:T(8,128)(2,1)S(1)}, bf16[128,1024]{1,0:T(8,128)(2,1)S(1)}, bf1...) custom-call(s32[1]{0:T(128)} %copy.93.length_ref, s32[1]{0:T(128)} %bitcast.place_ref, ...), custom_call_target="tpu_custom_call" | custom-call | flops 1100000000 | bytes 65947652 | tf_op jit(solution)/shard_map/pallas_call | solution.py:144
  210.8 3.0 collective-permute-start.17
  215.1 4.9 collective-permute-done.17.refs_2_
  221.7 3.1 collective-permute-start.20
  224.9 5.8 %all-to-all-start.5 = ((bf16[32,8,512]{2,1,0:T(8,128)(2,1)}), bf16[32,8,512]{2,1,0:T(8,128)(2,1)}, u32[]{:S(2)}, u32[]{:S(2)}) async-start(bf16[32,8,512]{2,1,0:T(8,128)(2,1)} %bitcast.138), calls=%async_computation.5 | async-start | bytes 524288 | tf_op jit(solution)/shard_map/all_to_all | solution.py:60
  235.1 4.7 all-to-all-done.5
  240.7 4.4 shard_map.524
  248.9 4.6 all-to-all-start.6
  253.5 9.0 %all-to-all-done.6 = bf16[32,8,512]{2,1,0:T(8,128)(2,1)} async-done(((bf16[32,8,512]{2,1,0:T(8,128)(2,1)}), bf16[32,8,512]{2,1,0:T(8,128)(2,1)}, u32[]{:S(2)}, u32[]{:S(2)}) %all-to-all-start.6) | async-done | bytes 262176 | tf_op jit(solution)/shard_map/all_to_all | solution.py:60
  264.4 6.1 %collective-permute-start.25 = (bf16[192,512]{1,0:T(8,128)(2,1)}, bf16[192,512]{1,0:T(8,128)(2,1)}, u32[]{:S(2)}, u32[]{:S(2)}) collective-permute-start(bf16[192,512]{1,0:T(8,128)(2,1)} %shard_map.525.refs_0_), channel_id=1, source_target_pairs={{0,1},{1,2},{2,3},{3,0},{4,5},{5,6},{6,7},{7,4},{8,9},{9,10},{10,1... | collective-permute-start | bytes 589832 | tf_op jit(solution)/shard_map/ppermute | solution.py:35
  270.4 2.4 collective-permute-start.27
  276.0 3.6 shard_map.523
  280.3 2.5 shard_map.526
  286.0 3.3 multiply_reduce_fusion.3
  289.4 2.3 multiply_convert_fusion.1
  296.0 2.5 collective-permute-start.28
  303.0 3.1 collective-permute-start.32
  309.5 7.5 %collective-permute-done.29.refs_6_ = bf16[384,512]{1,0:T(8,128)(2,1)S(1)} collective-permute-done((bf16[384,512]{1,0:T(8,128)(2,1)S(1)}, bf16[384,512]{1,0:T(8,128)(2,1)S(1)}, u32[]{:S(2)}, u32[]{:S(2)}) %collective-permute-start.29) | collective-permute-done | bytes 393248 | tf_op jit(solution)/shard_map/ppermute | solution.py:35
  317.7 11.7 %shard_map.527 = (f32[512,512]{1,0:T(8,128)S(1)}, f32[1,512]{1,0:T(1,128)S(1)}, bf16[512,512]{1,0:T(8,128)(2,1)S(1)}) custom-call(s32[1]{0:T(128)} %copy.93.length_ref, s32[1]{0:T(128)} %bitcast.place_ref, f32[512,512]{1,0:T(8,128)S(1)} %multiply_add_fusion.grad_ref, f32[512,512]{1,0:T(8,128)S(1)} %copy-done.27, ...), custom_call_target="tpu_custom_call" | custom-call | flops 8999999488 | bytes 22022144 | tf_op jit(solution)/shard_map/pallas_call | solution.py:144
  329.5 8.5 %collective-permute-done.31.refs_1_ = f32[512,512]{1,0:T(8,128)S(1)} collective-permute-done((f32[512,512]{1,0:T(8,128)S(1)}, f32[512,512]{1,0:T(8,128)S(1)}, u32[]{:S(2)}, u32[]{:S(2)}) %collective-permute-start.31) | collective-permute-done | bytes 1048608 | tf_op jit(solution)/shard_map/ppermute | solution.py:35
  339.7 6.6 %all-to-all-start.7 = ((bf16[32,8,512]{2,1,0:T(8,128)(2,1)}), bf16[32,8,512]{2,1,0:T(8,128)(2,1)}, u32[]{:S(2)}, u32[]{:S(2)}) async-start(bf16[32,8,512]{2,1,0:T(8,128)(2,1)} %bitcast.137), calls=%async_computation.7 | async-start | bytes 524288 | tf_op jit(solution)/shard_map/all_to_all | solution.py:60
  350.5 4.7 all-to-all-done.7
  359.5 3.8 shard_map.530
  364.8 3.8 all-to-all-start.8
  373.9 3.5 shard_map.534
  377.6 7.5 %all-to-all-start.10 = ((bf16[32,16,1408]{2,1,0:T(8,128)(2,1)}), bf16[32,16,1408]{2,1,0:T(8,128)(2,1)}, u32[]{:S(2)}, u32[]{:S(2)}) async-start(bf16[32,16,1408]{2,1,0:T(8,128)(2,1)} %bitcast.72), calls=%async_computation.10 | async-start | bytes 2883584 | tf_op jit(solution)/shard_map/all_to_all | solution.py:60
  392.2 3.6 shard_map.528
  399.5 2.4 collective-permute-start.38
  406.9 9.0 %all-to-all-start.9 = ((bf16[32,16,768]{2,1,0:T(8,128)(2,1)}), bf16[32,16,768]{2,1,0:T(8,128)(2,1)S(1)}, u32[]{:S(2)}, u32[]{:S(2)}) async-start(bf16[32,16,768]{2,1,0:T(8,128)(2,1)} %bitcast.71), calls=%async_computation.9 | async-start | bytes 1572864 | tf_op jit(solution)/shard_map/all_to_all | solution.py:60
  419.9 2.6 shard_map.535.refs_8_.two_ref
  423.9 5.8 %shard_map.536 = (f32[2,512,512]{2,1,0:T(8,128)}, f32[1,512]{1,0:T(1,128)S(1)}, bf16[512,512]{1,0:T(8,128)(2,1)S(1)}, bf16[512,512]{1,0:T(8,128)(2,1)}, bf16[512...) custom-call(s32[1]{0:T(128)} %bitcast.place_ref, bf16[384,512]{1,0:T(8,128)(2,1)S(1)} %copy-done.57, ...), custom_call_target="tpu_custom_call" | custom-call | flops 805306368 | bytes 9439232 | tf_op jit(solution)/shard_map/pallas_call | solution.py:144
  437.1 9.5 %all-to-all-start.11 = ((f32[128,1,128]{2,1,0:T(1,128)}), f32[128,1,128]{2,1,0:T(1,128)S(1)}, u32[]{:S(2)}, u32[]{:S(2)}) async-start(f32[128,1,128]{2,1,0:T(1,128)} %get-tuple-element.256), calls=%async_computation.11 | async-start | bytes 131072 | tf_op jit(solution)/shard_map/all_to_all | solution.py:1350
  446.6 3.0 collective-permute-start.41
  449.5 10.1 %collective-permute-done.40.refs_1_ = f32[16,896]{1,0:T(8,128)S(1)} collective-permute-done((f32[16,896]{1,0:T(8,128)S(1)}, f32[16,896]{1,0:T(8,128)S(1)}, u32[]{:S(2)}, u32[]{:S(2)}) %collective-permute-start.40) | collective-permute-done | bytes 57376 | tf_op jit(solution)/shard_map/ppermute | solution.py:35
  459.8 3.1 collective-permute-done.42.refs_3_
  463.0 24.5 %shard_map.540 = (bf16[512,512]{1,0:T(8,128)(2,1)S(1)}, bf16[512,512]{1,0:T(8,128)(2,1)}, bf16[512,512]{1,0:T(8,128)(2,1)}, bf16[512,512]{1,0:T(8,128)(2,1)}) custom-call(s32[1]{0:T(128)} %bitcast.place_ref, f32[128,1,128]{2,1,0:T(1,128)S(1)} %all-to-all-done.11.totals_ref, f32[512,512]{1,0:T(8,128)S(1)} %copy-done.28, f32[512,512]{1,0:T(8,128)} %copy-done.191, ...), custom_call_target="tpu_custom_call" | custom-call | flops 19000000512 | bytes 8454144 | tf_op jit(solution)/shard_map/pallas_call | solution.py:144
  489.5 3.9 shard_map.539
  495.6 3.3 collective-permute-done.46.refs_1_
  498.9 2.7 collective-permute-done.47.refs_2_
  501.7 13.6 %collective-permute-done.48.refs_3_ = bf16[512,512]{1,0:T(8,128)(2,1)S(1)} collective-permute-done((bf16[512,512]{1,0:T(8,128)(2,1)}, bf16[512,512]{1,0:T(8,128)(2,1)S(1)}, u32[]{:S(2)}, u32[]{:S(2)}) %collective-permute-start.48) | collective-permute-done | bytes 524320 | tf_op jit(solution)/shard_map/ppermute | solution.py:35
  515.3 2.6 shard_map.541
  (524 shorter events, 140.3 us)
Async XLA Ops:
  7.2 117.4 %all-gather.4.cloned.1.call-start = ((), (), s32[]{:S(2)}) async-start(), calls=%async_computation.12 | async-start | bytes 8110080 | tf_op jit(solution)/shard_map/all_gather | solution.py:1229
  8.1 5.8 %collective-permute-start.7 = (bf16[16,1024]{1,0:T(8,128)(2,1)S(1)}, bf16[16,1024]{1,0:T(8,128)(2,1)S(1)}, u32[]{:S(2)}, u32[]{:S(2)}) collective-permute-start(bf16[16,1024]{1,0:T(8,128)(2,1)S(1)} %convert_element_type.39.refs_0_), channel_id=1, source_target_pairs={{0,1},{1,2},{2,3},{3,0},{4,5},{5,6},{6,7},{7,4},{8,9},{9,10},{10,1... | collective-permute-start | bytes 98312 | tf_op jit(solution)/shard_map/ppermute | solution.py:35
  10.2 4.3 collective-permute-start.8
  12.8 3.1 collective-permute-start.9
  22.9 57.1 %copy-start.9 = (bf16[2,512,512]{2,1,0:T(8,128)(2,1)}, bf16[2,512,512]{2,1,0:T(8,128)(2,1)S(1)}, u32[]{:S(2)}) copy-start(bf16[2,512,512]{2,1,0:T(8,128)(2,1)S(1)} %get-tuple-element.417.refs_0_) | copy-start | bytes 3145732
  22.9 27.0 %collective-permute-start = (bf16[2,512,512]{2,1,0:T(8,128)(2,1)S(1)}, bf16[2,512,512]{2,1,0:T(8,128)(2,1)S(1)}, u32[]{:S(2)}, u32[]{:S(2)}) collective-permute-start(bf16[2,512,512]{2,1,0:T(8,128)(2,1)S(1)} %get-tuple-element.417.refs_0_), channel_id=1, source_target_pairs={{0,1},{1,2},{2,3},{3,0},{4,5},{5,6},{6,7},{7,4},{8,9},{9,10},{10,1... | collective-permute-start | bytes 3145736 | tf_op jit(solution)/shard_map/ppermute | solution.py:35
  22.9 27.0 %collective-permute-start.1 = (bf16[2,512,512]{2,1,0:T(8,128)(2,1)S(1)}, bf16[2,512,512]{2,1,0:T(8,128)(2,1)}, u32[]{:S(2)}, u32[]{:S(2)}) collective-permute-start(bf16[2,512,512]{2,1,0:T(8,128)(2,1)S(1)} %get-tuple-element.417.refs_0_), channel_id=1, source_target_pairs={{0,3},{1,0},{2,1},{3,2},{4,7},{5,4},{6,5},{7,6},{8,11},{9,8},{10,9... | collective-permute-start | bytes 3145736 | tf_op jit(solution)/shard_map/ppermute | solution.py:35
  26.6 23.3 %all-to-all-start = ((f32[32,16,256]{2,1,0:T(8,128)}), f32[32,16,256]{2,1,0:T(8,128)S(1)}, u32[]{:S(2)}, u32[]{:S(2)}) async-start(f32[32,16,256]{2,1,0:T(8,128)} %shard_map.510), calls=%async_computation | async-start | bytes 1048576 | tf_op jit(solution)/shard_map/all_to_all | solution.py:60
  37.2 122.2 %all-gather.6.cloned.1.call-start = ((), (), s32[]{:S(2)}) async-start(), calls=%async_computation.13 | async-start | bytes 5242880 | tf_op jit(solution)/shard_map/all_gather | solution.py:1242
  55.1 66.8 %copy-start.7 = (f32[512,512]{1,0:T(8,128)}, f32[512,512]{1,0:T(8,128)S(1)}, u32[]{:S(2)}) copy-start(f32[512,512]{1,0:T(8,128)S(1)} %get-tuple-element.165.base_ref.values_ref) | copy-start | bytes 3145732
  56.6 23.4 %collective-permute-start.2 = (bf16[512,512]{1,0:T(8,128)(2,1)S(1)}, bf16[512,512]{1,0:T(8,128)(2,1)S(1)}, u32[]{:S(2)}, u32[]{:S(2)}) collective-permute-start(bf16[512,512]{1,0:T(8,128)(2,1)S(1)} %slice_bitcast_fusion.6), channel_id=1, source_target_pairs={{0,1},{1,2},{2,3},{3,0},{4,5},{5,6},{6,7},{7,4},{8,9},{9,10},{10,1... | collective-permute-start | bytes 1572872 | tf_op jit(solution)/shard_map/ppermute | solution.py:35
  57.8 22.3 %collective-permute-start.3 = (bf16[512,512]{1,0:T(8,128)(2,1)S(1)}, bf16[512,512]{1,0:T(8,128)(2,1)S(1)}, u32[]{:S(2)}, u32[]{:S(2)}) collective-permute-start(bf16[512,512]{1,0:T(8,128)(2,1)S(1)} %slice_bitcast_fusion.5), channel_id=1, source_target_pairs={{0,3},{1,0},{2,1},{3,2},{4,7},{5,4},{6,5},{7,6},{8,11},{9,8},{10,9... | collective-permute-start | bytes 1572872 | tf_op jit(solution)/shard_map/ppermute | solution.py:35
  87.2 13.3 %all-to-all-start.2 = ((bf16[32,8,512]{2,1,0:T(8,128)(2,1)}), bf16[32,8,512]{2,1,0:T(8,128)(2,1)S(1)}, u32[]{:S(2)}, u32[]{:S(2)}) async-start(bf16[32,8,512]{2,1,0:T(8,128)(2,1)} %bitcast.144), calls=%async_computation.2 | async-start | bytes 524288 | tf_op jit(solution)/shard_map/all_to_all | solution.py:60
  100.8 12.7 %collective-permute-start.4 = (bf16[192,512]{1,0:T(8,128)(2,1)S(1)}, bf16[192,512]{1,0:T(8,128)(2,1)S(1)}, u32[]{:S(2)}, u32[]{:S(2)}) collective-permute-start(bf16[192,512]{1,0:T(8,128)(2,1)S(1)} %shard_map.513.refs_0_), channel_id=1, source_target_pairs={{0,1},{1,2},{2,3},{3,0},{4,5},{5,6},{6,7},{7,4},{8,9},{9,10},{10,1... | collective-permute-start | bytes 589832 | tf_op jit(solution)/shard_map/ppermute | solution.py:35
  100.8 19.6 %collective-permute-start.5 = (bf16[192,512]{1,0:T(8,128)(2,1)S(1)}, bf16[192,512]{1,0:T(8,128)(2,1)S(1)}, u32[]{:S(2)}, u32[]{:S(2)}) collective-permute-start(bf16[192,512]{1,0:T(8,128)(2,1)S(1)} %shard_map.513.refs_0_), channel_id=1, source_target_pairs={{0,2},{1,3},{2,0},{3,1},{4,6},{5,7},{6,4},{7,5},{8,10},{9,11},{10,... | collective-permute-start | bytes 589832 | tf_op jit(solution)/shard_map/ppermute | solution.py:35
  102.6 19.3 %collective-permute-start.6 = (bf16[192,512]{1,0:T(8,128)(2,1)S(1)}, bf16[192,512]{1,0:T(8,128)(2,1)S(1)}, u32[]{:S(2)}, u32[]{:S(2)}) collective-permute-start(bf16[192,512]{1,0:T(8,128)(2,1)S(1)} %shard_map.513.refs_0_), channel_id=1, source_target_pairs={{0,3},{1,0},{2,1},{3,2},{4,7},{5,4},{6,5},{7,6},{8,11},{9,8},{10,9... | collective-permute-start | bytes 589832 | tf_op jit(solution)/shard_map/ppermute | solution.py:35
  150.8 14.5 %all-to-all-start.3 = ((bf16[32,8,512]{2,1,0:T(8,128)(2,1)}), bf16[32,8,512]{2,1,0:T(8,128)(2,1)}, u32[]{:S(2)}, u32[]{:S(2)}) async-start(bf16[32,8,512]{2,1,0:T(8,128)(2,1)} %bitcast.141), calls=%async_computation.3 | async-start | bytes 524288 | tf_op jit(solution)/shard_map/all_to_all | solution.py:60
  156.2 21.3 %collective-permute-start.10 = (bf16[384,512]{1,0:T(8,128)(2,1)}, bf16[384,512]{1,0:T(8,128)(2,1)}, u32[]{:S(2)}, u32[]{:S(2)}) collective-permute-start(bf16[384,512]{1,0:T(8,128)(2,1)} %copy-done.122), channel_id=1, source_target_pairs={{0,1},{1,2},{2,3},{3,0},{4,5},{5,6},{6,7},{7,4},{8,9},{9,10},{10,1... | collective-permute-start | bytes 1179656 | tf_op jit(solution)/shard_map/ppermute | solution.py:35
  156.3 21.2 %collective-permute-start.11 = (bf16[384,512]{1,0:T(8,128)(2,1)}, bf16[384,512]{1,0:T(8,128)(2,1)}, u32[]{:S(2)}, u32[]{:S(2)}) collective-permute-start(bf16[384,512]{1,0:T(8,128)(2,1)} %copy-done.121), channel_id=1, source_target_pairs={{0,2},{1,3},{2,0},{3,1},{4,6},{5,7},{6,4},{7,5},{8,10},{9,11},{10,... | collective-permute-start | bytes 1179656 | tf_op jit(solution)/shard_map/ppermute | solution.py:35
  156.8 20.8 %collective-permute-start.12 = (bf16[384,512]{1,0:T(8,128)(2,1)}, bf16[384,512]{1,0:T(8,128)(2,1)}, u32[]{:S(2)}, u32[]{:S(2)}) collective-permute-start(bf16[384,512]{1,0:T(8,128)(2,1)} %copy-done.120), channel_id=1, source_target_pairs={{0,3},{1,0},{2,1},{3,2},{4,7},{5,4},{6,5},{7,6},{8,11},{9,8},{10,9... | collective-permute-start | bytes 1179656 | tf_op jit(solution)/shard_map/ppermute | solution.py:35
  173.1 13.5 %all-to-all-start.4 = ((bf16[32,8,512]{2,1,0:T(8,128)(2,1)}), bf16[32,8,512]{2,1,0:T(8,128)(2,1)}, u32[]{:S(2)}, u32[]{:S(2)}) async-start(bf16[32,8,512]{2,1,0:T(8,128)(2,1)} %bitcast.143), calls=%async_computation.4 | async-start | bytes 524288 | tf_op jit(solution)/shard_map/all_to_all | solution.py:60
  188.4 12.0 %collective-permute-start.13 = (bf16[192,512]{1,0:T(8,128)(2,1)}, bf16[192,512]{1,0:T(8,128)(2,1)}, u32[]{:S(2)}, u32[]{:S(2)}) collective-permute-start(bf16[192,512]{1,0:T(8,128)(2,1)} %shard_map.519.refs_0_), channel_id=1, source_target_pairs={{0,1},{1,2},{2,3},{3,0},{4,5},{5,6},{6,7},{7,4},{8,9},{9,10},{10,1... | collective-permute-start | bytes 589832 | tf_op jit(solution)/shard_map/ppermute | solution.py:35
  188.4 12.0 %collective-permute-start.14 = (bf16[192,512]{1,0:T(8,128)(2,1)}, bf16[192,512]{1,0:T(8,128)(2,1)}, u32[]{:S(2)}, u32[]{:S(2)}) collective-permute-start(bf16[192,512]{1,0:T(8,128)(2,1)} %shard_map.519.refs_0_), channel_id=1, source_target_pairs={{0,2},{1,3},{2,0},{3,1},{4,6},{5,7},{6,4},{7,5},{8,10},{9,11},{10,... | collective-permute-start | bytes 589832 | tf_op jit(solution)/shard_map/ppermute | solution.py:35
  188.8 11.9 %collective-permute-start.15 = (bf16[192,512]{1,0:T(8,128)(2,1)}, bf16[192,512]{1,0:T(8,128)(2,1)}, u32[]{:S(2)}, u32[]{:S(2)}) collective-permute-start(bf16[192,512]{1,0:T(8,128)(2,1)} %shard_map.519.refs_0_), channel_id=1, source_target_pairs={{0,3},{1,0},{2,1},{3,2},{4,7},{5,4},{6,5},{7,6},{8,11},{9,8},{10,9... | collective-permute-start | bytes 589832 | tf_op jit(solution)/shard_map/ppermute | solution.py:35
  209.9 5.3 %collective-permute-start.16 = (bf16[144,512]{1,0:T(8,128)(2,1)S(1)}, bf16[144,512]{1,0:T(8,128)(2,1)S(1)}, u32[]{:S(2)}, u32[]{:S(2)}) collective-permute-start(bf16[144,512]{1,0:T(8,128)(2,1)S(1)} %get-tuple-element.185.refs_0_), channel_id=1, source_target_pairs={{0,1},{1,2},{2,3},{3,0},{4,5},{5,6},{6,7},{7,4},{8,9},{9,10},{10,1... | collective-permute-start | bytes 442376 | tf_op jit(solution)/shard_map/ppermute | solution.py:35
  210.8 9.2 %collective-permute-start.17 = (bf16[144,512]{1,0:T(8,128)(2,1)S(1)}, bf16[144,512]{1,0:T(8,128)(2,1)S(1)}, u32[]{:S(2)}, u32[]{:S(2)}) collective-permute-start(bf16[144,512]{1,0:T(8,128)(2,1)S(1)} %get-tuple-element.185.refs_0_), channel_id=1, source_target_pairs={{0,2},{1,3},{2,0},{3,1},{4,6},{5,7},{6,4},{7,5},{8,10},{9,11},{10,... | collective-permute-start | bytes 442376 | tf_op jit(solution)/shard_map/ppermute | solution.py:35
  213.7 6.3 %collective-permute-start.18 = (bf16[144,512]{1,0:T(8,128)(2,1)S(1)}, bf16[144,512]{1,0:T(8,128)(2,1)S(1)}, u32[]{:S(2)}, u32[]{:S(2)}) collective-permute-start(bf16[144,512]{1,0:T(8,128)(2,1)S(1)} %get-tuple-element.185.refs_0_), channel_id=1, source_target_pairs={{0,3},{1,0},{2,1},{3,2},{4,7},{5,4},{6,5},{7,6},{8,11},{9,8},{10,9... | collective-permute-start | bytes 442376 | tf_op jit(solution)/shard_map/ppermute | solution.py:35
  221.2 11.9 %collective-permute-start.19 = (bf16[128,1024]{1,0:T(8,128)(2,1)}, bf16[128,1024]{1,0:T(8,128)(2,1)}, u32[]{:S(2)}, u32[]{:S(2)}) collective-permute-start(bf16[128,1024]{1,0:T(8,128)(2,1)} %get-tuple-element.197), channel_id=1, source_target_pairs={{0,1},{1,2},{2,3},{3,0},{4,5},{5,6},{6,7},{7,4},{8,9},{9,10},{10,1... | collective-permute-start | bytes 786440 | tf_op jit(solution)/shard_map/ppermute | solution.py:35
  221.7 18.0 %collective-permute-start.20 = (bf16[128,1024]{1,0:T(8,128)(2,1)}, bf16[128,1024]{1,0:T(8,128)(2,1)}, u32[]{:S(2)}, u32[]{:S(2)}) collective-permute-start(bf16[128,1024]{1,0:T(8,128)(2,1)} %get-tuple-element.198), channel_id=1, source_target_pairs={{0,2},{1,3},{2,0},{3,1},{4,6},{5,7},{6,4},{7,5},{8,10},{9,11},{10,... | collective-permute-start | bytes 786440 | tf_op jit(solution)/shard_map/ppermute | solution.py:35
  224.9 14.9 %collective-permute-start.21 = (bf16[128,1024]{1,0:T(8,128)(2,1)}, bf16[128,1024]{1,0:T(8,128)(2,1)}, u32[]{:S(2)}, u32[]{:S(2)}) collective-permute-start(bf16[128,1024]{1,0:T(8,128)(2,1)} %get-tuple-element.199), channel_id=1, source_target_pairs={{0,3},{1,0},{2,1},{3,2},{4,7},{5,4},{6,5},{7,6},{8,11},{9,8},{10,9... | collective-permute-start | bytes 786440 | tf_op jit(solution)/shard_map/ppermute | solution.py:35
  224.9 14.9 %all-to-all-start.5 = ((bf16[32,8,512]{2,1,0:T(8,128)(2,1)}), bf16[32,8,512]{2,1,0:T(8,128)(2,1)}, u32[]{:S(2)}, u32[]{:S(2)}) async-start(bf16[32,8,512]{2,1,0:T(8,128)(2,1)} %bitcast.138), calls=%async_computation.5 | async-start | bytes 524288 | tf_op jit(solution)/shard_map/all_to_all | solution.py:60
  230.7 22.8 %collective-permute-start.22 = (bf16[384,512]{1,0:T(8,128)(2,1)}, bf16[384,512]{1,0:T(8,128)(2,1)}, u32[]{:S(2)}, u32[]{:S(2)}) collective-permute-start(bf16[384,512]{1,0:T(8,128)(2,1)} %copy-done.119), channel_id=1, source_target_pairs={{0,1},{1,2},{2,3},{3,0},{4,5},{5,6},{6,7},{7,4},{8,9},{9,10},{10,1... | collective-permute-start | bytes 1179656 | tf_op jit(solution)/shard_map/ppermute | solution.py:35
  232.5 21.0 %collective-permute-start.23 = (bf16[384,512]{1,0:T(8,128)(2,1)}, bf16[384,512]{1,0:T(8,128)(2,1)}, u32[]{:S(2)}, u32[]{:S(2)}) collective-permute-start(bf16[384,512]{1,0:T(8,128)(2,1)} %copy-done.118), channel_id=1, source_target_pairs={{0,2},{1,3},{2,0},{3,1},{4,6},{5,7},{6,4},{7,5},{8,10},{9,11},{10,... | collective-permute-start | bytes 1179656 | tf_op jit(solution)/shard_map/ppermute | solution.py:35
  233.1 20.4 %collective-permute-start.24 = (bf16[384,512]{1,0:T(8,128)(2,1)}, bf16[384,512]{1,0:T(8,128)(2,1)}, u32[]{:S(2)}, u32[]{:S(2)}) collective-permute-start(bf16[384,512]{1,0:T(8,128)(2,1)} %copy-done.117), channel_id=1, source_target_pairs={{0,3},{1,0},{2,1},{3,2},{4,7},{5,4},{6,5},{7,6},{8,11},{9,8},{10,9... | collective-permute-start | bytes 1179656 | tf_op jit(solution)/shard_map/ppermute | solution.py:35
  248.9 13.7 %all-to-all-start.6 = ((bf16[32,8,512]{2,1,0:T(8,128)(2,1)}), bf16[32,8,512]{2,1,0:T(8,128)(2,1)}, u32[]{:S(2)}, u32[]{:S(2)}) async-start(bf16[32,8,512]{2,1,0:T(8,128)(2,1)} %bitcast.142), calls=%async_computation.6 | async-start | bytes 524288 | tf_op jit(solution)/shard_map/all_to_all | solution.py:60
  264.4 15.9 %collective-permute-start.25 = (bf16[192,512]{1,0:T(8,128)(2,1)}, bf16[192,512]{1,0:T(8,128)(2,1)}, u32[]{:S(2)}, u32[]{:S(2)}) collective-permute-start(bf16[192,512]{1,0:T(8,128)(2,1)} %shard_map.525.refs_0_), channel_id=1, source_target_pairs={{0,1},{1,2},{2,3},{3,0},{4,5},{5,6},{6,7},{7,4},{8,9},{9,10},{10,1... | collective-permute-start | bytes 589832 | tf_op jit(solution)/shard_map/ppermute | solution.py:35
  270.4 9.8 %collective-permute-start.26 = (bf16[192,512]{1,0:T(8,128)(2,1)}, bf16[192,512]{1,0:T(8,128)(2,1)}, u32[]{:S(2)}, u32[]{:S(2)}) collective-permute-start(bf16[192,512]{1,0:T(8,128)(2,1)} %shard_map.525.refs_0_), channel_id=1, source_target_pairs={{0,2},{1,3},{2,0},{3,1},{4,6},{5,7},{6,4},{7,5},{8,10},{9,11},{10,... | collective-permute-start | bytes 589832 | tf_op jit(solution)/shard_map/ppermute | solution.py:35
  270.4 9.8 %collective-permute-start.27 = (bf16[192,512]{1,0:T(8,128)(2,1)}, bf16[192,512]{1,0:T(8,128)(2,1)}, u32[]{:S(2)}, u32[]{:S(2)}) collective-permute-start(bf16[192,512]{1,0:T(8,128)(2,1)} %shard_map.525.refs_0_), channel_id=1, source_target_pairs={{0,3},{1,0},{2,1},{3,2},{4,7},{5,4},{6,5},{7,6},{8,11},{9,8},{10,9... | collective-permute-start | bytes 589832 | tf_op jit(solution)/shard_map/ppermute | solution.py:35
  296.0 11.1 %collective-permute-start.28 = (bf16[384,512]{1,0:T(8,128)(2,1)S(1)}, bf16[384,512]{1,0:T(8,128)(2,1)S(1)}, u32[]{:S(2)}, u32[]{:S(2)}) collective-permute-start(bf16[384,512]{1,0:T(8,128)(2,1)S(1)} %copy-done.116), channel_id=1, source_target_pairs={{0,1},{1,2},{2,3},{3,0},{4,5},{5,6},{6,7},{7,4},{8,9},{9,10},{10,1... | collective-permute-start | bytes 1179656 | tf_op jit(solution)/shard_map/ppermute | solution.py:35
  298.5 18.4 %collective-permute-start.29 = (bf16[384,512]{1,0:T(8,128)(2,1)S(1)}, bf16[384,512]{1,0:T(8,128)(2,1)S(1)}, u32[]{:S(2)}, u32[]{:S(2)}) collective-permute-start(bf16[384,512]{1,0:T(8,128)(2,1)S(1)} %copy-done.114), channel_id=1, source_target_pairs={{0,2},{1,3},{2,0},{3,1},{4,6},{5,7},{6,4},{7,5},{8,10},{9,11},{10,... | collective-permute-start | bytes 1179656 | tf_op jit(solution)/shard_map/ppermute | solution.py:35
  299.8 17.9 %collective-permute-start.30 = (bf16[384,512]{1,0:T(8,128)(2,1)S(1)}, bf16[384,512]{1,0:T(8,128)(2,1)S(1)}, u32[]{:S(2)}, u32[]{:S(2)}) collective-permute-start(bf16[384,512]{1,0:T(8,128)(2,1)S(1)} %copy-done.112), channel_id=1, source_target_pairs={{0,3},{1,0},{2,1},{3,2},{4,7},{5,4},{6,5},{7,6},{8,11},{9,8},{10,9... | collective-permute-start | bytes 1179656 | tf_op jit(solution)/shard_map/ppermute | solution.py:35
  303.0 35.0 %collective-permute-start.31 = (f32[512,512]{1,0:T(8,128)S(1)}, f32[512,512]{1,0:T(8,128)S(1)}, u32[]{:S(2)}, u32[]{:S(2)}) collective-permute-start(f32[512,512]{1,0:T(8,128)S(1)} %get-tuple-element.415), channel_id=1, source_target_pairs={{0,1},{1,2},{2,3},{3,0},{4,5},{5,6},{6,7},{7,4},{8,9},{9,10},{10,1... | collective-permute-start | bytes 3145736 | tf_op jit(solution)/shard_map/ppermute | solution.py:35
  303.0 47.4 %collective-permute-start.32 = (f32[512,512]{1,0:T(8,128)}, f32[512,512]{1,0:T(8,128)}, u32[]{:S(2)}, u32[]{:S(2)}) collective-permute-start(f32[512,512]{1,0:T(8,128)} %get-tuple-element.414), channel_id=1, source_target_pairs={{0,3},{1,0},{2,1},{3,2},{4,7},{5,4},{6,5},{7,6},{8,11},{9,8},{10,9... | collective-permute-start | bytes 3145736 | tf_op jit(solution)/shard_map/ppermute | solution.py:35
  307.9 69.6 %collective-permute-start.33 = (f32[512,512]{1,0:T(8,128)}, f32[512,512]{1,0:T(8,128)}, u32[]{:S(2)}, u32[]{:S(2)}) collective-permute-start(f32[512,512]{1,0:T(8,128)} %get-tuple-element.413), channel_id=1, source_target_pairs={{0,2},{1,3},{2,0},{3,1},{4,6},{5,7},{6,4},{7,5},{8,10},{9,11},{10,... | collective-permute-start | bytes 3145736 | tf_op jit(solution)/shard_map/ppermute | solution.py:35
  339.7 15.5 %all-to-all-start.7 = ((bf16[32,8,512]{2,1,0:T(8,128)(2,1)}), bf16[32,8,512]{2,1,0:T(8,128)(2,1)}, u32[]{:S(2)}, u32[]{:S(2)}) async-start(bf16[32,8,512]{2,1,0:T(8,128)(2,1)} %bitcast.137), calls=%async_computation.7 | async-start | bytes 524288 | tf_op jit(solution)/shard_map/all_to_all | solution.py:60
  364.8 12.8 %all-to-all-start.8 = ((bf16[32,8,512]{2,1,0:T(8,128)(2,1)}), bf16[32,8,512]{2,1,0:T(8,128)(2,1)S(1)}, u32[]{:S(2)}, u32[]{:S(2)}) async-start(bf16[32,8,512]{2,1,0:T(8,128)(2,1)} %bitcast.139), calls=%async_computation.8 | async-start | bytes 524288 | tf_op jit(solution)/shard_map/all_to_all | solution.py:60
  377.6 29.3 %all-to-all-start.10 = ((bf16[32,16,1408]{2,1,0:T(8,128)(2,1)}), bf16[32,16,1408]{2,1,0:T(8,128)(2,1)}, u32[]{:S(2)}, u32[]{:S(2)}) async-start(bf16[32,16,1408]{2,1,0:T(8,128)(2,1)} %bitcast.72), calls=%async_computation.10 | async-start | bytes 2883584 | tf_op jit(solution)/shard_map/all_to_all | solution.py:60
  385.4 10.4 %collective-permute-start.34 = (bf16[192,512]{1,0:T(8,128)(2,1)S(1)}, bf16[192,512]{1,0:T(8,128)(2,1)S(1)}, u32[]{:S(2)}, u32[]{:S(2)}) collective-permute-start(bf16[192,512]{1,0:T(8,128)(2,1)S(1)} %shard_map.531.refs_0_), channel_id=1, source_target_pairs={{0,1},{1,2},{2,3},{3,0},{4,5},{5,6},{6,7},{7,4},{8,9},{9,10},{10,1... | collective-permute-start | bytes 589832 | tf_op jit(solution)/shard_map/ppermute | solution.py:35
  387.6 9.9 %collective-permute-start.35 = (bf16[192,512]{1,0:T(8,128)(2,1)S(1)}, bf16[192,512]{1,0:T(8,128)(2,1)}, u32[]{:S(2)}, u32[]{:S(2)}) collective-permute-start(bf16[192,512]{1,0:T(8,128)(2,1)S(1)} %shard_map.531.refs_0_), channel_id=1, source_target_pairs={{0,2},{1,3},{2,0},{3,1},{4,6},{5,7},{6,4},{7,5},{8,10},{9,11},{10,... | collective-permute-start | bytes 589832 | tf_op jit(solution)/shard_map/ppermute | solution.py:35
  388.5 9.0 %collective-permute-start.36 = (bf16[192,512]{1,0:T(8,128)(2,1)S(1)}, bf16[192,512]{1,0:T(8,128)(2,1)}, u32[]{:S(2)}, u32[]{:S(2)}) collective-permute-start(bf16[192,512]{1,0:T(8,128)(2,1)S(1)} %shard_map.531.refs_0_), channel_id=1, source_target_pairs={{0,3},{1,0},{2,1},{3,2},{4,7},{5,4},{6,5},{7,6},{8,11},{9,8},{10,9... | collective-permute-start | bytes 589832 | tf_op jit(solution)/shard_map/ppermute | solution.py:35
  397.6 26.3 %collective-permute-start.37 = (bf16[384,512]{1,0:T(8,128)(2,1)}, bf16[384,512]{1,0:T(8,128)(2,1)}, u32[]{:S(2)}, u32[]{:S(2)}) collective-permute-start(bf16[384,512]{1,0:T(8,128)(2,1)} %get-tuple-element.247), channel_id=1, source_target_pairs={{0,1},{1,2},{2,3},{3,0},{4,5},{5,6},{6,7},{7,4},{8,9},{9,10},{10,1... | collective-permute-start | bytes 1179656 | tf_op jit(solution)/shard_map/ppermute | solution.py:35
  399.5 24.4 %collective-permute-start.38 = (bf16[384,512]{1,0:T(8,128)(2,1)}, bf16[384,512]{1,0:T(8,128)(2,1)}, u32[]{:S(2)}, u32[]{:S(2)}) collective-permute-start(bf16[384,512]{1,0:T(8,128)(2,1)} %get-tuple-element.248), channel_id=1, source_target_pairs={{0,2},{1,3},{2,0},{3,1},{4,6},{5,7},{6,4},{7,5},{8,10},{9,11},{10,... | collective-permute-start | bytes 1179656 | tf_op jit(solution)/shard_map/ppermute | solution.py:35
  401.9 21.9 %collective-permute-start.39 = (bf16[384,512]{1,0:T(8,128)(2,1)}, bf16[384,512]{1,0:T(8,128)(2,1)}, u32[]{:S(2)}, u32[]{:S(2)}) collective-permute-start(bf16[384,512]{1,0:T(8,128)(2,1)} %get-tuple-element.249), channel_id=1, source_target_pairs={{0,3},{1,0},{2,1},{3,2},{4,7},{5,4},{6,5},{7,6},{8,11},{9,8},{10,9... | collective-permute-start | bytes 1179656 | tf_op jit(solution)/shard_map/ppermute | solution.py:35
  406.9 27.9 %all-to-all-start.9 = ((bf16[32,16,768]{2,1,0:T(8,128)(2,1)}), bf16[32,16,768]{2,1,0:T(8,128)(2,1)S(1)}, u32[]{:S(2)}, u32[]{:S(2)}) async-start(bf16[32,16,768]{2,1,0:T(8,128)(2,1)} %bitcast.71), calls=%async_computation.9 | async-start | bytes 1572864 | tf_op jit(solution)/shard_map/all_to_all | solution.py:60
  430.6 32.3 %collective-permute-start.43 = (bf16[512,512]{1,0:T(8,128)(2,1)}, bf16[512,512]{1,0:T(8,128)(2,1)S(1)}, u32[]{:S(2)}, u32[]{:S(2)}) collective-permute-start(bf16[512,512]{1,0:T(8,128)(2,1)} %get-tuple-element.290), channel_id=1, source_target_pairs={{0,1},{1,2},{2,3},{3,0},{4,5},{5,6},{6,7},{7,4},{8,9},{9,10},{10,1... | collective-permute-start | bytes 1572872 | tf_op jit(solution)/shard_map/ppermute | solution.py:35
  430.9 32.0 %collective-permute-start.44 = (bf16[512,512]{1,0:T(8,128)(2,1)}, bf16[512,512]{1,0:T(8,128)(2,1)}, u32[]{:S(2)}, u32[]{:S(2)}) collective-permute-start(bf16[512,512]{1,0:T(8,128)(2,1)} %get-tuple-element.291), channel_id=1, source_target_pairs={{0,2},{1,3},{2,0},{3,1},{4,6},{5,7},{6,4},{7,5},{8,10},{9,11},{10,... | collective-permute-start | bytes 1572872 | tf_op jit(solution)/shard_map/ppermute | solution.py:35
  431.9 31.0 %collective-permute-start.45 = (bf16[512,512]{1,0:T(8,128)(2,1)}, bf16[512,512]{1,0:T(8,128)(2,1)}, u32[]{:S(2)}, u32[]{:S(2)}) collective-permute-start(bf16[512,512]{1,0:T(8,128)(2,1)} %get-tuple-element.292), channel_id=1, source_target_pairs={{0,3},{1,0},{2,1},{3,2},{4,7},{5,4},{6,5},{7,6},{8,11},{9,8},{10,9... | collective-permute-start | bytes 1572872 | tf_op jit(solution)/shard_map/ppermute | solution.py:35
  436.4 23.2 %collective-permute-start.40 = (f32[16,896]{1,0:T(8,128)S(1)}, f32[16,896]{1,0:T(8,128)S(1)}, u32[]{:S(2)}, u32[]{:S(2)}) collective-permute-start(f32[16,896]{1,0:T(8,128)S(1)} %pad_maximum_fusion.refs_0_), channel_id=1, source_target_pairs={{0,1},{1,2},{2,3},{3,0},{4,5},{5,6},{6,7},{7,4},{8,9},{9,10},{10,1... | collective-permute-start | bytes 172040 | tf_op jit(solution)/shard_map/ppermute | solution.py:35
  437.1 25.9 %all-to-all-start.11 = ((f32[128,1,128]{2,1,0:T(1,128)}), f32[128,1,128]{2,1,0:T(1,128)S(1)}, u32[]{:S(2)}, u32[]{:S(2)}) async-start(f32[128,1,128]{2,1,0:T(1,128)} %get-tuple-element.256), calls=%async_computation.11 | async-start | bytes 131072 | tf_op jit(solution)/shard_map/all_to_all | solution.py:1350
  446.6 13.2 %collective-permute-start.41 = (f32[16,896]{1,0:T(8,128)S(1)}, f32[16,896]{1,0:T(8,128)S(1)}, u32[]{:S(2)}, u32[]{:S(2)}) collective-permute-start(f32[16,896]{1,0:T(8,128)S(1)} %pad_maximum_fusion.refs_0_), channel_id=1, source_target_pairs={{0,2},{1,3},{2,0},{3,1},{4,6},{5,7},{6,4},{7,5},{8,10},{9,11},{10,... | collective-permute-start | bytes 172040 | tf_op jit(solution)/shard_map/ppermute | solution.py:35
  459.6 3.3 collective-permute-start.42
  487.5 11.5 %collective-permute-start.46 = (bf16[512,512]{1,0:T(8,128)(2,1)}, bf16[512,512]{1,0:T(8,128)(2,1)S(1)}, u32[]{:S(2)}, u32[]{:S(2)}) collective-permute-start(bf16[512,512]{1,0:T(8,128)(2,1)} %get-tuple-element.294), channel_id=1, source_target_pairs={{0,3},{1,0},{2,1},{3,2},{4,7},{5,4},{6,5},{7,6},{8,11},{9,8},{10,9... | collective-permute-start | bytes 1572872 | tf_op jit(solution)/shard_map/ppermute | solution.py:35
  488.6 13.0 %collective-permute-start.47 = (bf16[512,512]{1,0:T(8,128)(2,1)}, bf16[512,512]{1,0:T(8,128)(2,1)S(1)}, u32[]{:S(2)}, u32[]{:S(2)}) collective-permute-start(bf16[512,512]{1,0:T(8,128)(2,1)} %get-tuple-element.295), channel_id=1, source_target_pairs={{0,2},{1,3},{2,0},{3,1},{4,6},{5,7},{6,4},{7,5},{8,10},{9,11},{10,... | collective-permute-start | bytes 1572872 | tf_op jit(solution)/shard_map/ppermute | solution.py:35
  488.8 26.4 %collective-permute-start.48 = (bf16[512,512]{1,0:T(8,128)(2,1)}, bf16[512,512]{1,0:T(8,128)(2,1)S(1)}, u32[]{:S(2)}, u32[]{:S(2)}) collective-permute-start(bf16[512,512]{1,0:T(8,128)(2,1)} %get-tuple-element.296), channel_id=1, source_target_pairs={{0,1},{1,2},{2,3},{3,0},{4,5},{5,6},{6,7},{7,4},{8,9},{9,10},{10,1... | collective-permute-start | bytes 1572872 | tf_op jit(solution)/shard_map/ppermute | solution.py:35
  (190 other events, 1119.9 us)
Sparse Core Ops, SparseCore 0:
  19.3 61.2 all-gather.3
  82.9 55.7 all-gather.5
